TPU v7x, 256 devices: a whole 4x4x8 slice. The times are simulated.
256 devices in a mesh: range: 64 (over y, z, core), chan: 4 (over x).
Axes of the slice: x: 4, y: 4, z: 8, core: 2. Of those that a mesh axis runs over, the one named last changes fastest.
Arguments:
- features: bfloat16 [256, 65536], P('chan', 'range'), may hold values from -6 to 6
- hilbert_rank: int32 [65536], P('range'), may hold values from 0 to 65535, as said below
- neighbours: int32 [27, 65536], P(None, 'range'), may hold values from -1 to 512, as said below
- qkv_weight: bfloat16 [3, 256, 256], P(None, None, 'chan')
- out_weight: bfloat16 [256, 256], P(None, 'chan'), may hold values from -0.375 to 0.375
- conv_weight: bfloat16 [27, 256, 256], P(None, 'chan'), may hold values from -0.109375 to 0.109375
- up_weight: bfloat16 [256, 1024], P(None, 'chan'), may hold values from -0.375 to 0.375
- down_weight: bfloat16 [1024, 256], P('chan'), may hold values from -0.1875 to 0.1875
Outputs:
- restored: bfloat16 [256, 65536], P('chan', 'range')
Inputs may be any that keep to these rules, and one draw needn't show every extreme that they name: `hilbert_rank`: A permutation of the voxels. The owner of rank r is range r // 1024; the rows of one range device send at most 32 voxels to one owner, and exactly 32 in some pairs of every draw. `neighbours`: row 13 is 256 (the voxel itself); every entry that is not -1 names a rank of the grid, and both 0 and 512 occur.
All inputs are finite; a program needn't handle non-finite values.
Results may differ from a plain program's by a relative error of at most 0.012.
The roundings to bfloat16 on the way count: a program that leaves them out, or rounds other values in their place, can miss the bound.
Values may be sent and summed in bfloat16 or wider, within the bound.
No kernel may reach another device: no remote copies, remote signals or barrier semaphores. Data moves between devices by JAX's collectives and lax.ppermute only.
A program may use at most 64 MiB of HBM per device.

v0:
```python
import jax
import jax.numpy as jnp
from jax import lax
from jax.sharding import PartitionSpec as P

PATCH = 1024
HD = 16
KER = 27
HW = 256


def with_halo(x, sides, width):
    for axis, dim in sides:
        size, length = (lax.axis_size(axis), x.shape[dim])
        up = [(i, (i + 1) % size) for i in range(size - 1)]
        down = [(j, i) for i, j in up]
        last = lax.slice_in_dim(x, length - width, length, axis=dim)
        first = lax.slice_in_dim(x, 0, width, axis=dim)
        before = lax.ppermute(last, axis, up)
        after = lax.ppermute(first, axis, down)
        x = jnp.concatenate([before, x, after], axis=dim)
    return x


def layer_norm(values):
    values = values.astype(jnp.float32)
    mean = jnp.mean(values, axis=-1, keepdims=True)
    centred = values - mean
    var = jnp.mean(centred * centred, axis=-1, keepdims=True)
    return centred * lax.rsqrt(var + 1e-05)


def patch_heads(q, k, v):
    patches = q.shape[0] // PATCH
    heads = q.shape[1] // HD

    def split(t):
        t = t.reshape(patches, PATCH, heads, HD)
        return jnp.transpose(t, (0, 2, 1, 3)).reshape(patches * heads, PATCH, HD)

    def one_head(items):
        query, keys, values = items
        scores = jnp.einsum(
            "qd,kd->qk", query, keys, preferred_element_type=jnp.float32
        ) / jnp.sqrt(jnp.float32(HD))
        top = jnp.max(scores, axis=-1, keepdims=True)
        expo = jnp.exp(scores - top)
        probs = (expo / jnp.sum(expo, axis=-1, keepdims=True)).astype(jnp.bfloat16)
        return jnp.dot(probs, values, preferred_element_type=jnp.float32).astype(jnp.bfloat16)

    outs = lax.map(one_head, (split(q), split(k), split(v)))
    outs = outs.reshape(patches, heads, PATCH, HD)
    return jnp.transpose(outs, (0, 2, 1, 3)).reshape(patches * PATCH, heads * HD)


def running_slots(onehot):
    count = onehot.shape[0]
    owners = onehot.shape[1]
    blocks = onehot.reshape(count // 128, 128, owners).astype(jnp.float32)
    lower = (
        jnp.arange(128, dtype=jnp.int32)[:, None] >= jnp.arange(128, dtype=jnp.int32)[None, :]
    ).astype(jnp.float32)
    inner = jnp.einsum("ij,bjo->bio", lower, blocks, precision=lax.Precision.HIGHEST)
    totals = inner[:, -1, :]
    prior = jnp.cumsum(totals, axis=0) - totals
    before = (inner + prior[:, None, :] - 1.0).reshape(count, owners)
    return jnp.sum(onehot.astype(jnp.float32) * before, axis=1).astype(jnp.int32)


def shards(
    features, hilbert_rank, neighbours, qkv_weight, out_weight, conv_weight, up_weight, down_weight
):
    quarter = features.shape[0]
    rows = features.shape[1]
    owners = lax.axis_size("range")
    capacity = 2 * rows // owners
    whole = lax.all_gather(features, "chan", axis=0, tiled=True)
    norm1 = layer_norm(whole.T).astype(jnp.bfloat16)
    query = jnp.dot(norm1, qkv_weight[0], preferred_element_type=jnp.float32).astype(jnp.bfloat16)
    keys = jnp.dot(norm1, qkv_weight[1], preferred_element_type=jnp.float32).astype(jnp.bfloat16)
    values = jnp.dot(norm1, qkv_weight[2], preferred_element_type=jnp.float32).astype(jnp.bfloat16)
    heads_out = patch_heads(query, keys, values)
    attended = jnp.dot(
        lax.all_gather(heads_out, "chan", axis=1, tiled=True),
        out_weight,
        preferred_element_type=jnp.float32,
    )
    first = (features.T.astype(jnp.float32) + attended).astype(jnp.bfloat16)
    owner = hilbert_rank // rows
    onehot = (owner[:, None] == jnp.arange(owners, dtype=jnp.int32)[None, :]).astype(jnp.int32)
    slot = running_slots(onehot)
    flat_target = owner * capacity + slot
    row_ids = jnp.arange(rows, dtype=jnp.int32)
    source = jnp.full((owners * capacity,), rows, jnp.int32).at[flat_target].set(row_ids)
    send_rows = jnp.take(first, source, axis=0, mode="fill", fill_value=0).reshape(
        owners, capacity, quarter
    )
    local_rank = hilbert_rank % rows
    send_place = jnp.where(
        source < rows, jnp.take(local_rank, jnp.minimum(source, rows - 1), axis=0), -1
    ).reshape(owners, capacity)
    got_rows, got_place = (
        lax.all_to_all(send_rows, "range", split_axis=0, concat_axis=0, tiled=True),
        lax.all_to_all(send_place, "range", split_axis=0, concat_axis=0, tiled=True),
    )
    place = jnp.where(got_place < 0, rows, got_place).reshape(-1)
    inverse = (
        jnp.zeros((rows,), jnp.int32)
        .at[place]
        .set(jnp.arange(owners * capacity, dtype=jnp.int32), mode="drop")
    )
    grouped = jnp.take(got_rows.reshape(-1, quarter), inverse, axis=0)
    rimmed = with_halo(grouped, (("range", 0),), HW)
    extended = lax.all_gather(rimmed, "chan", axis=1, tiled=True)
    block_rows = min(256, rows)
    window = block_rows + 2 * HW
    channels = extended.shape[1]
    kernel_flat = jnp.transpose(conv_weight, (0, 2, 1)).reshape(KER * channels, quarter)
    window_ids = jnp.arange(window, dtype=jnp.int32)
    block_ids = jnp.arange(block_rows, dtype=jnp.int32)

    def conv_block(index):
        start = index * block_rows
        rim_rows = lax.dynamic_slice_in_dim(extended, start, window, 0)
        near = lax.dynamic_slice_in_dim(neighbours, start, block_rows, 1)
        target = jnp.where(near < 0, -1, block_ids[None, :] + near)
        table = (target.T[:, :, None] == window_ids[None, None, :]).astype(jnp.bfloat16)
        picked = jnp.einsum(
            "rjw,wc->rjc", table, rim_rows, preferred_element_type=jnp.float32
        ).astype(jnp.bfloat16)
        return jnp.dot(
            picked.reshape(block_rows, KER * channels),
            kernel_flat,
            preferred_element_type=jnp.float32,
        )

    conv = lax.map(conv_block, jnp.arange(rows // block_rows, dtype=jnp.int32)).reshape(
        rows, quarter
    )
    second = (grouped.astype(jnp.float32) + conv).astype(jnp.bfloat16)
    second_whole = lax.all_gather(second, "chan", axis=1, tiled=True)
    norm2 = layer_norm(second_whole).astype(jnp.bfloat16)
    hidden = jax.nn.gelu(
        jnp.dot(norm2, up_weight, preferred_element_type=jnp.float32), approximate=False
    ).astype(jnp.bfloat16)
    partial_rows = jnp.dot(hidden, down_weight, preferred_element_type=jnp.float32)
    mlp_out = lax.psum_scatter(
        partial_rows.astype(jnp.bfloat16), "chan", scatter_dimension=1, tiled=True
    ).astype(jnp.float32)
    third = (second.astype(jnp.float32) + mlp_out).astype(jnp.bfloat16)
    back_rows = jnp.take(third, place, axis=0, mode="fill", fill_value=0).reshape(
        owners, capacity, quarter
    )
    returned = lax.all_to_all(back_rows, "range", split_axis=0, concat_axis=0, tiled=True)
    return jnp.take(returned.reshape(-1, quarter), flat_target, axis=0).T


def solution(mesh):
    in_specs = (
        P("chan", "range"),
        P("range"),
        P(None, "range"),
        P(None, None, "chan"),
        P(None, "chan"),
        P(None, "chan", None),
        P(None, "chan"),
        P("chan", None),
    )
    out_specs = P("chan", "range")
    return jax.shard_map(shards, mesh=mesh, in_specs=in_specs, out_specs=out_specs, check_vma=False)
```

profile of v0, /device:TPU:1, one launch (start us, length us, event | category | flops | bytes accessed | tf_op | source)
XLA Modules:
  0.0 250.4 jit_solution(10631214302170166700)
XLA Ops:
  8.8 4.3 %scatter_custom_fusion = s32[2048]{0:T(1024)S(1)} fusion(s32[1024]{0:T(1024)S(1)} %get-tuple-element.116, s32[1024]{0:T(1024)S(1)} %iota.34, s32[]{:T(128)} %constant.67.clone.1), kind=kCustom, calls=%fused_computation.153 | custom fusion | bytes 8196 | tf_op jit(solution)/shard_map/scatter | solution.py:94
  13.1 8.6 %gather_fusion = s32[2048]{0:T(1024)S(1)} fusion(s32[1024]{0:T(1024)S(1)} %get-tuple-element.123, s32[2048]{0:T(1024)S(1)} %fusion.102), kind=kCustom, calls=%fused_computation.4 | custom fusion | bytes 24576 | tf_op jit(solution)/shard_map/jit(_take)/gather | solution.py:100
  22.4 13.2 %all-to-all-start.1 = ((s32[64,1,32]{2,1,0:T(1,128)}), s32[64,1,32]{2,1,0:T(1,128)S(1)}, u32[]{:S(2)}, u32[]{:S(2)}) async-start(s32[64,1,32]{2,1,0:T(1,128)} %bitcast.8), calls=%async_computation.1 | async-start | bytes 65536 | tf_op jit(solution)/shard_map/all_to_all | solution.py:104
  35.6 11.1 %all_gather.12 = bf16[256,1024]{1,0:T(8,128)(2,1)S(1)} all-gather(bf16[64,1024]{1,0:T(8,128)(2,1)S(1)} %copy-done.2), channel_id=1, replica_groups=mesh['range'=64,'chan'=4] {'chan'}, dimensions={0}, use_global_device_ids=true | all-gather | bytes 655360 | tf_op jit(solution)/shard_map/all_gather | solution.py:77
  47.8 9.5 %while.21 = (s32[]{:T(128)}, bf16[4,1024,16]{1,2,0:T(8,128)(2,1)S(1)}, bf16[4,1024,16]{1,2,0:T(8,128)(2,1)S(1)}, bf16[4,1024,16]{1,2,0:T(8,128)(2,1)S(1)}, bf16[4,1024,16]{1,2,0:T(8,128)(2,1)S(1)}, /*index=5*/s32[]{:T(128)}) while((s32[]{:T(128)}, bf16[4,1024,16]{1,2,0:T(8,128)(2,1)S(1)}, bf16[4,1024,16]{1,2,0:T(8,128)(2,1)S(1)}, ...), condition=%wide.region_5.6_spmd, body=%wide.region_2.5_spmd.sunk | while | flops 76560384 | bytes 12736589 | solution.py:51
  57.3 9.9 %all_gather.13 = bf16[1024,256]{0,1:T(8,128)(2,1)S(1)} all-gather(bf16[1024,64]{0,1:T(8,128)(2,1)S(1)} %bitcast.126), channel_id=1, replica_groups=mesh['range'=64,'chan'=4] {'chan'}, dimensions={1}, use_global_device_ids=true | all-gather | bytes 655360 | tf_op jit(solution)/shard_map/all_gather | solution.py:84
  67.6 6.2 %gather_fusion.1 = bf16[2048,64]{1,0:T(8,128)(2,1)S(1)} fusion(bf16[1024,64]{1,0:T(8,128)(2,1)S(1)} %copy.22, s32[2048]{0:T(1024)S(1)} %get-tuple-element.122), kind=kCustom, calls=%fused_computation.clone | custom fusion | bytes 532480 | tf_op jit(solution)/shard_map/jit(_take)/gather | solution.py:95
  75.1 15.5 %all-to-all-start = ((bf16[64,2,1024]{2,1,0:T(2,128)(2,1)}), bf16[64,2,1024]{2,1,0:T(2,128)(2,1)S(1)}, u32[]{:S(2)}, u32[]{:S(2)}) async-start(bf16[64,2,1024]{2,1,0:T(2,128)(2,1)} %reshape.252), calls=%async_computation | async-start | bytes 524288 | tf_op jit(solution)/shard_map/all_to_all | solution.py:103
  90.8 8.0 %scatter_custom_fusion.1 = s32[1024]{0:T(1024)S(1)} fusion(s32[2048]{0:T(1024)S(1)} %bitcast.127, s32[2048]{0:T(1024)S(1)} %iota.35, s32[]{:T(128)} %constant.85.clone.1), kind=kCustom, calls=%fused_computation.162 | custom fusion | bytes 4100 | tf_op jit(solution)/shard_map/scatter | solution.py:110
  98.9 3.8 %all-to-all-done = bf16[64,2,1024]{2,1,0:T(2,128)(2,1)S(1)} async-done(((bf16[64,2,1024]{2,1,0:T(2,128)(2,1)}), bf16[64,2,1024]{2,1,0:T(2,128)(2,1)S(1)}, u32[]{:S(2)}, u32[]{:S(2)}) %all-to-all-start) | async-done | bytes 262176 | tf_op jit(solution)/shard_map/all_to_all | solution.py:103
  103.0 3.2 %gather_fusion.2 = bf16[1024,64]{1,0:T(8,128)(2,1)S(1)} fusion(bf16[2048,64]{1,0:T(8,128)(2,1)S(1)} %bitcast.116, s32[1024]{0:T(1024)S(1)} %fusion.107), kind=kCustom, calls=%fused_computation.1.clone | custom fusion | bytes 266240 | tf_op jit(solution)/shard_map/jit(_take)/gather | solution.py:112
  106.4 3.3 %collective-permute-start = (bf16[256,64]{0,1:T(8,128)(2,1)S(1)}, bf16[256,64]{0,1:T(8,128)(2,1)S(1)}, u32[]{:S(2)}, u32[]{:S(2)}) collective-permute-start(bf16[256,64]{0,1:T(8,128)(2,1)S(1)} %get-tuple-element.119), channel_id=1, source_target_pairs={{0,4},{4,8},{8,12},{12,16},{16,20},{20,24},{24,28},{28,32},{32,36}... | collective-permute-start | bytes 98312 | tf_op jit(solution)/shard_map/ppermute | solution.py:19
  114.9 12.4 %all_gather.14 = bf16[1536,256]{0,1:T(8,128)(2,1)S(1)} all-gather(bf16[1536,64]{0,1:T(8,128)(2,1)S(1)} %pad_maximum_fusion), channel_id=1, replica_groups=mesh['range'=64,'chan'=4] {'chan'}, dimensions={1}, use_global_device_ids=true | all-gather | bytes 983040 | tf_op jit(solution)/shard_map/all_gather | solution.py:114
  127.4 39.8 %while.22 = (s32[]{:T(128)}, f32[4,256,64]{1,0,2:T(4,128)S(1)}, s32[4]{0:T(128)S(1)}, s32[27,1024]{1,0:T(8,128)}, bf16[1536,256]{0,1:T(8,128)(2,1)S(1)}, /*index...) while((s32[]{:T(128)}, f32[4,256,64]{1,0,2:T(4,128)S(1)}, ...), condition=%wide.region_11.14_spmd.clone, body=%wide.region_10.13_spmd.clone.sunk | while | flops 2951500032 | bytes 8771796 | solution.py:137
  129.5 5.8 %fusion.165 = bf16[256,27,256]{0,2,1:T(8,128)(2,1)S(1)} fusion(s32[256,27]{0,1:T(8,128)S(1)} %fusion.164, bf16[1536,256]{0,1:T(8,128)(2,1)S(1)} %get-tuple-element.241, s32[]{:T(128)S(6)} %select_n.154), kind=kOutput, calls=%fused_computation.30.clone.1 | convolution fusion | flops 2724986880 | bytes 3964932 | tf_op jit(solution)/shard_map/while/body/eval_jaxpr/rjw,wc->rjc/dot_general | solution.py:128
  139.4 6.0 %fusion.165 = bf16[256,27,256]{0,2,1:T(8,128)(2,1)S(1)} fusion(s32[256,27]{0,1:T(8,128)S(1)} %fusion.164, bf16[1536,256]{0,1:T(8,128)(2,1)S(1)} %get-tuple-element.241, s32[]{:T(128)S(6)} %select_n.154), kind=kOutput, calls=%fused_computation.30.clone.1 | convolution fusion | flops 2724986880 | bytes 3964932 | tf_op jit(solution)/shard_map/while/body/eval_jaxpr/rjw,wc->rjc/dot_general | solution.py:128
  149.4 5.9 %fusion.165 = bf16[256,27,256]{0,2,1:T(8,128)(2,1)S(1)} fusion(s32[256,27]{0,1:T(8,128)S(1)} %fusion.164, bf16[1536,256]{0,1:T(8,128)(2,1)S(1)} %get-tuple-element.241, s32[]{:T(128)S(6)} %select_n.154), kind=kOutput, calls=%fused_computation.30.clone.1 | convolution fusion | flops 2724986880 | bytes 3964932 | tf_op jit(solution)/shard_map/while/body/eval_jaxpr/rjw,wc->rjc/dot_general | solution.py:128
  159.3 6.0 %fusion.165 = bf16[256,27,256]{0,2,1:T(8,128)(2,1)S(1)} fusion(s32[256,27]{0,1:T(8,128)S(1)} %fusion.164, bf16[1536,256]{0,1:T(8,128)(2,1)S(1)} %get-tuple-element.241, s32[]{:T(128)S(6)} %select_n.154), kind=kOutput, calls=%fused_computation.30.clone.1 | convolution fusion | flops 2724986880 | bytes 3964932 | tf_op jit(solution)/shard_map/while/body/eval_jaxpr/rjw,wc->rjc/dot_general | solution.py:128
  167.3 10.9 %all_gather.15 = bf16[1024,256]{0,1:T(8,128)(2,1)S(1)} all-gather(bf16[1024,64]{0,1:T(8,128)(2,1)S(1)} %add_convert_fusion.1), channel_id=1, replica_groups=mesh['range'=64,'chan'=4] {'chan'}, dimensions={1}, use_global_device_ids=true | all-gather | bytes 655360 | tf_op jit(solution)/shard_map/all_gather | solution.py:141
  178.5 3.6 %convolution_convert_fusion = bf16[1024,256]{0,1:T(8,128)(2,1)} fusion(bf16[256,256]{1,0:T(8,128)(2,1)S(1)} %copy-done, bf16[256,256]{1,0:T(8,128)(2,1)S(1)} %copy-done.4, bf16[1024,256]{0,1:T(8,128)(2,1)S(1)} %all_gather.15, f32[1024]{0:T(1024)S(1)} %add_rsqrt_fusion, f32[1024]{0:T(1024)S(1)} %broadcast_multiply_fusion), kind=kOutput, calls=%fused_computation.43 | convolution fusion | flops 286785536 | bytes 1318912 | tf_op jit(solution)/shard_map/dot_general | solution.py:146
  183.4 22.6 %reduce-scatter.2.cloned.1.call-done = bf16[1024,64]{0,1:T(8,128)(2,1)} async-done(((bf16[1024,256]{0,1:T(8,128)(2,1)}), bf16[1024,64]{0,1:T(8,128)(2,1)}) %reduce-scatter.2.cloned.1.call-update) | async-done | bytes 131088 | tf_op jit(solution)/shard_map/reduce_scatter | solution.py:147
  207.1 6.2 %gather_fusion.3 = bf16[2048,64]{1,0:T(8,128)(2,1)S(1)} fusion(bf16[1024,64]{1,0:T(8,128)(2,1)S(1)} %copy.26, s32[2048]{0:T(1024)S(1)} %fusion.103), kind=kCustom, calls=%fused_computation.2.clone | custom fusion | bytes 532480 | tf_op jit(solution)/shard_map/jit(_take)/gather | solution.py:151
  214.6 12.3 %all-to-all-start.2 = ((bf16[64,2,1024]{2,1,0:T(2,128)(2,1)}), bf16[64,2,1024]{2,1,0:T(2,128)(2,1)S(1)}, u32[]{:S(2)}, u32[]{:S(2)}) async-start(bf16[64,2,1024]{2,1,0:T(2,128)(2,1)} %reshape.254), calls=%async_computation.3 | async-start | bytes 524288 | tf_op jit(solution)/shard_map/all_to_all | solution.py:154
  227.0 12.0 %all-to-all-done.2 = bf16[64,2,1024]{2,1,0:T(2,128)(2,1)S(1)} async-done(((bf16[64,2,1024]{2,1,0:T(2,128)(2,1)}), bf16[64,2,1024]{2,1,0:T(2,128)(2,1)S(1)}, u32[]{:S(2)}, u32[]{:S(2)}) %all-to-all-start.2) | async-done | bytes 262176 | tf_op jit(solution)/shard_map/all_to_all | solution.py:154
  (105 shorter events, 43.0 us)
Async XLA Ops:
  6.5 171.9 %copy-start = (bf16[256,256]{1,0:T(8,128)(2,1)S(1)}, bf16[256,256]{1,0:T(8,128)(2,1)}, u32[]{:S(2)}) copy-start(bf16[256,256]{1,0:T(8,128)(2,1)} %param.23) | copy-start | bytes 393220
  13.1 22.5 %copy-start.2 = (bf16[64,1024]{1,0:T(8,128)(2,1)S(1)}, bf16[64,1024]{1,0:T(8,128)(2,1)}, u32[]{:S(2)}) copy-start(bf16[64,1024]{1,0:T(8,128)(2,1)} %param.16) | copy-start | bytes 393220
  13.1 33.8 %copy-start.5 = (bf16[3,256,64]{1,2,0:T(8,128)(2,1)S(1)}, bf16[3,256,64]{1,2,0:T(8,128)(2,1)}, u32[]{:S(2)}) copy-start(bf16[3,256,64]{1,2,0:T(8,128)(2,1)} %param.19) | copy-start | bytes 294916
  22.4 52.7 %all-to-all-start.1 = ((s32[64,1,32]{2,1,0:T(1,128)}), s32[64,1,32]{2,1,0:T(1,128)S(1)}, u32[]{:S(2)}, u32[]{:S(2)}) async-start(s32[64,1,32]{2,1,0:T(1,128)} %bitcast.8), calls=%async_computation.1 | async-start | bytes 65536 | tf_op jit(solution)/shard_map/all_to_all | solution.py:104
  47.8 19.4 %copy-start.3 = (bf16[256,64]{0,1:T(8,128)(2,1)S(1)}, bf16[256,64]{0,1:T(8,128)(2,1)}, u32[]{:S(2)}) copy-start(bf16[256,64]{0,1:T(8,128)(2,1)} %param.20) | copy-start | bytes 98308
  73.8 37.9 %copy-start.1 = (bf16[27,64,256]{2,1,0:T(8,128)(2,1)S(1)}, bf16[27,64,256]{2,1,0:T(8,128)(2,1)}, u32[]{:S(2)}) copy-start(bf16[27,64,256]{2,1,0:T(8,128)(2,1)} %param.21) | copy-start | bytes 2654212
  75.1 27.5 %all-to-all-start = ((bf16[64,2,1024]{2,1,0:T(2,128)(2,1)}), bf16[64,2,1024]{2,1,0:T(2,128)(2,1)S(1)}, u32[]{:S(2)}, u32[]{:S(2)}) async-start(bf16[64,2,1024]{2,1,0:T(2,128)(2,1)} %reshape.252), calls=%async_computation | async-start | bytes 524288 | tf_op jit(solution)/shard_map/all_to_all | solution.py:103
  90.7 115.3 %reduce-scatter.2.cloned.1.call-start = ((), (), s32[]{:S(2)}) async-start(), calls=%async_computation.4 | async-start | bytes 655360 | tf_op jit(solution)/shard_map/reduce_scatter | solution.py:147
  106.4 6.3 %collective-permute-start = (bf16[256,64]{0,1:T(8,128)(2,1)S(1)}, bf16[256,64]{0,1:T(8,128)(2,1)S(1)}, u32[]{:S(2)}, u32[]{:S(2)}) collective-permute-start(bf16[256,64]{0,1:T(8,128)(2,1)S(1)} %get-tuple-element.119), channel_id=1, source_target_pairs={{0,4},{4,8},{8,12},{12,16},{16,20},{20,24},{24,28},{28,32},{32,36}... | collective-permute-start | bytes 98312 | tf_op jit(solution)/shard_map/ppermute | solution.py:19
  109.7 5.2 %collective-permute-start.1 = (bf16[256,64]{0,1:T(8,128)(2,1)S(1)}, bf16[256,64]{0,1:T(8,128)(2,1)S(1)}, u32[]{:S(2)}, u32[]{:S(2)}) collective-permute-start(bf16[256,64]{0,1:T(8,128)(2,1)S(1)} %get-tuple-element.120), channel_id=1, source_target_pairs={{4,0},{8,4},{12,8},{16,12},{20,16},{24,20},{28,24},{32,28},{36,32}... | collective-permute-start | bytes 98312 | tf_op jit(solution)/shard_map/ppermute | solution.py:20
  127.4 51.1 %copy-start.4 = (bf16[256,256]{1,0:T(8,128)(2,1)S(1)}, bf16[256,256]{1,0:T(8,128)(2,1)}, u32[]{:S(2)}) copy-start(bf16[256,256]{1,0:T(8,128)(2,1)} %param.22) | copy-start | bytes 393220
  214.6 24.3 %all-to-all-start.2 = ((bf16[64,2,1024]{2,1,0:T(2,128)(2,1)}), bf16[64,2,1024]{2,1,0:T(2,128)(2,1)S(1)}, u32[]{:S(2)}, u32[]{:S(2)}) async-start(bf16[64,2,1024]{2,1,0:T(2,128)(2,1)} %reshape.254), calls=%async_computation.3 | async-start | bytes 524288 | tf_op jit(solution)/shard_map/all_to_all | solution.py:154
Sparse Core Ops, SparseCore 0:
  182.2 23.7 reduce-scatter.1
where the time goes:
time: 251 us; the launch traced here: 250 us
  local copies, waits for them, and re-layouts  52.8 us (21%)
  starting transfers between devices  46.3 us (18%)
  blocking collectives  44.2 us (18%)
  waiting for transfers between devices  40.5 us (16%)
  matrix products  38.5 us (15%)
  between operations  13.8 us (5%)
  other arithmetic  11.2 us (4%)
  loops' own time  3.01 us (1%)
    dot_general x4, matrix products, conv_block(): jnp.einsum('rjw,wc->rjc', table, rim_rows, preferred_element_type=jnp.flo...  23.6 us
    reduce_scatter x1, waiting for transfers between devices, shards(): lax.psum_scatter(partial_rows.astype(jnp.bfloat16), 'chan', scatter_dimen...  22.6 us
    all_to_all x1, starting transfers between devices, shards(): lax.all_to_all(send_rows, 'range', split_axis=0, concat_axis=0, tiled=True)  15.5 us
    all_to_all x1, starting transfers between devices, shards(): lax.all_to_all(send_place, 'range', split_axis=0, concat_axis=0, tiled=True)  13.2 us
    all_gather x1, blocking collectives, shards(): extended = lax.all_gather(rimmed, 'chan', axis=1, tiled=True)  12.4 us
    all_to_all x1, starting transfers between devices, shards(): lax.all_to_all(back_rows, 'range', split_axis=0, concat_axis=0, tiled=True)  12.3 us
    all_to_all x1, waiting for transfers between devices, shards(): lax.all_to_all(back_rows, 'range', split_axis=0, concat_axis=0, tiled=True)  12 us
    all_gather x1, blocking collectives, shards(): whole = lax.all_gather(features, 'chan', axis=0, tiled=True)  11.1 us
  transfers between devices with their start and end apart: 6, of which 4 were waited for; matrix products, arithmetic and copies ran while one was open for 12% of the time, Pallas kernels for 0%

commit v1 on v0

v1 whole, which is shorter than its diff:
```python
import jax
import jax.numpy as jnp
from jax import lax
from jax.experimental import pallas as pl
from jax.experimental.pallas import tpu as pltpu
from jax.sharding import PartitionSpec as P

HD = 16
KER = 27
HW = 256
CHAN = 4
SLOTS = 32
HALF = SLOTS // 2
F32 = jnp.float32
BF16 = jnp.bfloat16

NN = (((1,), (0,)), ((), ()))
NT = (((1,), (1,)), ((), ()))
TN = (((0,), (0,)), ((), ()))


def dot(a, b, dims=NN):
    return lax.dot_general(a, b, dims, preferred_element_type=F32)


def kernel_call(body, outs, cost, operands, scratch=(), vmem=48):
    specs = [pl.BlockSpec(memory_space=pltpu.SMEM if x.shape == (1,) else pltpu.VMEM) for x in operands]
    call = pl.pallas_call(
        body,
        out_shape=outs,
        in_specs=specs,
        scratch_shapes=list(scratch),
        compiler_params=pltpu.CompilerParams(vmem_limit_bytes=vmem * 1024 * 1024),
        cost_estimate=pl.CostEstimate(flops=cost, bytes_accessed=1 << 20, transcendentals=0),
    )
    return call(*operands)


def column_norm(x):
    mean = jnp.mean(x, axis=0, keepdims=True)
    centred = x - mean
    var = jnp.mean(centred * centred, axis=0, keepdims=True)
    return (centred * lax.rsqrt(var + 1e-05)).astype(BF16)


def place_blocks(dst, blocks, me):
    for k, block in enumerate(blocks):
        owner = lax.rem(me + CHAN - k, CHAN)
        size = block.shape[0]
        dst[pl.ds(pl.multiple_of(owner * size, size), size), :] = block[...]


def attention_body(me_ref, x0, x1, x2, x3, w_ref, out_ref, xs, qkv):
    place_blocks(xs, (x0, x1, x2, x3), me_ref[0])
    rows = xs.shape[1]
    norm = column_norm(xs[...].astype(F32))
    proj = dot(w_ref[...], norm)
    width = out_ref.shape[0]
    qkv[0:width, :] = (proj[0:width].astype(BF16) * BF16(0.25)).astype(BF16)
    qkv[width:, :] = proj[width:].astype(BF16)
    ones = (lax.broadcasted_iota(jnp.int32, (HD, rows), 0) == 0).astype(F32).astype(BF16)
    block = 256
    for head in range(width // HD):
        lo = head * HD
        keys = qkv[width + lo : width + lo + HD, :]
        vals = jnp.concatenate([qkv[2 * width + lo : 2 * width + lo + HD, :], ones], axis=0)
        for part in range(rows // block):
            cols = slice(part * block, (part + 1) * block)
            scores = dot(keys, qkv[lo : lo + HD, cols], TN)
            top = jnp.max(scores, axis=0, keepdims=True)
            expo = jnp.exp(scores - top).astype(BF16)
            res = dot(vals, expo)
            out_ref[lo : lo + HD, cols] = (res[0:HD] / res[HD : HD + 1]).astype(BF16)


def slot_match(code, half, start, size, cols):
    rows = lax.broadcasted_iota(jnp.int32, (size, cols), 0) + (start + half * 1024)
    return (rows == code).astype(F32).astype(BF16)


def send_body(me_ref, h0, h1, h2, h3, x_ref, w_ref, code_ref, out_ref, hs):
    place_blocks(hs, (h0, h1, h2, h3), me_ref[0])
    first = (x_ref[...].astype(F32) + dot(w_ref[...], hs[...])).astype(BF16)
    zero = jnp.zeros_like(first)
    low = jnp.concatenate([first, zero], axis=0)
    high = jnp.concatenate([zero, first], axis=0)
    code = code_ref[...]
    block = 256
    for start in range(0, out_ref.shape[0], block):
        res = dot(slot_match(code, 0, start, block, code.shape[1]), low, NT)
        res += dot(slot_match(code, 1, start, block, code.shape[1]), high, NT)
        out_ref[start : start + block, :] = res.astype(BF16)


def group_body(me_ref, got_ref, place_ref, own_ref, m1_ref, m2_ref, m3_ref, first_ref, last_ref, tmp):
    me = me_ref[0]
    width = own_ref.shape[1]
    got = got_ref[...].astype(F32).T.astype(BF16)
    for q in range(CHAN):
        rows = lax.broadcasted_iota(jnp.int32, (256, got.shape[1]), 0) + q * 256
        res = 0.0
        for half in range(2):
            match = (rows == place_ref[half : half + 1, :]).astype(F32).astype(BF16)
            res += dot(got[half * width : (half + 1) * width], match, NT)
        tmp[q] = res.astype(BF16)
    for k, ref in enumerate((own_ref, m1_ref, m2_ref, m3_ref)):
        target = lax.rem(me + k, CHAN)
        for b in range(3):
            ref[b] = tmp[jnp.clip(target - 1 + b, 0, CHAN - 1)]
    first_ref[...] = tmp[0]
    last_ref[...] = tmp[CHAN - 1]


def conv_body(me_ref, *refs):
    msgs = refs[0:4]
    halos = refs[4:8]
    near_ref, conv_ref, up_ref, down_ref = refs[8:12]
    outs = refs[12:16]
    win, acc, third_ref = refs[16:19]
    me = me_ref[0]
    quarter = 64
    for k in range(CHAN):
        owner = lax.rem(me + CHAN - k, CHAN)
        at = pl.ds(pl.multiple_of(owner * quarter, quarter), quarter)
        for b in range(3):
            win[at, b * 256 : (b + 1) * 256] = msgs[k][b]

    @pl.when(me == 0)
    def _():
        for k in range(CHAN):
            win[k * quarter : (k + 1) * quarter, 0:256] = halos[k][...]

    @pl.when(me == CHAN - 1)
    def _():
        for k in range(CHAN):
            src = (k + 1) % CHAN
            win[src * quarter : (src + 1) * quarter, 512:768] = halos[k][...]

    rows = lax.broadcasted_iota(jnp.int32, (768, 256), 0)
    lane = lax.broadcasted_iota(jnp.int32, (1, 256), 1)
    acc[...] = jnp.zeros_like(acc)

    def step(j, carry):
        near = near_ref[pl.ds(j, 1), :]
        target = jnp.where(near < 0, -1, near + lane)
        match = (rows == target).astype(F32).astype(BF16)
        picked = dot(win[...], match).astype(BF16)
        weight = jnp.concatenate([conv_ref[i, j] for i in range(CHAN)], axis=0)
        acc[...] += dot(weight, picked)
        return carry

    lax.fori_loop(0, KER, step, 0)
    second = (win[:, 256:512].astype(F32) + acc[...]).astype(BF16)
    norm = column_norm(second.astype(F32))
    total = second.astype(F32)
    for i in range(CHAN):
        hidden = dot(up_ref[i], norm)
        hidden = (0.5 * hidden * (1.0 + lax.erf(hidden * (2.0 ** -0.5)))).astype(BF16)
        total += dot(down_ref[i], hidden)
    third_ref[...] = total.astype(BF16)
    for k in range(CHAN):
        to = lax.rem(me + k, CHAN)
        outs[k][...] = third_ref[pl.ds(pl.multiple_of(to * quarter, quarter), quarter), :]


def back_body(me_ref, t0, t1, t2, t3, place_ref, out_ref, tmp):
    me = me_ref[0]
    for k, ref in enumerate((t0, t1, t2, t3)):
        tmp[lax.rem(me + CHAN - k, CHAN)] = ref[...]
    third = jnp.concatenate([tmp[q] for q in range(CHAN)], axis=1)
    zero = jnp.zeros_like(third)
    low = jnp.concatenate([third, zero], axis=0)
    high = jnp.concatenate([zero, third], axis=0)
    column = place_ref[...].astype(F32).T
    block = 256
    rank = lax.broadcasted_iota(jnp.int32, (block, third.shape[1]), 1).astype(F32)
    for start in range(0, out_ref.shape[0], block):
        res = 0.0
        for half, rhs in enumerate((low, high)):
            match = (rank == column[start : start + block, half : half + 1]).astype(F32).astype(BF16)
            res += dot(match, rhs, NT)
        out_ref[start : start + block, :] = res.astype(BF16)


def restore_body(got_ref, code_ref, out_ref):
    width = out_ref.shape[0]
    got = got_ref[...].astype(F32).T.astype(BF16)
    code = code_ref[...]
    res = 0.0
    for half in range(2):
        for start in range(0, got.shape[1], 256):
            match = slot_match(code, half, start, 256, code.shape[1])
            res += dot(got[half * width : (half + 1) * width, start : start + 256], match)
    out_ref[...] = res.astype(BF16)


def turn(k):
    return [(i, (i + k) % CHAN) for i in range(CHAN)]


def gather_chan(x):
    return [x] + [lax.ppermute(x, "chan", turn(k)) for k in range(1, CHAN)]


def slot_codes(rank, rows, owners):
    owner = rank // rows
    onehot = (owner[:, None] == jnp.arange(owners, dtype=jnp.int32)[None, :]).astype(F32)
    blocks = onehot.reshape(rows // 128, 128, owners)
    ids = jnp.arange(128, dtype=jnp.int32)
    lower = (ids[:, None] >= ids[None, :]).astype(F32)
    inner = jnp.einsum("ij,bjo->bio", lower, blocks)
    totals = inner[:, -1, :]
    prior = jnp.cumsum(totals, axis=0) - totals
    before = (inner + prior[:, None, :] - 1.0).reshape(rows, owners)
    slot = jnp.sum(onehot * before, axis=1).astype(jnp.int32)
    return (slot // HALF) * 1024 + owner * HALF + slot % HALF


def shards(
    features, hilbert_rank, neighbours, qkv_weight, out_weight, conv_weight, up_weight, down_weight
):
    quarter, rows = features.shape
    owners = lax.axis_size("range")
    me = lax.axis_index("chan").astype(jnp.int32)
    me_ref = me[None]
    sds = jax.ShapeDtypeStruct

    with jax.named_scope("gather_features"):
        blocks = gather_chan(features)
    with jax.named_scope("gather_weights"):
        conv_all = lax.all_gather(conv_weight, "chan", axis=0)
        up_all = lax.all_gather(up_weight.T, "chan", axis=0)
        down_all = lax.all_gather(down_weight.T, "chan", axis=0)

    with jax.named_scope("codes"):
        code = slot_codes(hilbert_rank, rows, owners)
        ids = jnp.arange(2 * rows, dtype=jnp.int32)
        table = jnp.max(
            jnp.where(code[None, :] == ids[:, None], (hilbert_rank % rows)[None, :], -1), axis=1
        )
        tables = lax.all_gather(table, "range", axis=0)
        mine = lax.dynamic_index_in_dim(
            tables.reshape(owners, 2, owners, HALF), lax.axis_index("range"), 2, keepdims=False
        )
        place = jnp.transpose(mine, (1, 0, 2)).reshape(2, rows)
        place = jnp.concatenate([place, jnp.full((6, rows), -1, jnp.int32)], axis=0)
        code = code[None, :]

    qkv = jnp.transpose(qkv_weight, (0, 2, 1)).reshape(3 * quarter, -1)
    with jax.named_scope("attention"):
        heads = kernel_call(
            attention_body,
            sds((quarter, rows), BF16),
            1 << 32,
            [me_ref] + blocks + [qkv],
            [pltpu.VMEM((CHAN * quarter, rows), BF16), pltpu.VMEM((3 * quarter, rows), BF16)],
        )
    with jax.named_scope("gather_heads"):
        blocks = gather_chan(heads)
    with jax.named_scope("send"):
        send = kernel_call(
            send_body,
            sds((owners * HALF, 2 * quarter), BF16),
            1 << 30,
            [me_ref] + blocks + [features, out_weight.T, code],
            [pltpu.VMEM((CHAN * quarter, rows), BF16)],
        )
        got = exchange(send, owners)
    with jax.named_scope("group"):
        part = sds((3, quarter, 256), BF16)
        edge = sds((quarter, 256), BF16)
        own, m1, m2, m3, first_edge, last_edge = kernel_call(
            group_body,
            (part, part, part, part, edge, edge),
            1 << 30,
            [me_ref, got, place],
            [pltpu.VMEM((CHAN, quarter, 256), BF16)],
        )
    with jax.named_scope("gather_window"):
        msgs = [own] + [lax.ppermute(m, "chan", turn(k)) for k, m in ((1, m1), (2, m2), (3, m3))]
        halos = []
        for k in range(CHAN):
            other = (k + 1) % CHAN
            up = [(r * CHAN + k, (r + 1) * CHAN) for r in range(owners - 1)]
            down = [((r + 1) * CHAN + other, r * CHAN + CHAN - 1) for r in range(owners - 1)]
            halos.append(
                lax.ppermute(jnp.where(me == k, last_edge, first_edge), ("range", "chan"), up + down)
            )
    with jax.named_scope("conv_mlp"):
        near = lax.dynamic_slice_in_dim(neighbours, me * 256, 256, 1)
        thirds = kernel_call(
            conv_body,
            (edge, edge, edge, edge),
            1 << 32,
            [me_ref] + msgs + halos + [near, conv_all, up_all, down_all],
            [
                pltpu.VMEM((CHAN * quarter, 768), BF16),
                pltpu.VMEM((CHAN * quarter, 256), F32),
                pltpu.VMEM((CHAN * quarter, 256), BF16),
            ],
        )
    with jax.named_scope("turn_back"):
        thirds = [thirds[0]] + [lax.ppermute(thirds[k], "chan", turn(k)) for k in range(1, CHAN)]
    with jax.named_scope("back"):
        back = kernel_call(
            back_body,
            sds((owners * HALF, 2 * quarter), BF16),
            1 << 30,
            [me_ref] + thirds + [place],
            [pltpu.VMEM((CHAN, quarter, 256), BF16)],
        )
        returned = exchange(back, owners)
    with jax.named_scope("restore"):
        return kernel_call(restore_body, sds((quarter, rows), BF16), 1 << 30, [returned, code])


def exchange(rows, owners):
    parts = rows.reshape(owners, HALF, rows.shape[1])
    parts = lax.all_to_all(parts, "range", split_axis=0, concat_axis=0, tiled=True)
    return parts.reshape(rows.shape)


def solution(mesh):
    in_specs = (
        P("chan", "range"),
        P("range"),
        P(None, "range"),
        P(None, None, "chan"),
        P(None, "chan"),
        P(None, "chan", None),
        P(None, "chan"),
        P("chan", None),
    )
    out_specs = P("chan", "range")
    return jax.shard_map(shards, mesh=mesh, in_specs=in_specs, out_specs=out_specs, check_vma=False)
```

time: 251 us -> 221 us (0.88)
  blocking collectives: 44.2 us -> 102 us
  local copies, waits for them, and re-layouts: 52.8 us -> 7.98 us
  matrix products: 38.5 us -> 0.19 us
  Pallas kernels: 0 us -> 32.4 us
  waiting for transfers between devices: 40.5 us -> 21.7 us
  other arithmetic: 11.2 us -> 2.39 us
  starting transfers between devices: 46.3 us -> 40.2 us
  loops' own time: 3.01 us -> 0 us
    dot_general x22 -> x1, matrix products: 38.5 us -> 0.19 us  [slot_codes(): inner = jnp.einsum('ij,bjo->bio', lower, blocks)]
    all_gather x4 -> x3, blocking collectives: 44.2 us -> 78.8 us  [the longest x1 51.2 us: shards(): tables = lax.all_gather(table, 'range', axis=0)]
    pallas_call x0 -> x6, Pallas kernels: none -> 32.4 us  [kernel_call(): return call(*operands)]
    gather x6 -> x0, local copies, waits for them, and re-layouts: 27.5 us -> none  [the longest x1 8.58 us: shards(): jnp.take(local_rank, jnp.minimum(source, rows - 1), axis=0)]
    all_to_all x3 -> x1, starting transfers between devices: 41 us -> 14.3 us  [exchange(): lax.all_to_all(parts, 'range', split_axis=0, concat_axis=0, tiled=True)]
    all_to_all x0 -> x1, blocking collectives: none -> 22.9 us  [exchange(): lax.all_to_all(parts, 'range', split_axis=0, concat_axis=0, tiled=True)]
    reduce_scatter x1 -> x0, waiting for transfers between devices: 22.6 us -> none  [shards(): lax.psum_scatter(partial_rows.astype(jnp.bfloat16), 'chan', scatter_dimen...]
    ppermute x2 -> x16, starting transfers between devices: 5.21 us -> 25.8 us  [the longest x6 9.76 us: gather_chan(): return [x] + [lax.ppermute(x, 'chan', turn(k)) for k in range(1, CHAN)]]
  transfers between devices with their start and end apart: 6 -> 18, of which waited for: 4 -> 10; matrix products, arithmetic and copies ran while one was open for 12% -> 3% of each run, Pallas kernels for 0% -> 6%
where the time goes in v1:
time: 221 us; the launch traced here: 220 us
  blocking collectives  102 us (46%)
  starting transfers between devices  40.2 us (18%)
  Pallas kernels  32.4 us (15%)
  waiting for transfers between devices  21.7 us (10%)
  between operations  13.6 us (6%)
  local copies, waits for them, and re-layouts  7.98 us (4%)
  other arithmetic  2.39 us (1%)
    all_gather x1, blocking collectives, shards(): tables = lax.all_gather(table, 'range', axis=0)  51.2 us
    pallas_call x6, Pallas kernels, kernel_call(): return call(*operands)  32.4 us
    all_to_all x1, blocking collectives, exchange(): lax.all_to_all(parts, 'range', split_axis=0, concat_axis=0, tiled=True)  22.9 us
    all_gather x1, blocking collectives, shards(): down_all = lax.all_gather(down_weight.T, 'chan', axis=0)  17.2 us
    ppermute x6, waiting for transfers between devices, gather_chan(): return [x] + [lax.ppermute(x, 'chan', turn(k)) for k in range(1, CHAN)]  14.4 us
    all_to_all x1, starting transfers between devices, exchange(): lax.all_to_all(parts, 'range', split_axis=0, concat_axis=0, tiled=True)  14.3 us
    all_gather x1, blocking collectives, shards(): up_all = lax.all_gather(up_weight.T, 'chan', axis=0)  10.3 us
    ppermute x6, starting transfers between devices, gather_chan(): return [x] + [lax.ppermute(x, 'chan', turn(k)) for k in range(1, CHAN)]  9.76 us
  transfers between devices with their start and end apart: 18, of which 10 were waited for; matrix products, arithmetic and copies ran while one was open for 3% of the time, Pallas kernels for 6%

profile of v1, /device:TPU:1, one launch (start us, length us, event | category | flops | bytes accessed | tf_op | source)
XLA Modules:
  0.0 220.1 jit_solution(11109073116936136713)
XLA Ops:
  7.3 2.1 collective-permute-start
  9.4 2.5 %collective-permute-start.1 = (bf16[64,1024]{1,0:T(8,128)(2,1)}, bf16[64,1024]{1,0:T(8,128)(2,1)S(1)}, u32[]{:S(2)}, u32[]{:S(2)}) collective-permute-start(bf16[64,1024]{1,0:T(8,128)(2,1)} %x_ref.1), channel_id=1, source_target_pairs={{0,2},{1,3},{2,0},{3,1},{4,6},{5,7},{6,4},{7,5},{8,10},{9,11},{10,... | collective-permute-start | bytes 393224 | tf_op jit(solution)/shard_map/gather_features/ppermute | solution.py:202
  14.4 3.4 %collective-permute-done.1.x2 = bf16[64,1024]{1,0:T(8,128)(2,1)S(1)} collective-permute-done((bf16[64,1024]{1,0:T(8,128)(2,1)}, bf16[64,1024]{1,0:T(8,128)(2,1)S(1)}, u32[]{:S(2)}, u32[]{:S(2)}) %collective-permute-start.1) | collective-permute-done | bytes 131104 | tf_op jit(solution)/shard_map/gather_features/ppermute | solution.py:202
  19.6 11.5 %attention.1.h0 = bf16[64,1024]{1,0:T(8,128)(2,1)S(1)} custom-call(s32[1]{0:T(128)} %bitcast.me_ref, bf16[64,1024]{1,0:T(8,128)(2,1)S(1)} %copy-done.2, bf16[64,1024]{1,0:T(8,128)(2,1)S(1)} %collective-permute-done.x1, bf16[64,1024]{1,0:T(8,128)(2,1)S(1)} %collective-permute-done.1.x2, bf16[64,1024]{1,0:T(8,128)(2,1)S(1)} %collective-permute-done.2.x3, ...), custom_call_target="tpu_custom_call" | custom-call | flops 4294967296 | bytes 1048576 | tf_op jit(solution)/shard_map/attention/pallas_call | solution.py:36
  31.2 2.0 collective-permute-start.4
  33.2 1.9 collective-permute-start.5
  35.1 5.3 %collective-permute-done.3.h1 = bf16[64,1024]{1,0:T(8,128)(2,1)S(1)} collective-permute-done((bf16[64,1024]{1,0:T(8,128)(2,1)S(1)}, bf16[64,1024]{1,0:T(8,128)(2,1)S(1)}, u32[]{:S(2)}, u32[]{:S(2)}) %collective-permute-start.3) | collective-permute-done | bytes 131104 | tf_op jit(solution)/shard_map/gather_heads/ppermute | solution.py:202
  40.4 4.1 %collective-permute-done.4.h2 = bf16[64,1024]{1,0:T(8,128)(2,1)S(1)} collective-permute-done((bf16[64,1024]{1,0:T(8,128)(2,1)S(1)}, bf16[64,1024]{1,0:T(8,128)(2,1)S(1)}, u32[]{:S(2)}, u32[]{:S(2)}) %collective-permute-start.4) | collective-permute-done | bytes 131104 | tf_op jit(solution)/shard_map/gather_heads/ppermute | solution.py:202
  44.5 1.7 collective-permute-done.5.h3
  46.1 2.2 send.1
  48.3 14.3 %all-to-all-start = ((bf16[64,16,128]{2,1,0:T(8,128)(2,1)}), bf16[64,16,128]{2,1,0:T(8,128)(2,1)S(1)}, u32[]{:S(2)}, u32[]{:S(2)}) async-start(bf16[64,16,128]{2,1,0:T(8,128)(2,1)} %bitcast.9), calls=%async_computation | async-start | bytes 524288 | tf_op jit(solution)/shard_map/send/all_to_all | solution.py:319
  63.8 51.2 %all-gather = s32[131072]{0:T(1024)S(1)} all-gather(s32[2048]{0:T(1024)S(1)} %select_reduce_fusion), channel_id=2, replica_groups=mesh['range'=64,'chan'=4] {'range'}, dimensions={0}, use_global_device_ids=true | all-gather | bytes 532480 | tf_op jit(solution)/shard_map/codes/all_gather | solution.py:241
  115.1 2.6 %reshape.49 = s32[64,2,64,16]{3,2,1,0:T(8,128)} reshape(s32[131072]{0:T(1024)S(1)} %all-gather) | data formatting | bytes 1048576 | tf_op jit(solution)/shard_map/codes/reshape | solution.py:243
  118.9 10.3 %all-gather.2 = bf16[1024,256]{0,1:T(8,128)(2,1)S(1)} all-gather(bf16[256,256]{0,1:T(8,128)(2,1)S(1)} %bitcast.58), channel_id=4, replica_groups=mesh['range'=64,'chan'=4] {'chan'}, dimensions={0}, use_global_device_ids=true | all-gather | bytes 655360 | tf_op jit(solution)/shard_map/gather_weights/all_gather | solution.py:232
  133.3 17.2 %all-gather.3 = bf16[1024,256]{0,1:T(8,128)(2,1)S(1)} all-gather(bf16[256,256]{0,1:T(8,128)(2,1)S(1)} %bitcast.59), channel_id=5, replica_groups=mesh['range'=64,'chan'=4] {'chan'}, dimensions={0}, use_global_device_ids=true | all-gather | bytes 655360 | tf_op jit(solution)/shard_map/gather_weights/all_gather | solution.py:233
  150.5 1.9 collective-permute-start.12
  152.4 3.1 %collective-permute-start.9 = (bf16[64,256]{1,0:T(8,128)(2,1)S(1)}, bf16[64,256]{1,0:T(8,128)(2,1)S(1)}, u32[]{:S(2)}, u32[]{:S(2)}) collective-permute-start(bf16[64,256]{1,0:T(8,128)(2,1)S(1)} %get-tuple-element.28), channel_id=1, source_target_pairs={{0,4},{4,8},{8,12},{12,16},{16,20},{20,24},{24,28},{28,32},{32,36}... | collective-permute-start | bytes 98312 | tf_op jit(solution)/shard_map/gather_window/ppermute | solution.py:287
  155.5 2.4 %collective-permute-start.6 = (bf16[3,64,256]{2,1,0:T(8,128)(2,1)S(1)}, bf16[3,64,256]{2,1,0:T(8,128)(2,1)S(1)}, u32[]{:S(2)}, u32[]{:S(2)}) collective-permute-start(bf16[3,64,256]{2,1,0:T(8,128)(2,1)S(1)} %get-tuple-element.16), channel_id=1, source_target_pairs={{0,1},{1,2},{2,3},{3,0},{4,5},{5,6},{6,7},{7,4},{8,9},{9,10},{10,1... | collective-permute-start | bytes 294920 | tf_op jit(solution)/shard_map/gather_window/ppermute | solution.py:280
  158.6 1.9 collective-permute-start.8
  161.2 2.5 %collective-permute-done.7.refs_2_ = bf16[3,64,256]{2,1,0:T(8,128)(2,1)S(1)} collective-permute-done((bf16[3,64,256]{2,1,0:T(8,128)(2,1)S(1)}, bf16[3,64,256]{2,1,0:T(8,128)(2,1)S(1)}, u32[]{:S(2)}, u32[]{:S(2)}) %collective-permute-start.7) | collective-permute-done | bytes 98336 | tf_op jit(solution)/shard_map/gather_window/ppermute | solution.py:280
  164.7 2.0 copy-done.1
  166.7 14.2 %conv_mlp.1 = (bf16[64,256]{1,0:T(8,128)(2,1)S(1)}, bf16[64,256]{1,0:T(8,128)(2,1)S(1)}, bf16[64,256]{1,0:T(8,128)(2,1)S(1)}, bf16[64,256]{1,0:T(8,128)(2,1)S(1)}) custom-call(s32[1]{0:T(128)} %bitcast.me_ref, bf16[3,64,256]{2,1,0:T(8,128)(2,1)S(1)} %get-tuple-element.15.refs_0_, bf16[3,64,256]{2,1,0:T(8,128)(2,1)S(1)} %collective-permute-done.6.refs_1_, ...), custom_call_target="tpu_custom_call" | custom-call | flops 4294967296 | bytes 1048576 | tf_op jit(solution)/shard_map/conv_mlp/pallas_call | solution.py:36
  181.2 3.2 %collective-permute-start.14 = (bf16[64,256]{1,0:T(8,128)(2,1)S(1)}, bf16[64,256]{1,0:T(8,128)(2,1)S(1)}, u32[]{:S(2)}, u32[]{:S(2)}) collective-permute-start(bf16[64,256]{1,0:T(8,128)(2,1)S(1)} %get-tuple-element.23), channel_id=1, source_target_pairs={{0,2},{1,3},{2,0},{3,1},{4,6},{5,7},{6,4},{7,5},{8,10},{9,11},{10,... | collective-permute-start | bytes 98312 | tf_op jit(solution)/shard_map/turn_back/ppermute | solution.py:303
  188.7 22.9 %all_to_all.10 = bf16[64,16,128]{2,1,0:T(8,128)(2,1)S(1)} all-to-all(bf16[64,16,128]{2,1,0:T(8,128)(2,1)S(1)} %bitcast.50), channel_id=1, replica_groups=mesh['range'=64,'chan'=4] {'range'}, dimensions={0} | all-to-all | bytes 524288 | tf_op jit(solution)/shard_map/back/all_to_all | solution.py:319
  (54 shorter events, 20.3 us)
Async XLA Ops:
  6.5 153.9 %copy-start = (s32[27,1024]{1,0:T(8,128)S(1)}, s32[27,1024]{1,0:T(8,128)}, u32[]{:S(2)}) copy-start(s32[27,1024]{1,0:T(8,128)} %param.10) | copy-start | bytes 331780
  6.5 158.1 %all-gather.6.cloned.1.call-start = ((), (), s32[]{:S(2)}) async-start(), calls=%async_computation.2 | async-start | bytes 4423680 | tf_op jit(solution)/shard_map/gather_weights/all_gather | solution.py:231
  7.3 7.1 %collective-permute-start = (bf16[64,1024]{1,0:T(8,128)(2,1)}, bf16[64,1024]{1,0:T(8,128)(2,1)S(1)}, u32[]{:S(2)}, u32[]{:S(2)}) collective-permute-start(bf16[64,1024]{1,0:T(8,128)(2,1)} %x_ref.1), channel_id=1, source_target_pairs={{0,1},{1,2},{2,3},{3,0},{4,5},{5,6},{6,7},{7,4},{8,9},{9,10},{10,1... | collective-permute-start | bytes 393224 | tf_op jit(solution)/shard_map/gather_features/ppermute | solution.py:202
  9.4 8.4 %collective-permute-start.1 = (bf16[64,1024]{1,0:T(8,128)(2,1)}, bf16[64,1024]{1,0:T(8,128)(2,1)S(1)}, u32[]{:S(2)}, u32[]{:S(2)}) collective-permute-start(bf16[64,1024]{1,0:T(8,128)(2,1)} %x_ref.1), channel_id=1, source_target_pairs={{0,2},{1,3},{2,0},{3,1},{4,6},{5,7},{6,4},{7,5},{8,10},{9,11},{10,... | collective-permute-start | bytes 393224 | tf_op jit(solution)/shard_map/gather_features/ppermute | solution.py:202
  11.8 5.9 %collective-permute-start.2 = (bf16[64,1024]{1,0:T(8,128)(2,1)}, bf16[64,1024]{1,0:T(8,128)(2,1)S(1)}, u32[]{:S(2)}, u32[]{:S(2)}) collective-permute-start(bf16[64,1024]{1,0:T(8,128)(2,1)} %x_ref.1), channel_id=1, source_target_pairs={{0,3},{1,0},{2,1},{3,2},{4,7},{5,4},{6,5},{7,6},{8,11},{9,8},{10,9... | collective-permute-start | bytes 393224 | tf_op jit(solution)/shard_map/gather_features/ppermute | solution.py:202
  19.5 15.5 %copy-start.7 = (s32[1024]{0:T(1024)S(1)}, s32[1024]{0:T(1024)}, u32[]{:S(2)}) copy-start(s32[1024]{0:T(1024)} %param.9) | copy-start | bytes 12292
  19.6 26.6 %copy-start.4 = (bf16[256,64]{0,1:T(8,128)(2,1)S(1)}, bf16[256,64]{0,1:T(8,128)(2,1)}, u32[]{:S(2)}) copy-start(bf16[256,64]{0,1:T(8,128)(2,1)} %param.12) | copy-start | bytes 98308
  31.0 9.3 %collective-permute-start.3 = (bf16[64,1024]{1,0:T(8,128)(2,1)S(1)}, bf16[64,1024]{1,0:T(8,128)(2,1)S(1)}, u32[]{:S(2)}, u32[]{:S(2)}) collective-permute-start(bf16[64,1024]{1,0:T(8,128)(2,1)S(1)} %attention.1.h0), channel_id=1, source_target_pairs={{0,1},{1,2},{2,3},{3,0},{4,5},{5,6},{6,7},{7,4},{8,9},{9,10},{10,1... | collective-permute-start | bytes 393224 | tf_op jit(solution)/shard_map/gather_heads/ppermute | solution.py:202
  31.2 13.2 %collective-permute-start.4 = (bf16[64,1024]{1,0:T(8,128)(2,1)S(1)}, bf16[64,1024]{1,0:T(8,128)(2,1)S(1)}, u32[]{:S(2)}, u32[]{:S(2)}) collective-permute-start(bf16[64,1024]{1,0:T(8,128)(2,1)S(1)} %attention.1.h0), channel_id=1, source_target_pairs={{0,2},{1,3},{2,0},{3,1},{4,6},{5,7},{6,4},{7,5},{8,10},{9,11},{10,... | collective-permute-start | bytes 393224 | tf_op jit(solution)/shard_map/gather_heads/ppermute | solution.py:202
  33.2 12.9 %collective-permute-start.5 = (bf16[64,1024]{1,0:T(8,128)(2,1)S(1)}, bf16[64,1024]{1,0:T(8,128)(2,1)S(1)}, u32[]{:S(2)}, u32[]{:S(2)}) collective-permute-start(bf16[64,1024]{1,0:T(8,128)(2,1)S(1)} %attention.1.h0), channel_id=1, source_target_pairs={{0,3},{1,0},{2,1},{3,2},{4,7},{5,4},{6,5},{7,6},{8,11},{9,8},{10,9... | collective-permute-start | bytes 393224 | tf_op jit(solution)/shard_map/gather_heads/ppermute | solution.py:202
  46.1 72.7 %copy-start.5 = (bf16[256,256]{1,0:T(8,128)(2,1)S(1)}, bf16[256,256]{1,0:T(8,128)(2,1)}, u32[]{:S(2)}) copy-start(bf16[256,256]{1,0:T(8,128)(2,1)} %param.14) | copy-start | bytes 393220
  48.3 80.9 %all-to-all-start = ((bf16[64,16,128]{2,1,0:T(8,128)(2,1)}), bf16[64,16,128]{2,1,0:T(8,128)(2,1)S(1)}, u32[]{:S(2)}, u32[]{:S(2)}) async-start(bf16[64,16,128]{2,1,0:T(8,128)(2,1)} %bitcast.9), calls=%async_computation | async-start | bytes 524288 | tf_op jit(solution)/shard_map/send/all_to_all | solution.py:319
  115.1 18.2 %copy-start.6 = (bf16[256,256]{1,0:T(8,128)(2,1)S(1)}, bf16[256,256]{1,0:T(8,128)(2,1)}, u32[]{:S(2)}) copy-start(bf16[256,256]{1,0:T(8,128)(2,1)} %param.15) | copy-start | bytes 393220
  130.7 27.3 %collective-permute-start.10 = (bf16[64,256]{1,0:T(8,128)(2,1)S(1)}, bf16[64,256]{1,0:T(8,128)(2,1)S(1)}, u32[]{:S(2)}, u32[]{:S(2)}) collective-permute-start(bf16[64,256]{1,0:T(8,128)(2,1)S(1)} %get-tuple-element.27), channel_id=1, source_target_pairs={{1,4},{5,8},{9,12},{13,16},{17,20},{21,24},{25,28},{29,32},{33,36}... | collective-permute-start | bytes 98312 | tf_op jit(solution)/shard_map/gather_window/ppermute | solution.py:287
  132.0 26.6 %collective-permute-start.11 = (bf16[64,256]{1,0:T(8,128)(2,1)S(1)}, bf16[64,256]{1,0:T(8,128)(2,1)S(1)}, u32[]{:S(2)}, u32[]{:S(2)}) collective-permute-start(bf16[64,256]{1,0:T(8,128)(2,1)S(1)} %get-tuple-element.26), channel_id=1, source_target_pairs={{2,4},{6,8},{10,12},{14,16},{18,20},{22,24},{26,28},{30,32},{34,36... | collective-permute-start | bytes 98312 | tf_op jit(solution)/shard_map/gather_window/ppermute | solution.py:287
  150.5 10.4 %collective-permute-start.12 = (bf16[64,256]{1,0:T(8,128)(2,1)S(1)}, bf16[64,256]{1,0:T(8,128)(2,1)S(1)}, u32[]{:S(2)}, u32[]{:S(2)}) collective-permute-start(bf16[64,256]{1,0:T(8,128)(2,1)S(1)} %get-tuple-element.25), channel_id=1, source_target_pairs={{3,4},{7,8},{11,12},{15,16},{19,20},{23,24},{27,28},{31,32},{35,36... | collective-permute-start | bytes 98312 | tf_op jit(solution)/shard_map/gather_window/ppermute | solution.py:287
  152.4 8.5 %collective-permute-start.9 = (bf16[64,256]{1,0:T(8,128)(2,1)S(1)}, bf16[64,256]{1,0:T(8,128)(2,1)S(1)}, u32[]{:S(2)}, u32[]{:S(2)}) collective-permute-start(bf16[64,256]{1,0:T(8,128)(2,1)S(1)} %get-tuple-element.28), channel_id=1, source_target_pairs={{0,4},{4,8},{8,12},{12,16},{16,20},{20,24},{24,28},{28,32},{32,36}... | collective-permute-start | bytes 98312 | tf_op jit(solution)/shard_map/gather_window/ppermute | solution.py:287
  155.5 5.6 %collective-permute-start.6 = (bf16[3,64,256]{2,1,0:T(8,128)(2,1)S(1)}, bf16[3,64,256]{2,1,0:T(8,128)(2,1)S(1)}, u32[]{:S(2)}, u32[]{:S(2)}) collective-permute-start(bf16[3,64,256]{2,1,0:T(8,128)(2,1)S(1)} %get-tuple-element.16), channel_id=1, source_target_pairs={{0,1},{1,2},{2,3},{3,0},{4,5},{5,6},{6,7},{7,4},{8,9},{9,10},{10,1... | collective-permute-start | bytes 294920 | tf_op jit(solution)/shard_map/gather_window/ppermute | solution.py:280
  157.9 5.7 %collective-permute-start.7 = (bf16[3,64,256]{2,1,0:T(8,128)(2,1)S(1)}, bf16[3,64,256]{2,1,0:T(8,128)(2,1)S(1)}, u32[]{:S(2)}, u32[]{:S(2)}) collective-permute-start(bf16[3,64,256]{2,1,0:T(8,128)(2,1)S(1)} %get-tuple-element.17), channel_id=1, source_target_pairs={{0,2},{1,3},{2,0},{3,1},{4,6},{5,7},{6,4},{7,5},{8,10},{9,11},{10,... | collective-permute-start | bytes 294920 | tf_op jit(solution)/shard_map/gather_window/ppermute | solution.py:280
  158.6 6.1 %collective-permute-start.8 = (bf16[3,64,256]{2,1,0:T(8,128)(2,1)S(1)}, bf16[3,64,256]{2,1,0:T(8,128)(2,1)S(1)}, u32[]{:S(2)}, u32[]{:S(2)}) collective-permute-start(bf16[3,64,256]{2,1,0:T(8,128)(2,1)S(1)} %get-tuple-element.18), channel_id=1, source_target_pairs={{0,3},{1,0},{2,1},{3,2},{4,7},{5,4},{6,5},{7,6},{8,11},{9,8},{10,9... | collective-permute-start | bytes 294920 | tf_op jit(solution)/shard_map/gather_window/ppermute | solution.py:280
  164.7 2.0 copy-start.1
  180.8 4.1 %collective-permute-start.13 = (bf16[64,256]{1,0:T(8,128)(2,1)S(1)}, bf16[64,256]{1,0:T(8,128)(2,1)S(1)}, u32[]{:S(2)}, u32[]{:S(2)}) collective-permute-start(bf16[64,256]{1,0:T(8,128)(2,1)S(1)} %get-tuple-element.22), channel_id=1, source_target_pairs={{0,1},{1,2},{2,3},{3,0},{4,5},{5,6},{6,7},{7,4},{8,9},{9,10},{10,1... | collective-permute-start | bytes 98312 | tf_op jit(solution)/shard_map/turn_back/ppermute | solution.py:303
  181.2 5.0 %collective-permute-start.14 = (bf16[64,256]{1,0:T(8,128)(2,1)S(1)}, bf16[64,256]{1,0:T(8,128)(2,1)S(1)}, u32[]{:S(2)}, u32[]{:S(2)}) collective-permute-start(bf16[64,256]{1,0:T(8,128)(2,1)S(1)} %get-tuple-element.23), channel_id=1, source_target_pairs={{0,2},{1,3},{2,0},{3,1},{4,6},{5,7},{6,4},{7,5},{8,10},{9,11},{10,... | collective-permute-start | bytes 98312 | tf_op jit(solution)/shard_map/turn_back/ppermute | solution.py:303
  184.4 2.8 %collective-permute-start.15 = (bf16[64,256]{1,0:T(8,128)(2,1)S(1)}, bf16[64,256]{1,0:T(8,128)(2,1)S(1)}, u32[]{:S(2)}, u32[]{:S(2)}) collective-permute-start(bf16[64,256]{1,0:T(8,128)(2,1)S(1)} %get-tuple-element.24), channel_id=1, source_target_pairs={{0,3},{1,0},{2,1},{3,2},{4,7},{5,4},{6,5},{7,6},{8,11},{9,8},{10,9... | collective-permute-start | bytes 98312 | tf_op jit(solution)/shard_map/turn_back/ppermute | solution.py:303
  (2 other events, 1.8 us)
Sparse Core Ops, SparseCore 0:
  9.2 54.7 all-gather.5

commit v2 on v1

v2 whole, which is shorter than its diff:
```python
import jax
import jax.numpy as jnp
from jax import lax
from jax.experimental import pallas as pl
from jax.experimental.pallas import tpu as pltpu
from jax.sharding import PartitionSpec as P

HD = 16
KER = 27
HW = 256
CHAN = 4
SLOTS = 32
HALF = SLOTS // 2
F32 = jnp.float32
BF16 = jnp.bfloat16

NN = (((1,), (0,)), ((), ()))
NT = (((1,), (1,)), ((), ()))
TN = (((0,), (0,)), ((), ()))


def dot(a, b, dims=NN):
    return lax.dot_general(a, b, dims, preferred_element_type=F32)


def kernel_call(body, outs, cost, operands, scratch=(), vmem=48):
    specs = [pl.BlockSpec(memory_space=pltpu.SMEM if x.shape == (1,) else pltpu.VMEM) for x in operands]
    call = pl.pallas_call(
        body,
        out_shape=outs,
        in_specs=specs,
        scratch_shapes=list(scratch),
        compiler_params=pltpu.CompilerParams(vmem_limit_bytes=vmem * 1024 * 1024),
        cost_estimate=pl.CostEstimate(flops=cost, bytes_accessed=1 << 20, transcendentals=0),
    )
    return call(*operands)


def column_norm(x):
    mean = jnp.mean(x, axis=0, keepdims=True)
    centred = x - mean
    var = jnp.mean(centred * centred, axis=0, keepdims=True)
    return (centred * lax.rsqrt(var + 1e-05)).astype(BF16)


def place_blocks(dst, blocks, me):
    for k, block in enumerate(blocks):
        owner = lax.rem(me + CHAN - k, CHAN)
        size = block.shape[0]
        dst[pl.ds(pl.multiple_of(owner * size, size), size), :] = block[...]


def attention_body(me_ref, x0, x1, x2, x3, w_ref, out_ref, xs, qkv):
    place_blocks(xs, (x0, x1, x2, x3), me_ref[0])
    rows = xs.shape[1]
    norm = column_norm(xs[...].astype(F32))
    proj = dot(w_ref[...], norm)
    width = out_ref.shape[0]
    qkv[0:width, :] = (proj[0:width].astype(BF16) * BF16(0.25)).astype(BF16)
    qkv[width:, :] = proj[width:].astype(BF16)
    ones = (lax.broadcasted_iota(jnp.int32, (HD, rows), 0) == 0).astype(F32).astype(BF16)
    block = 256
    for head in range(width // HD):
        lo = head * HD
        keys = qkv[width + lo : width + lo + HD, :]
        vals = jnp.concatenate([qkv[2 * width + lo : 2 * width + lo + HD, :], ones], axis=0)
        for part in range(rows // block):
            cols = slice(part * block, (part + 1) * block)
            scores = dot(qkv[lo : lo + HD, cols], keys, TN)
            top = jnp.max(scores, axis=1, keepdims=True)
            expo = jnp.exp(scores - top).astype(BF16)
            res = dot(vals, expo, NT)
            out_ref[lo : lo + HD, cols] = (res[0:HD] / res[HD : HD + 1]).astype(BF16)


def pack_body(core_ref, conv_ref, up_ref, down_ref, out_ref):
    half = pl.ds(pl.multiple_of(core_ref[0] * 128, 128), 128)
    rows = conv_ref.shape[0]
    out_ref[0:rows, :] = conv_ref[:, half]
    size = up_ref.shape[1]
    out_ref[rows : rows + size, :] = up_ref[half, :].astype(F32).T.astype(BF16)
    out_ref[rows + size :, :] = down_ref[half, :].astype(F32).T.astype(BF16)


def code_body(rank_ref, code_ref):
    rank = rank_ref[...]
    rows = rank.shape[1]
    owner = rank // rows
    onehot = (lax.broadcasted_iota(jnp.int32, (rows // HALF, rows), 0) == owner).astype(F32)
    up_to = lax.broadcasted_iota(jnp.int32, (rows, rows), 0) <= lax.broadcasted_iota(
        jnp.int32, (rows, rows), 1
    )
    count = dot(onehot.astype(BF16), up_to.astype(F32).astype(BF16))
    slot = jnp.sum(onehot * count, axis=0, keepdims=True).astype(jnp.int32) - 1
    high = (slot >= HALF).astype(jnp.int32)
    code_ref[...] = owner * HALF + slot + high * (rows - HALF)


def slot_match(code, half, start, size, cols):
    rows = lax.broadcasted_iota(jnp.int32, (size, cols), 0) + (start + half * 1024)
    return (rows == code).astype(F32).astype(BF16)


def send_body(me_ref, range_ref, h0, h1, h2, h3, x_ref, w_ref, code_ref, rank_ref, out_ref, hs):
    place_blocks(hs, (h0, h1, h2, h3), me_ref[0])
    first = (x_ref[...].astype(F32) + dot(w_ref[...], hs[...])).astype(BF16)
    zero = jnp.zeros_like(first)
    low = jnp.concatenate([first, zero], axis=0)
    high = jnp.concatenate([zero, first], axis=0)
    code = code_ref[...]
    rows = code.shape[1]
    local = rank_ref[...] % rows
    tens = (local // 32 + 1).astype(F32)
    ones = (local % 32).astype(F32)
    line = lax.broadcasted_iota(jnp.int32, (8, rows), 0)
    low_info = jnp.where(line == 0, tens, jnp.where(line == 1, ones, 0.0)).astype(BF16)
    high_info = jnp.where(line == 2, tens, jnp.where(line == 3, ones, 0.0)).astype(BF16)
    block = 256
    at = lax.rem(range_ref[0], 8) * HALF
    lane = lax.broadcasted_iota(jnp.int32, (8, 128), 1)
    keep = (lane >= at) & (lane < at + HALF)
    for start in range(0, rows, block):
        low_match = slot_match(code, 0, start, block, rows)
        high_match = slot_match(code, 1, start, block, rows)
        res = dot(low_match, low, NT) + dot(high_match, high, NT)
        info = dot(low_info, low_match, NT) + dot(high_info, high_match, NT)
        first_owner = start // HALF
        owners = block // HALF
        out_ref[first_owner : first_owner + owners, 0:HALF, :] = res.astype(BF16).reshape(
            owners, HALF, 128
        )
        for i in range(owners):
            turned = pltpu.roll(info, lax.rem(at + block - i * HALF, block), 1)
            out_ref[first_owner + i, HALF : HALF + 8, :] = jnp.where(
                keep, turned[:, 0:128], 0.0
            ).astype(BF16)


def group_body(got_ref, core_ref, quarters_ref, near_edge, far_edge, place_ref):
    core = core_ref[0]
    width = quarters_ref.shape[1]
    owners = got_ref.shape[0]
    slots = owners * HALF
    got = got_ref[:, 0:HALF, :].reshape(slots, 2 * width).astype(F32).T.astype(BF16)
    info = got_ref[:, HALF : HALF + 8, :].astype(F32).reshape(owners // 8, 8, 8, 128)
    info = jnp.sum(info, axis=1)
    info = jnp.concatenate([info[g] for g in range(owners // 8)], axis=1)
    low_place = info[0:1] * 32.0 + info[1:2] - 32.0
    high_place = info[2:3] * 32.0 + info[3:4] - 32.0
    place_ref[...] = jnp.concatenate([low_place, high_place, jnp.zeros((6, slots), F32)], axis=0)
    for q in range(CHAN):
        rows = lax.broadcasted_iota(jnp.int32, (256, slots), 0).astype(F32) + q * 256.0
        res = 0.0
        for half, place in enumerate((low_place, high_place)):
            match = (rows == place).astype(F32).astype(BF16)
            res += dot(got[half * width : (half + 1) * width], match, NT)
        quarters_ref[q] = res.astype(BF16)

    @pl.when(core == 0)
    def _():
        near_edge[...] = quarters_ref[CHAN - 1]
        far_edge[...] = quarters_ref[0]

    @pl.when(core == 1)
    def _():
        near_edge[...] = quarters_ref[0]
        far_edge[...] = quarters_ref[CHAN - 1]


def window_body(me_ref, core_ref, quarters_ref, near_edge, far_edge, m0, m1, m2, m3, ext):
    core = core_ref[0]
    for q in range(CHAN):
        ext[q + 1] = quarters_ref[q]

    @pl.when(core == 0)
    def _():
        ext[0] = far_edge[...]
        ext[CHAN + 1] = near_edge[...]

    @pl.when(core == 1)
    def _():
        ext[0] = near_edge[...]
        ext[CHAN + 1] = far_edge[...]

    for k, ref in enumerate((m0, m1, m2, m3)):
        ref[...] = ext[pl.ds(lax.rem(me_ref[0] + k, CHAN), 3)]


def conv_body(me_ref, core_ref, *refs):
    msgs = refs[0:4]
    near_ref, near_w, far_w = refs[4:7]
    outs = refs[7:11]
    win, third_ref = refs[11:13]
    me = me_ref[0]
    core = core_ref[0]
    quarter = 64
    whole = CHAN * quarter
    shift = 2 * core

    def rotated(owner):
        return pl.ds(pl.multiple_of(lax.rem(owner + shift, CHAN) * quarter, quarter), quarter)

    def weight(block, at, size):
        rows = pl.ds(pl.multiple_of(at, quarter), size)
        return jnp.concatenate([near_w[block, rows, :], far_w[block, rows, :]], axis=1)

    def kernel(j):
        return jnp.concatenate(
            [weight(lax.rem(i + shift, CHAN), j * quarter, quarter) for i in range(CHAN)], axis=0
        )

    for k in range(CHAN):
        at = rotated(me + CHAN - k)
        for b in range(3):
            win[at, b * 256 : (b + 1) * 256] = msgs[k][b]

    near = near_ref[...]
    target = jnp.where(near < 0, -1, near + lax.broadcasted_iota(jnp.int32, near.shape, 1))
    target = jnp.concatenate([target.astype(F32), jnp.zeros((5, whole), F32)], axis=0).T
    cols = lax.broadcasted_iota(jnp.int32, (256, 768), 1).astype(F32)
    second = win[:, 256:512].astype(F32)
    group = 3
    for start in range(0, KER, group):
        match = [(cols == target[:, j : j + 1]).astype(F32).astype(BF16) for j in range(start, start + group)]
        picked = dot(jnp.concatenate(match, axis=0), win[...], NT).astype(BF16)
        picked = jnp.concatenate([picked[i * 256 : (i + 1) * 256] for i in range(group)], axis=1)
        kernels = jnp.concatenate([kernel(j) for j in range(start, start + group)], axis=1)
        second += dot(kernels, picked, NT)
    second = second.astype(BF16)
    norm = column_norm(second.astype(F32))
    total = second.astype(F32)
    half = whole // 2
    lo, hi = half * core, half * (1 - core)
    for i in range(CHAN):
        base = KER * quarter
        up = jnp.concatenate([weight(i, base + lo, half), weight(i, base + hi, half)], axis=0)
        base = base + whole
        down = jnp.concatenate([weight(i, base + lo, half), weight(i, base + hi, half)], axis=0)
        hidden = dot(up, norm)
        hidden = (0.5 * hidden * (1.0 + lax.erf(hidden * (2.0 ** -0.5)))).astype(BF16)
        total += dot(down, hidden)
    third_ref[...] = total.astype(BF16)
    for k in range(CHAN):
        outs[k][...] = third_ref[rotated(me + k), :]


def back_body(me_ref, t0, t1, t2, t3, place_ref, out_ref, tmp):
    me = me_ref[0]
    for k, ref in enumerate((t0, t1, t2, t3)):
        tmp[lax.rem(me + CHAN - k, CHAN)] = ref[...]
    third = jnp.concatenate([tmp[q] for q in range(CHAN)], axis=1)
    zero = jnp.zeros_like(third)
    low = jnp.concatenate([third, zero], axis=0)
    high = jnp.concatenate([zero, third], axis=0)
    column = place_ref[...].T
    block = 256
    rank = lax.broadcasted_iota(jnp.int32, (block, third.shape[1]), 1).astype(F32)
    for start in range(0, column.shape[0], block):
        res = 0.0
        for half, rhs in enumerate((low, high)):
            match = (rank == column[start : start + block, half : half + 1]).astype(F32).astype(BF16)
            res += dot(match, rhs, NT)
        owner = start // HALF
        out_ref[owner : owner + block // HALF] = res.astype(BF16).reshape(block // HALF, HALF, 128)


def restore_body(got_ref, code_ref, out_ref):
    width = out_ref.shape[0]
    got = got_ref[...].reshape(-1, 2 * width).astype(F32).T.astype(BF16)
    code = code_ref[...]
    res = 0.0
    for half in range(2):
        for start in range(0, got.shape[1], 256):
            match = slot_match(code, half, start, 256, code.shape[1])
            res += dot(got[half * width : (half + 1) * width, start : start + 256], match)
    out_ref[...] = res.astype(BF16)


def turn(k):
    return [(i, (i + k) % CHAN) for i in range(CHAN)]


def gather_chan(x):
    return [x] + [lax.ppermute(x, "chan", turn(k)) for k in range(1, CHAN)]


def shards(
    features, hilbert_rank, neighbours, qkv_weight, out_weight, conv_weight, up_weight, down_weight
):
    quarter, rows = features.shape
    owners = lax.axis_size("range")
    me = lax.axis_index("chan").astype(jnp.int32)
    me_ref = me[None]
    sds = jax.ShapeDtypeStruct

    with jax.named_scope("gather_features"):
        blocks = gather_chan(features)
    core = lax.rem(lax.axis_index("range").astype(jnp.int32), 2)
    core_ref = core[None]
    rank = hilbert_rank[None, :]
    with jax.named_scope("gather_weights"):
        packed = kernel_call(
            pack_body,
            sds((KER * quarter + 2 * up_weight.shape[1], 128), BF16),
            1 << 20,
            [core_ref, conv_weight.reshape(KER * quarter, -1), up_weight, down_weight],
        )
        near_w = lax.all_gather(packed, "chan", axis=0)
    with jax.named_scope("codes"):
        code = kernel_call(code_body, sds((1, rows), jnp.int32), 1 << 20, [rank])

    qkv = jnp.transpose(qkv_weight, (0, 2, 1)).reshape(3 * quarter, -1)
    with jax.named_scope("attention"):
        heads = kernel_call(
            attention_body,
            sds((quarter, rows), BF16),
            1 << 32,
            [me_ref] + blocks + [qkv],
            [pltpu.VMEM((CHAN * quarter, rows), BF16), pltpu.VMEM((3 * quarter, rows), BF16)],
        )
    with jax.named_scope("gather_heads"):
        blocks = gather_chan(heads)
    with jax.named_scope("send"):
        range_ref = lax.axis_index("range").astype(jnp.int32)[None]
        send = kernel_call(
            send_body,
            sds((owners, HALF + 8, 2 * quarter), BF16),
            1 << 30,
            [me_ref, range_ref] + blocks + [features, out_weight.T, code, rank],
            [pltpu.VMEM((CHAN * quarter, rows), BF16)],
        )
        got = exchange(send)
        near_w, got = lax.optimization_barrier((near_w, got))
        far_w = lax.ppermute(near_w, "range", [(i, i ^ 1) for i in range(owners)])
    with jax.named_scope("group"):
        part = sds((3, quarter, 256), BF16)
        edge = sds((quarter, 256), BF16)
        quarters, near_edge, far_edge, place = kernel_call(
            group_body,
            (sds((CHAN, quarter, 256), BF16), edge, edge, sds((8, rows), F32)),
            1 << 30,
            [got, core_ref],
        )
    with jax.named_scope("halo"):
        near_edge = lax.ppermute(near_edge, "range", [(i, i ^ 1) for i in range(owners)])
        pairs = [(i, i + 1) for i in range(1, owners - 1, 2)]
        far_edge = lax.ppermute(far_edge, "range", pairs + [(j, i) for i, j in pairs])
    with jax.named_scope("gather_window"):
        msgs = kernel_call(
            window_body,
            (part, part, part, part),
            1 << 20,
            [me_ref, core_ref, quarters, near_edge, far_edge],
            [pltpu.VMEM((CHAN + 2, quarter, 256), BF16)],
        )
        msgs = [msgs[0]] + [lax.ppermute(msgs[k], "chan", turn(k)) for k in range(1, CHAN)]
    with jax.named_scope("conv_mlp"):
        near = lax.dynamic_slice_in_dim(neighbours, me * 256, 256, 1)
        thirds = kernel_call(
            conv_body,
            (edge, edge, edge, edge),
            1 << 32,
            [me_ref, core_ref] + msgs + [near, near_w, far_w],
            [
                pltpu.VMEM((CHAN * quarter, 768), BF16),
                pltpu.VMEM((CHAN * quarter, 256), BF16),
            ],
        )
    with jax.named_scope("turn_back"):
        thirds = [thirds[0]] + [lax.ppermute(thirds[k], "chan", turn(k)) for k in range(1, CHAN)]
    with jax.named_scope("back"):
        back = kernel_call(
            back_body,
            sds((owners, HALF, 2 * quarter), BF16),
            1 << 30,
            [me_ref] + thirds + [place],
            [pltpu.VMEM((CHAN, quarter, 256), BF16)],
        )
        returned = exchange(back)
    with jax.named_scope("restore"):
        return kernel_call(restore_body, sds((quarter, rows), BF16), 1 << 30, [returned, code])


def exchange(parts):
    return lax.all_to_all(parts, "range", split_axis=0, concat_axis=0, tiled=True)


def solution(mesh):
    in_specs = (
        P("chan", "range"),
        P("range"),
        P(None, "range"),
        P(None, None, "chan"),
        P(None, "chan"),
        P(None, "chan", None),
        P(None, "chan"),
        P("chan", None),
    )
    out_specs = P("chan", "range")
    return jax.shard_map(shards, mesh=mesh, in_specs=in_specs, out_specs=out_specs, check_vma=False)
```

time: 221 us -> 133 us (0.60)
  blocking collectives: 102 us -> 50.1 us
  starting transfers between devices: 40.2 us -> 18 us
  Pallas kernels: 32.4 us -> 21.1 us
  waiting for transfers between devices: 21.7 us -> 27.1 us
  local copies, waits for them, and re-layouts: 7.98 us -> 3.04 us
  other arithmetic: 2.39 us -> 0 us
    all_gather x3 -> x0, blocking collectives: 78.8 us -> none  [the longest x1 51.2 us: shards(): tables = lax.all_gather(table, 'range', axis=0)]
    all_to_all x1 -> x2, blocking collectives: 22.9 us -> 50.1 us  [exchange(): lax.all_to_all(parts, 'range', split_axis=0, concat_axis=0, tiled=True)]
    all_to_all x1 -> x0, starting transfers between devices: 14.3 us -> none  [exchange(): lax.all_to_all(parts, 'range', split_axis=0, concat_axis=0, tiled=True)]
    pallas_call x6 -> x9, Pallas kernels: 32.4 us -> 21.1 us  [kernel_call(): return call(*operands)]
    ppermute x6, waiting for transfers between devices: 14.4 us -> 19.6 us  [gather_chan(): return [x] + [lax.ppermute(x, 'chan', turn(k)) for k in range(1, CHAN)]]
    ppermute x7 -> x6, starting transfers between devices: 12.5 us -> 8.5 us  [the longest x3 4.54 us: shards(): lax.ppermute(msgs[k], 'chan', turn(k))]
    ppermute x6, starting transfers between devices: 9.76 us -> 5.98 us  [gather_chan(): return [x] + [lax.ppermute(x, 'chan', turn(k)) for k in range(1, CHAN)]]
    reshape x2 -> x0, local copies, waits for them, and re-layouts: 2.65 us -> none  [the longest x1 2.55 us: shards(): tables.reshape(owners, 2, owners, HALF)]
  transfers between devices with their start and end apart: 18 -> 16, of which waited for: 10 -> 13; matrix products, arithmetic and copies ran while one was open for 3% -> 0% of each run, Pallas kernels for 6% -> 6%
where the time goes in v2:
time: 133 us
  blocking collectives  50.1 us (38%)
  waiting for transfers between devices  27.1 us (20%)
  Pallas kernels  21.1 us (16%)
  starting transfers between devices  18 us (14%)
  between operations  13.5 us (10%)
  local copies, waits for them, and re-layouts  3.04 us (2%)
    all_to_all x2, blocking collectives, exchange(): lax.all_to_all(parts, 'range', split_axis=0, concat_axis=0, tiled=True)  50.1 us
    pallas_call x9, Pallas kernels, kernel_call(): return call(*operands)  21.1 us
    ppermute x6, waiting for transfers between devices, gather_chan(): return [x] + [lax.ppermute(x, 'chan', turn(k)) for k in range(1, CHAN)]  19.6 us
    ppermute x6, starting transfers between devices, gather_chan(): return [x] + [lax.ppermute(x, 'chan', turn(k)) for k in range(1, CHAN)]  5.98 us
    ppermute x3, starting transfers between devices, shards(): lax.ppermute(msgs[k], 'chan', turn(k))  4.54 us
    ppermute x3, waiting for transfers between devices, shards(): lax.ppermute(msgs[k], 'chan', turn(k))  3.59 us
    ppermute x3, starting transfers between devices, shards(): lax.ppermute(thirds[k], 'chan', turn(k))  3.53 us
    ppermute x1, starting transfers between devices, shards(): lax.ppermute(far_edge, 'range', pairs + [(j, i) for i, j in pairs])  3.36 us
  transfers between devices with their start and end apart: 16, of which 13 were waited for; matrix products, arithmetic and copies ran while one was open for 0% of the time, Pallas kernels for 6%

profile of v2, /device:TPU:1, one launch (start us, length us, event | category | flops | bytes accessed | tf_op | source)
XLA Modules:
  0.0 132.8 jit_solution(7700678023756892807)
XLA Ops:
  6.5 1.2 copy-done.1
  10.5 3.4 %collective-permute-start.2 = (bf16[64,1024]{1,0:T(8,128)(2,1)S(1)}, bf16[64,1024]{1,0:T(8,128)(2,1)S(1)}, u32[]{:S(2)}, u32[]{:S(2)}) collective-permute-start(bf16[64,1024]{1,0:T(8,128)(2,1)S(1)} %copy-done.6), channel_id=1, source_target_pairs={{0,3},{1,0},{2,1},{3,2},{4,7},{5,4},{6,5},{7,6},{8,11},{9,8},{10,9... | collective-permute-start | bytes 393224 | tf_op jit(solution)/shard_map/gather_features/ppermute | solution.py:284
  15.0 2.4 %collective-permute-done.2.x3 = bf16[64,1024]{1,0:T(8,128)(2,1)S(1)} collective-permute-done((bf16[64,1024]{1,0:T(8,128)(2,1)S(1)}, bf16[64,1024]{1,0:T(8,128)(2,1)S(1)}, u32[]{:S(2)}, u32[]{:S(2)}) %collective-permute-start.2) | collective-permute-done | bytes 131104 | tf_op jit(solution)/shard_map/gather_features/ppermute | solution.py:284
  17.5 1.9 %collective-permute-done.1.x2 = bf16[64,1024]{1,0:T(8,128)(2,1)S(1)} collective-permute-done((bf16[64,1024]{1,0:T(8,128)(2,1)S(1)}, bf16[64,1024]{1,0:T(8,128)(2,1)S(1)}, u32[]{:S(2)}, u32[]{:S(2)}) %collective-permute-start.1) | collective-permute-done | bytes 131104 | tf_op jit(solution)/shard_map/gather_features/ppermute | solution.py:284
  19.3 4.1 %collective-permute-done.x1 = bf16[64,1024]{1,0:T(8,128)(2,1)S(1)} collective-permute-done((bf16[64,1024]{1,0:T(8,128)(2,1)S(1)}, bf16[64,1024]{1,0:T(8,128)(2,1)S(1)}, u32[]{:S(2)}, u32[]{:S(2)}) %collective-permute-start) | collective-permute-done | bytes 131104 | tf_op jit(solution)/shard_map/gather_features/ppermute | solution.py:284
  23.5 5.5 %attention.1.h0 = bf16[64,1024]{1,0:T(8,128)(2,1)S(1)} custom-call(s32[1]{0:T(128)} %bitcast.me_ref, bf16[64,1024]{1,0:T(8,128)(2,1)S(1)} %copy-done.6, bf16[64,1024]{1,0:T(8,128)(2,1)S(1)} %collective-permute-done.x1, bf16[64,1024]{1,0:T(8,128)(2,1)S(1)} %collective-permute-done.1.x2, bf16[64,1024]{1,0:T(8,128)(2,1)S(1)} %collective-permute-done.2.x3, ...), custom_call_target="tpu_custom_call" | custom-call | flops 4294967296 | bytes 1048576 | tf_op jit(solution)/shard_map/attention/pallas_call | solution.py:36
  29.2 1.2 collective-permute-start.3
  30.9 6.0 %collective-permute-done.5.h3 = bf16[64,1024]{1,0:T(8,128)(2,1)S(1)} collective-permute-done((bf16[64,1024]{1,0:T(8,128)(2,1)S(1)}, bf16[64,1024]{1,0:T(8,128)(2,1)S(1)}, u32[]{:S(2)}, u32[]{:S(2)}) %collective-permute-start.5) | collective-permute-done | bytes 131104 | tf_op jit(solution)/shard_map/gather_heads/ppermute | solution.py:284
  36.9 1.5 %collective-permute-done.4.h2 = bf16[64,1024]{1,0:T(8,128)(2,1)S(1)} collective-permute-done((bf16[64,1024]{1,0:T(8,128)(2,1)S(1)}, bf16[64,1024]{1,0:T(8,128)(2,1)S(1)}, u32[]{:S(2)}, u32[]{:S(2)}) %collective-permute-start.4) | collective-permute-done | bytes 131104 | tf_op jit(solution)/shard_map/gather_heads/ppermute | solution.py:284
  38.4 3.7 %collective-permute-done.3.h1 = bf16[64,1024]{1,0:T(8,128)(2,1)S(1)} collective-permute-done((bf16[64,1024]{1,0:T(8,128)(2,1)S(1)}, bf16[64,1024]{1,0:T(8,128)(2,1)S(1)}, u32[]{:S(2)}, u32[]{:S(2)}) %collective-permute-start.3) | collective-permute-done | bytes 131104 | tf_op jit(solution)/shard_map/gather_heads/ppermute | solution.py:284
  42.1 2.6 %send.1 = bf16[64,24,128]{2,1,0:T(8,128)(2,1)S(1)} custom-call(s32[1]{0:T(128)} %bitcast.me_ref, s32[1]{0:T(128)} %bitcast.4.range_ref, bf16[64,1024]{1,0:T(8,128)(2,1)S(1)} %attention.1.h0, bf16[64,1024]{1,0:T(8,128)(2,1)S(1)} %collective-permute-done.3.h1, bf16[64,1024]{1,0:T(8,128)(2,1)S(1)} %collective-permute-done.4.h2, ...), custom_call_target="tpu_custom_call" | custom-call | flops 1073741824 | bytes 1048576 | tf_op jit(solution)/shard_map/send/pallas_call | solution.py:36
  44.7 27.4 %all_to_all.10.got_ref = bf16[64,24,128]{2,1,0:T(8,128)(2,1)S(1)} all-to-all(bf16[64,24,128]{2,1,0:T(8,128)(2,1)S(1)} %send.1), channel_id=1, replica_groups=mesh['range'=64,'chan'=4] {'range'}, dimensions={0} | all-to-all | bytes 786432 | tf_op jit(solution)/shard_map/send/all_to_all | solution.py:385
  72.4 1.4 %group.1 = (bf16[4,64,256]{2,1,0:T(8,128)(2,1)S(1)}, bf16[64,256]{1,0:T(8,128)(2,1)S(1)}, bf16[64,256]{1,0:T(8,128)(2,1)S(1)}, f32[8,1024]{1,0:T(8,128)S(1)}) custom-call(bf16[64,24,128]{2,1,0:T(8,128)(2,1)S(1)} %all_to_all.10.got_ref, s32[1]{0:T(128)} %bitcast.1.core_ref), custom_call_target="tpu_custom_call" | custom-call | flops 1073741824 | bytes 1048576 | tf_op jit(solution)/shard_map/group/pallas_call | solution.py:36
  74.1 3.4 %collective-permute-start.7 = (bf16[64,256]{1,0:T(8,128)(2,1)S(1)}, bf16[64,256]{1,0:T(8,128)(2,1)S(1)}, u32[]{:S(2)}, u32[]{:S(2)}) collective-permute-start(bf16[64,256]{1,0:T(8,128)(2,1)S(1)} %get-tuple-element.22), channel_id=1, source_target_pairs={{4,8},{12,16},{20,24},{28,32},{36,40},{44,48},{52,56},{60,64},{68,... | collective-permute-start | bytes 98312 | tf_op jit(solution)/shard_map/halo/ppermute | solution.py:347
  77.4 1.8 %collective-permute-done.7.far_edge = bf16[64,256]{1,0:T(8,128)(2,1)S(1)} collective-permute-done((bf16[64,256]{1,0:T(8,128)(2,1)S(1)}, bf16[64,256]{1,0:T(8,128)(2,1)S(1)}, u32[]{:S(2)}, u32[]{:S(2)}) %collective-permute-start.7) | collective-permute-done | bytes 32800 | tf_op jit(solution)/shard_map/halo/ppermute | solution.py:347
  79.3 1.8 %collective-permute-start.8 = (bf16[3,64,256]{2,1,0:T(8,128)(2,1)S(1)}, bf16[3,64,256]{2,1,0:T(8,128)(2,1)S(1)}, u32[]{:S(2)}, u32[]{:S(2)}) collective-permute-start(bf16[3,64,256]{2,1,0:T(8,128)(2,1)S(1)} %get-tuple-element.24), channel_id=1, source_target_pairs={{0,1},{1,2},{2,3},{3,0},{4,5},{5,6},{6,7},{7,4},{8,9},{9,10},{10,1... | collective-permute-start | bytes 294920 | tf_op jit(solution)/shard_map/gather_window/ppermute | solution.py:356
  81.1 2.8 %collective-permute-start.9 = (bf16[3,64,256]{2,1,0:T(8,128)(2,1)S(1)}, bf16[3,64,256]{2,1,0:T(8,128)(2,1)S(1)}, u32[]{:S(2)}, u32[]{:S(2)}) collective-permute-start(bf16[3,64,256]{2,1,0:T(8,128)(2,1)S(1)} %get-tuple-element.25), channel_id=1, source_target_pairs={{0,2},{1,3},{2,0},{3,1},{4,6},{5,7},{6,4},{7,5},{8,10},{9,11},{10,... | collective-permute-start | bytes 294920 | tf_op jit(solution)/shard_map/gather_window/ppermute | solution.py:356
  83.9 1.9 %collective-permute-done.8.refs_1_ = bf16[3,64,256]{2,1,0:T(8,128)(2,1)S(1)} collective-permute-done((bf16[3,64,256]{2,1,0:T(8,128)(2,1)S(1)}, bf16[3,64,256]{2,1,0:T(8,128)(2,1)S(1)}, u32[]{:S(2)}, u32[]{:S(2)}) %collective-permute-start.8) | collective-permute-done | bytes 98336 | tf_op jit(solution)/shard_map/gather_window/ppermute | solution.py:356
  85.7 1.4 %collective-permute-done.9.refs_2_ = bf16[3,64,256]{2,1,0:T(8,128)(2,1)S(1)} collective-permute-done((bf16[3,64,256]{2,1,0:T(8,128)(2,1)S(1)}, bf16[3,64,256]{2,1,0:T(8,128)(2,1)S(1)}, u32[]{:S(2)}, u32[]{:S(2)}) %collective-permute-start.9) | collective-permute-done | bytes 98336 | tf_op jit(solution)/shard_map/gather_window/ppermute | solution.py:356
  87.5 7.0 %conv_mlp.1 = (bf16[64,256]{1,0:T(8,128)(2,1)S(1)}, bf16[64,256]{1,0:T(8,128)(2,1)S(1)}, bf16[64,256]{1,0:T(8,128)(2,1)S(1)}, bf16[64,256]{1,0:T(8,128)(2,1)S(1)}) custom-call(s32[1]{0:T(128)} %bitcast.me_ref, s32[1]{0:T(128)} %bitcast.1.core_ref, bf16[3,64,256]{2,1,0:T(8,128)(2,1)S(1)} %get-tuple-element.23.refs_0_, ...), custom_call_target="tpu_custom_call" | custom-call | flops 4294967296 | bytes 1048576 | tf_op jit(solution)/shard_map/conv_mlp/pallas_call | solution.py:36
  94.8 2.5 %collective-permute-start.13 = (bf16[64,256]{1,0:T(8,128)(2,1)S(1)}, bf16[64,256]{1,0:T(8,128)(2,1)S(1)}, u32[]{:S(2)}, u32[]{:S(2)}) collective-permute-start(bf16[64,256]{1,0:T(8,128)(2,1)S(1)} %get-tuple-element.30), channel_id=1, source_target_pairs={{0,2},{1,3},{2,0},{3,1},{4,6},{5,7},{6,4},{7,5},{8,10},{9,11},{10,... | collective-permute-start | bytes 98312 | tf_op jit(solution)/shard_map/turn_back/ppermute | solution.py:370
  100.1 1.5 %back.1 = bf16[64,16,128]{2,1,0:T(8,128)(2,1)S(1)} custom-call(s32[1]{0:T(128)} %bitcast.me_ref, bf16[64,256]{1,0:T(8,128)(2,1)S(1)} %get-tuple-element.28.t0, bf16[64,256]{1,0:T(8,128)(2,1)S(1)} %collective-permute-done.12.t1, bf16[64,256]{1,0:T(8,128)(2,1)S(1)} %collective-permute-done.13.t2, bf16[64,256]{1,0:T(8,128)(2,1)S(1)} %collective-permute-done.14.t3, ...), custom_call_target="tpu_custom_call" | custom-call | flops 1073741824 | bytes 1048576 | tf_op jit(solution)/shard_map/back/pallas_call | solution.py:36
  101.6 22.7 %all_to_all.11.got_ref = bf16[64,16,128]{2,1,0:T(8,128)(2,1)S(1)} all-to-all(bf16[64,16,128]{2,1,0:T(8,128)(2,1)S(1)} %back.1), channel_id=1, replica_groups=mesh['range'=64,'chan'=4] {'range'}, dimensions={0} | all-to-all | bytes 524288 | tf_op jit(solution)/shard_map/back/all_to_all | solution.py:385
  124.3 1.6 %restore.1 = bf16[64,1024]{1,0:T(8,128)(2,1)} custom-call(bf16[64,16,128]{2,1,0:T(8,128)(2,1)S(1)} %all_to_all.11.got_ref, s32[1,1024]{1,0:T(1,128)S(1)} %codes.1.code_ref), custom_call_target="tpu_custom_call" | custom-call | flops 1073741824 | bytes 1048576 | tf_op jit(solution)/shard_map/restore/pallas_call | solution.py:36
  (39 shorter events, 8.6 us)
Async XLA Ops:
  6.5 77.3 %copy-start = (s32[27,1024]{1,0:T(8,128)S(1)}, s32[27,1024]{1,0:T(8,128)}, u32[]{:S(2)}) copy-start(s32[27,1024]{1,0:T(8,128)} %param.10) | copy-start | bytes 331780
  6.5 65.5 %all-gather.3.cloned.1.call-start = ((), (), s32[]{:S(2)}) async-start(), calls=%async_computation.2 | async-start | bytes 2867200 | tf_op jit(solution)/shard_map/gather_weights/all_gather | solution.py:308
  6.5 1.2 copy-start.1
  7.7 0.9 copy-start.2
  9.6 1.0 copy-start.6
  9.6 13.9 %copy-start.7 = (bf16[3,256,64]{1,2,0:T(8,128)(2,1)S(1)}, bf16[3,256,64]{1,2,0:T(8,128)(2,1)}, u32[]{:S(2)}) copy-start(bf16[3,256,64]{1,2,0:T(8,128)(2,1)} %param.11) | copy-start | bytes 294916
  10.5 6.9 %collective-permute-start.2 = (bf16[64,1024]{1,0:T(8,128)(2,1)S(1)}, bf16[64,1024]{1,0:T(8,128)(2,1)S(1)}, u32[]{:S(2)}, u32[]{:S(2)}) collective-permute-start(bf16[64,1024]{1,0:T(8,128)(2,1)S(1)} %copy-done.6), channel_id=1, source_target_pairs={{0,3},{1,0},{2,1},{3,2},{4,7},{5,4},{6,5},{7,6},{8,11},{9,8},{10,9... | collective-permute-start | bytes 393224 | tf_op jit(solution)/shard_map/gather_features/ppermute | solution.py:284
  13.9 5.4 %collective-permute-start.1 = (bf16[64,1024]{1,0:T(8,128)(2,1)S(1)}, bf16[64,1024]{1,0:T(8,128)(2,1)S(1)}, u32[]{:S(2)}, u32[]{:S(2)}) collective-permute-start(bf16[64,1024]{1,0:T(8,128)(2,1)S(1)} %copy-done.6), channel_id=1, source_target_pairs={{0,2},{1,3},{2,0},{3,1},{4,6},{5,7},{6,4},{7,5},{8,10},{9,11},{10,... | collective-permute-start | bytes 393224 | tf_op jit(solution)/shard_map/gather_features/ppermute | solution.py:284
  14.4 9.0 %collective-permute-start = (bf16[64,1024]{1,0:T(8,128)(2,1)S(1)}, bf16[64,1024]{1,0:T(8,128)(2,1)S(1)}, u32[]{:S(2)}, u32[]{:S(2)}) collective-permute-start(bf16[64,1024]{1,0:T(8,128)(2,1)S(1)} %copy-done.6), channel_id=1, source_target_pairs={{0,1},{1,2},{2,3},{3,0},{4,5},{5,6},{6,7},{7,4},{8,9},{9,10},{10,1... | collective-permute-start | bytes 393224 | tf_op jit(solution)/shard_map/gather_features/ppermute | solution.py:284
  23.5 7.0 %copy-start.4 = (s32[1024]{0:T(1024)S(1)}, s32[1024]{0:T(1024)}, u32[]{:S(2)}) copy-start(s32[1024]{0:T(1024)} %param.9) | copy-start | bytes 12292
  23.5 18.6 %copy-start.8 = (bf16[256,64]{0,1:T(8,128)(2,1)S(1)}, bf16[256,64]{0,1:T(8,128)(2,1)}, u32[]{:S(2)}) copy-start(bf16[256,64]{0,1:T(8,128)(2,1)} %param.12) | copy-start | bytes 98308
  29.0 7.9 %collective-permute-start.5 = (bf16[64,1024]{1,0:T(8,128)(2,1)S(1)}, bf16[64,1024]{1,0:T(8,128)(2,1)S(1)}, u32[]{:S(2)}, u32[]{:S(2)}) collective-permute-start(bf16[64,1024]{1,0:T(8,128)(2,1)S(1)} %attention.1.h0), channel_id=1, source_target_pairs={{0,3},{1,0},{2,1},{3,2},{4,7},{5,4},{6,5},{7,6},{8,11},{9,8},{10,9... | collective-permute-start | bytes 393224 | tf_op jit(solution)/shard_map/gather_heads/ppermute | solution.py:284
  29.0 9.4 %collective-permute-start.4 = (bf16[64,1024]{1,0:T(8,128)(2,1)S(1)}, bf16[64,1024]{1,0:T(8,128)(2,1)S(1)}, u32[]{:S(2)}, u32[]{:S(2)}) collective-permute-start(bf16[64,1024]{1,0:T(8,128)(2,1)S(1)} %attention.1.h0), channel_id=1, source_target_pairs={{0,2},{1,3},{2,0},{3,1},{4,6},{5,7},{6,4},{7,5},{8,10},{9,11},{10,... | collective-permute-start | bytes 393224 | tf_op jit(solution)/shard_map/gather_heads/ppermute | solution.py:284
  29.2 12.8 %collective-permute-start.3 = (bf16[64,1024]{1,0:T(8,128)(2,1)S(1)}, bf16[64,1024]{1,0:T(8,128)(2,1)S(1)}, u32[]{:S(2)}, u32[]{:S(2)}) collective-permute-start(bf16[64,1024]{1,0:T(8,128)(2,1)S(1)} %attention.1.h0), channel_id=1, source_target_pairs={{0,1},{1,2},{2,3},{3,0},{4,5},{5,6},{6,7},{7,4},{8,9},{9,10},{10,1... | collective-permute-start | bytes 393224 | tf_op jit(solution)/shard_map/gather_heads/ppermute | solution.py:284
  72.0 15.4 %copy-start.5 = (bf16[8960,128]{1,0:T(8,128)(2,1)S(1)}, bf16[8960,128]{1,0:T(8,128)(2,1)}, u32[]{:S(2)}) copy-start(bf16[8960,128]{1,0:T(8,128)(2,1)} %all-gather.3.cloned.1.call-done) | copy-start | bytes 6881284
  72.0 15.4 %collective-permute-start.11 = (bf16[4,2240,128]{2,1,0:T(8,128)(2,1)}, bf16[4,2240,128]{2,1,0:T(8,128)(2,1)}, u32[]{:S(2)}, u32[]{:S(2)}) collective-permute-start(bf16[4,2240,128]{2,1,0:T(8,128)(2,1)} %bitcast.13), channel_id=1, source_target_pairs={{0,4},{4,0},{8,12},{12,8},{16,20},{20,16},{24,28},{28,24},{32,36},... | collective-permute-start | bytes 6881288 | tf_op jit(solution)/shard_map/send/ppermute | solution.py:334
  73.9 3.6 %collective-permute-start.6 = (bf16[64,256]{1,0:T(8,128)(2,1)S(1)}, bf16[64,256]{1,0:T(8,128)(2,1)S(1)}, u32[]{:S(2)}, u32[]{:S(2)}) collective-permute-start(bf16[64,256]{1,0:T(8,128)(2,1)S(1)} %get-tuple-element.21), channel_id=1, source_target_pairs={{0,4},{4,0},{8,12},{12,8},{16,20},{20,16},{24,28},{28,24},{32,36},... | collective-permute-start | bytes 98312 | tf_op jit(solution)/shard_map/halo/ppermute | solution.py:345
  74.1 5.2 %collective-permute-start.7 = (bf16[64,256]{1,0:T(8,128)(2,1)S(1)}, bf16[64,256]{1,0:T(8,128)(2,1)S(1)}, u32[]{:S(2)}, u32[]{:S(2)}) collective-permute-start(bf16[64,256]{1,0:T(8,128)(2,1)S(1)} %get-tuple-element.22), channel_id=1, source_target_pairs={{4,8},{12,16},{20,24},{28,32},{36,40},{44,48},{52,56},{60,64},{68,... | collective-permute-start | bytes 98312 | tf_op jit(solution)/shard_map/halo/ppermute | solution.py:347
  79.3 6.4 %collective-permute-start.8 = (bf16[3,64,256]{2,1,0:T(8,128)(2,1)S(1)}, bf16[3,64,256]{2,1,0:T(8,128)(2,1)S(1)}, u32[]{:S(2)}, u32[]{:S(2)}) collective-permute-start(bf16[3,64,256]{2,1,0:T(8,128)(2,1)S(1)} %get-tuple-element.24), channel_id=1, source_target_pairs={{0,1},{1,2},{2,3},{3,0},{4,5},{5,6},{6,7},{7,4},{8,9},{9,10},{10,1... | collective-permute-start | bytes 294920 | tf_op jit(solution)/shard_map/gather_window/ppermute | solution.py:356
  81.1 6.0 %collective-permute-start.9 = (bf16[3,64,256]{2,1,0:T(8,128)(2,1)S(1)}, bf16[3,64,256]{2,1,0:T(8,128)(2,1)S(1)}, u32[]{:S(2)}, u32[]{:S(2)}) collective-permute-start(bf16[3,64,256]{2,1,0:T(8,128)(2,1)S(1)} %get-tuple-element.25), channel_id=1, source_target_pairs={{0,2},{1,3},{2,0},{3,1},{4,6},{5,7},{6,4},{7,5},{8,10},{9,11},{10,... | collective-permute-start | bytes 294920 | tf_op jit(solution)/shard_map/gather_window/ppermute | solution.py:356
  83.9 3.6 %collective-permute-start.10 = (bf16[3,64,256]{2,1,0:T(8,128)(2,1)S(1)}, bf16[3,64,256]{2,1,0:T(8,128)(2,1)S(1)}, u32[]{:S(2)}, u32[]{:S(2)}) collective-permute-start(bf16[3,64,256]{2,1,0:T(8,128)(2,1)S(1)} %get-tuple-element.26), channel_id=1, source_target_pairs={{0,3},{1,0},{2,1},{3,2},{4,7},{5,4},{6,5},{7,6},{8,11},{9,8},{10,9... | collective-permute-start | bytes 294920 | tf_op jit(solution)/shard_map/gather_window/ppermute | solution.py:356
  94.5 4.5 %collective-permute-start.12 = (bf16[64,256]{1,0:T(8,128)(2,1)S(1)}, bf16[64,256]{1,0:T(8,128)(2,1)S(1)}, u32[]{:S(2)}, u32[]{:S(2)}) collective-permute-start(bf16[64,256]{1,0:T(8,128)(2,1)S(1)} %get-tuple-element.29), channel_id=1, source_target_pairs={{0,1},{1,2},{2,3},{3,0},{4,5},{5,6},{6,7},{7,4},{8,9},{9,10},{10,1... | collective-permute-start | bytes 98312 | tf_op jit(solution)/shard_map/turn_back/ppermute | solution.py:370
  94.8 4.9 %collective-permute-start.13 = (bf16[64,256]{1,0:T(8,128)(2,1)S(1)}, bf16[64,256]{1,0:T(8,128)(2,1)S(1)}, u32[]{:S(2)}, u32[]{:S(2)}) collective-permute-start(bf16[64,256]{1,0:T(8,128)(2,1)S(1)} %get-tuple-element.30), channel_id=1, source_target_pairs={{0,2},{1,3},{2,0},{3,1},{4,6},{5,7},{6,4},{7,5},{8,10},{9,11},{10,... | collective-permute-start | bytes 98312 | tf_op jit(solution)/shard_map/turn_back/ppermute | solution.py:370
  97.3 2.8 %collective-permute-start.14 = (bf16[64,256]{1,0:T(8,128)(2,1)S(1)}, bf16[64,256]{1,0:T(8,128)(2,1)S(1)}, u32[]{:S(2)}, u32[]{:S(2)}) collective-permute-start(bf16[64,256]{1,0:T(8,128)(2,1)S(1)} %get-tuple-element.31), channel_id=1, source_target_pairs={{0,3},{1,0},{2,1},{3,2},{4,7},{5,4},{6,5},{7,6},{8,11},{9,8},{10,9... | collective-permute-start | bytes 98312 | tf_op jit(solution)/shard_map/turn_back/ppermute | solution.py:370
  (1 other events, 0.9 us)
Sparse Core Ops, SparseCore 0:
  10.6 44.4 all-gather.2

commit v3 on v1

v3 whole, which is shorter than its diff:
```python
import functools

import jax
import jax.numpy as jnp
from jax import lax
from jax.experimental import pallas as pl
from jax.experimental.pallas import tpu as pltpu
from jax.sharding import PartitionSpec as P

HD = 16
KER = 27
HW = 256
CHAN = 4
SLOTS = 32
TURN = SLOTS // CHAN
INFO = 16
TENS = 4
ONES = 5
F32 = jnp.float32
BF16 = jnp.bfloat16
I32 = jnp.int32

NN = (((1,), (0,)), ((), ()))
NT = (((1,), (1,)), ((), ()))
TN = (((0,), (0,)), ((), ()))


def dot(a, b, dims=NN):
    return lax.dot_general(a, b, dims, preferred_element_type=F32)


def iota(shape, axis):
    return lax.broadcasted_iota(I32, shape, axis)


def hot(mask):
    return mask.astype(F32).astype(BF16)


def kernel_call(body, outs, cost, operands, scratch=(), vmem=48, managed=False):
    place = None if managed else pltpu.VMEM
    specs = [pl.BlockSpec(memory_space=pltpu.SMEM if x.shape == (1,) else place) for x in operands]
    call = pl.pallas_call(
        body,
        out_shape=outs,
        in_specs=specs,
        scratch_shapes=list(scratch),
        compiler_params=pltpu.CompilerParams(vmem_limit_bytes=vmem * 1024 * 1024),
        cost_estimate=pl.CostEstimate(flops=cost, bytes_accessed=1 << 20, transcendentals=0),
    )
    return call(*operands)


def column_norm(x):
    mean = jnp.mean(x, axis=0, keepdims=True)
    centred = x - mean
    var = jnp.mean(centred * centred, axis=0, keepdims=True)
    return (centred * lax.rsqrt(var + 1e-05)).astype(BF16)


def sender(me, k):
    return lax.rem(me + CHAN - k, CHAN)


def code_body(owners, me_ref, rank_ref, out_ref):
    rank = rank_ref[...]
    rows = rank.shape[1]
    owner = rank // rows
    local = rank % rows
    onehot = (iota((owners, rows), 0) == owner).astype(F32)
    up_to = hot(iota((rows, rows), 0) <= iota((rows, rows), 1))
    count = dot(onehot.astype(BF16), up_to)
    below = hot(iota((owners, owners), 1) < iota((owners, owners), 0))
    start = dot(below, count[:, rows - 128 :].astype(BF16))[:, 127:128]
    begin = jnp.sum(onehot * start, axis=0, keepdims=True).astype(I32)
    place = jnp.sum(onehot * (start + count - 1.0), axis=0, keepdims=True).astype(I32)
    turn = place % CHAN
    row = place // CHAN
    slot = row - (begin - turn + CHAN - 1) // CHAN
    back = (turn // 2) * rows + owner * (2 * TURN) + (turn % 2) * TURN + slot
    mine = jnp.where(turn == me_ref[0], row, -1)
    lines = (back, mine, owner, slot, local // 32 + 1, local % 32)
    out_ref[...] = jnp.concatenate(lines + (back, back), axis=0)


def merge_body(x_ref, qkv_ref, out_w_ref, out_ref):
    quarter, rows = x_ref.shape
    whole = qkv_ref.shape[1]
    out_ref[0:quarter, :] = x_ref[...]
    for part in range(3):
        cut = slice(part * quarter, (part + 1) * quarter)
        out_ref[quarter:, part * whole : (part + 1) * whole] = qkv_ref[cut, :]
    out_ref[quarter:, 3 * whole :] = out_w_ref[...]


def attention_body(me_ref, range_ref, *refs):
    blocks = refs[0:4]
    codes_ref, send_ref, xs, ws, heads = refs[4:9]
    me = me_ref[0]
    quarter = blocks[0].shape[0] // 2
    for k in range(CHAN):
        owner = sender(me, k)
        xs[pl.ds(pl.multiple_of(owner * quarter, quarter), quarter), :] = blocks[k][0:quarter, :]
        ws[owner] = blocks[k][quarter:, :]

    codes = codes_ref[...]
    width, rows = xs.shape

    def weight(part):
        cut = slice(part * width, (part + 1) * width)
        return jnp.concatenate([ws[i, :, cut] for i in range(CHAN)], axis=0)

    mine = rows // CHAN
    x = xs[...]
    norm = column_norm(x.astype(F32))
    pick = hot(iota((mine, rows), 0) == codes[1:2])
    own = dot(x, pick, NT)
    own_norm = dot(norm, pick, NT).astype(BF16)
    digits = dot(codes.astype(F32).astype(BF16), pick, NT)
    q = (dot(weight(0), own_norm).astype(BF16) * BF16(0.25)).astype(BF16)
    keys = dot(weight(1), norm).astype(BF16)
    vals = dot(weight(2), norm).astype(BF16)
    ones = hot(iota((HD, rows), 0) == 0)
    for lo in range(0, width, HD):
        at = slice(lo, lo + HD)
        scores = dot(q[at], keys[at], TN)
        top = jnp.max(scores, axis=1, keepdims=True)
        expo = jnp.exp(scores - top).astype(BF16)
        res = dot(jnp.concatenate([vals[at], ones], axis=0), expo, NT)
        heads[at, :] = (res[0:HD] / res[HD : HD + 1]).astype(BF16)
    first = (own + dot(weight(3), heads[...])).astype(BF16)

    target = digits[2:3] * TURN + digits[3:4]
    low_digits = digits.astype(BF16)
    shift = lax.rem(range_ref[0], 128 // TURN) * TURN
    lane = iota((8, 128), 1)
    keep = (lane >= shift) & (lane < shift + TURN)
    block = 256
    owners = block // TURN
    for start in range(0, send_ref.shape[0] * TURN, block):
        match = hot((iota((block, mine), 0) + start).astype(F32) == target)
        res = dot(match, first, NT).reshape(owners, TURN, width)
        info = dot(low_digits, match, NT)
        tiles = []
        for i in range(owners):
            turned = pltpu.roll(info, lax.rem(shift + block - i * TURN, block), 1)
            tiles.append(jnp.where(keep, turned[:, 0:128], 0.0)[None])
        tiles = jnp.concatenate(tiles, axis=0)
        res = jnp.concatenate([res[:, :, 0:128], res[:, :, 128:], tiles], axis=1)
        owner = start // TURN
        send_ref[owner : owner + owners] = res.astype(BF16)


def compact_body(got_ref, out_ref):
    owners = got_ref.shape[0]
    slots = owners * TURN
    got = got_ref[...].astype(F32)
    info = got[:, 2 * TURN :, :].reshape(slots // 128, 128 // TURN, 8, 128)
    info = jnp.sum(info, axis=1)
    info = jnp.concatenate([info[g] for g in range(slots // 128)], axis=1)
    valid = info[TENS : TENS + 1] > 0.0
    before = hot(iota((slots, slots), 0) < iota((slots, slots), 1))
    line = jnp.broadcast_to(valid.astype(F32), (8, slots)).astype(BF16)
    position = jnp.where(valid, dot(line, before)[0:1], -1.0)
    match = hot(iota((slots, slots), 0).astype(F32) == position)
    rows = [got[:, i * TURN : (i + 1) * TURN, :].reshape(slots, 128) for i in range(2)]
    rows = jnp.concatenate(rows, axis=1).astype(BF16)
    limit = out_ref.shape[0] - INFO
    found = dot(match[0:limit], rows)
    packed = dot(info.astype(BF16), match, NT)
    lines = []
    for table in (packed, info):
        for digit in (TENS, ONES):
            lines += [table[digit : digit + 1, 0:256], table[digit : digit + 1, 256:]]
    lines.append(jnp.zeros((INFO - len(lines), 256), F32))
    out_ref[...] = jnp.concatenate([found] + lines, axis=0).astype(BF16)


def turned_lanes(x, core):
    half = x.shape[1] // 2
    return jnp.where(core == 1, jnp.concatenate([x[:, half:], x[:, :half]], axis=1), x)


def window_body(me_ref, core_ref, c0, c1, c2, c3, win_ref, third_ref, place_ref, stack):
    me = me_ref[0]
    for k, ref in enumerate((c0, c1, c2, c3)):
        stack[sender(me, k)] = ref[...]
    limit = stack.shape[1] - INFO
    line = iota((256, limit), 0)
    side = jnp.where(me == 0, 1, me - 1)
    other = jnp.where(me == 0, 3, jnp.where(me == 3, 0, me + 1))
    ranks = jnp.concatenate([line + me * 256, line + side * 256, line + other * 256], axis=0)
    ranks = ranks.astype(F32)
    total = 0.0
    places = []
    for i in range(CHAN):
        info = stack[i, limit:, :].astype(F32)

        def value(at):
            tens = jnp.concatenate([info[at : at + 1], info[at + 1 : at + 2]], axis=1)
            ones = jnp.concatenate([info[at + 2 : at + 3], info[at + 3 : at + 4]], axis=1)
            return tens * 32.0 + ones - 32.0

        places.append(value(4))
        total += dot(hot(ranks == value(0)[:, 0:limit]), stack[i, 0:limit, :])
    places.append(jnp.zeros_like(places[0]))
    place_ref[...] = jnp.concatenate(places + places[4:] * 3, axis=0)
    total = total.astype(BF16)
    win_ref[...] = turned_lanes(total[0:512], core_ref[0])
    third_ref[...] = total[512:]


def pack_body(core_ref, conv_ref, up_ref, down_ref, near_ref, far_ref):
    for mine, dst in ((core_ref[0], near_ref), (1 - core_ref[0], far_ref)):
        half = pl.ds(pl.multiple_of(mine * 128, 128), 128)
        at = conv_ref.shape[0]
        dst[0:at, :] = conv_ref[:, half]
        for ref in (up_ref, down_ref):
            size = ref.shape[1]
            dst[at : at + size, :] = ref[half, :].astype(F32).T.astype(BF16)
            at += size


def weight_reader(near_w, far_w, quarter):
    split = near_w[2].shape[0]

    def weight(k, section, at, size):
        if k == 2:
            piece = 2 if section < split else 3
            section = section % split
        else:
            piece = (0, 1, None, 4)[k]
        rows = pl.ds(pl.multiple_of(section + at, quarter), size)
        return jnp.concatenate([near_w[piece][rows, :], far_w[piece][rows, :]], axis=1)

    return weight


def rows_at(me, core, k, quarter):
    owner = lax.rem(me + CHAN - k + 2 * core, CHAN)
    return pl.ds(pl.multiple_of(owner * quarter, quarter), quarter)


def add_conv(total, near_ref, cols, rows, weight, quarter):
    near = near_ref[...]
    target = jnp.where(near < 0, -1, near + iota(near.shape, 1))
    target = jnp.concatenate([target.astype(F32), jnp.zeros((5, near.shape[1]), F32)], axis=0).T
    cols = cols.astype(F32)
    group = 3

    def kernel(j):
        return jnp.concatenate([weight(k, j * quarter, 0, quarter) for k in range(CHAN)], axis=0)

    for start in range(0, KER, group):
        js = range(start, start + group)
        match = jnp.concatenate([hot(cols == target[:, j : j + 1]) for j in js], axis=0)
        picked = dot(match, rows).astype(BF16)
        picked = jnp.concatenate([picked[i * 256 : (i + 1) * 256] for i in range(group)], axis=1)
        total += dot(jnp.concatenate([kernel(j) for j in js], axis=1), picked, NT)
    return total


def conv_first_body(me_ref, core_ref, win_ref, near_ref, *refs):
    near_w, far_w, out_ref, turned = refs[0:5], refs[5:10], refs[10], refs[11]
    me, core = me_ref[0], core_ref[0]
    quarter = 64
    turned[...] = win_ref[0:256, :].astype(F32).T
    own = [turned[rows_at(me, core, k, quarter), :] for k in range(CHAN)]
    lane = iota((256, 512), 1)
    cols = jnp.where(lane < 256, lane + 256, jnp.where(me == 0, lane + 256, lane - 256))
    weight = weight_reader(near_w, far_w, quarter)
    out_ref[...] = add_conv(
        jnp.concatenate(own, axis=0), near_ref, cols, win_ref[...], weight, quarter
    )


def conv_second_body(me_ref, core_ref, acc_ref, halo_ref, third_ref, near_ref, *refs):
    near_w, far_w, outs, norm_ref = refs[0:5], refs[5:10], refs[10:14], refs[14]
    me, core = me_ref[0], core_ref[0]
    quarter = 64
    whole = CHAN * quarter
    half = whole // 2
    weight = weight_reader(near_w, far_w, quarter)
    edge = (me == 0) | (me == CHAN - 1)
    rows = turned_lanes(jnp.where(edge, halo_ref[...], third_ref[...]), core)
    cols = iota((256, 256), 1) + jnp.where(me == 0, 0, 512)
    second = add_conv(acc_ref[...], near_ref, cols, rows, weight, quarter).astype(BF16)
    norm = column_norm(second.astype(F32))
    for k in range(CHAN):
        norm_ref[rows_at(me, core, k, quarter), :] = norm[k * quarter : (k + 1) * quarter]
    total = second.astype(F32)
    lo, hi = half * core, half * (1 - core)
    up_at = KER * quarter
    down_at = up_at + whole
    for k in range(CHAN):
        up = [weight(k, up_at, x, half) for x in (lo, hi)]
        hidden = dot(jnp.concatenate(up, axis=0), norm_ref[...])
        hidden = (0.5 * hidden * (1.0 + lax.erf(hidden * (2.0 ** -0.5)))).astype(BF16)
        down = [weight(k, down_at, sender(me, p) * quarter, quarter) for p in range(CHAN)]
        total += dot(jnp.concatenate(down, axis=0), hidden)
    third = total.astype(BF16)
    for k in range(CHAN):
        p = (CHAN - k) % CHAN
        outs[k][...] = third[p * quarter : (p + 1) * quarter]


def back_body(me_ref, t0, t1, t2, t3, place_ref, out_ref, tmp):
    me = me_ref[0]
    for k, ref in enumerate((t0, t1, t2, t3)):
        tmp[sender(me, k)] = ref[...]
    third = jnp.concatenate([tmp[q] for q in range(CHAN)], axis=1)
    zero = jnp.zeros_like(third)
    low = jnp.concatenate([third, zero], axis=0)
    high = jnp.concatenate([zero, third], axis=0)
    column = place_ref[...].T
    slots = column.shape[0]
    block = 256
    rank = iota((block, third.shape[1]), 1).astype(F32)
    for start in range(0, slots, block):
        res = []
        for odd in range(2):
            part = 0.0
            for half, rhs in enumerate((low, high)):
                i = 2 * half + odd
                part += dot(hot(rank == column[start : start + block, i : i + 1]), rhs, NT)
            res.append(part.reshape(block // TURN, TURN, 128))
        owner = start // TURN
        out_ref[owner : owner + block // TURN] = jnp.concatenate(res, axis=1).astype(BF16)


def restore_body(got_ref, codes_ref, out_ref):
    width, rows = out_ref.shape
    got = got_ref[...].reshape(-1, 2 * width).astype(F32).T.astype(BF16)
    code = codes_ref[0:1, :]
    res = 0.0
    for half in range(2):
        for start in range(0, got.shape[1], 256):
            match = hot(iota((256, rows), 0) + (start + half * rows) == code)
            res += dot(got[half * width : (half + 1) * width, start : start + 256], match)
    out_ref[...] = res.astype(BF16)


def turn(k):
    return [(i, (i + k) % CHAN) for i in range(CHAN)]


def gather_chan(x):
    return [x] + [lax.ppermute(x, "chan", turn(k)) for k in range(1, CHAN)]


def exchange(parts):
    return lax.all_to_all(parts, "range", split_axis=0, concat_axis=0, tiled=True)


def shards(
    features, hilbert_rank, neighbours, qkv_weight, out_weight, conv_weight, up_weight, down_weight
):
    quarter, rows = features.shape
    whole = CHAN * quarter
    owners = lax.axis_size("range")
    me = lax.axis_index("chan").astype(I32)
    position = lax.axis_index("range").astype(I32)
    core = lax.rem(position, 2)
    me_ref, core_ref, range_ref = me[None], core[None], position[None]
    swap = [(i, i ^ 1) for i in range(owners)]
    sds = jax.ShapeDtypeStruct
    vmem = pltpu.VMEM

    with jax.named_scope("gather_features"):
        qkv = jnp.transpose(qkv_weight, (0, 2, 1)).reshape(3 * quarter, whole)
        merged = kernel_call(
            merge_body,
            sds((2 * quarter, rows), BF16),
            1 << 20,
            [features, qkv, out_weight.T],
            managed=True,
        )
        blocks = gather_chan(merged)
    with jax.named_scope("codes"):
        codes = kernel_call(
            functools.partial(code_body, owners),
            sds((8, rows), I32),
            1 << 20,
            [me_ref, hilbert_rank[None, :]],
            managed=True,
        )
    with jax.named_scope("gather_weights"):
        size = KER * quarter + 2 * up_weight.shape[1]
        split = (size // quarter + 1) // 2 * quarter
        near0, far0 = kernel_call(
            pack_body,
            (sds((size, 128), BF16), sds((size, 128), BF16)),
            1 << 20,
            [core_ref, conv_weight.reshape(KER * quarter, whole), up_weight, down_weight],
            managed=True,
        )
        blocks, codes, near0, far0 = lax.optimization_barrier((blocks, codes, near0, far0))
        near1 = lax.ppermute(near0, "chan", turn(1))
        near3 = lax.ppermute(near0, "chan", turn(3))
    with jax.named_scope("attention"):
        send = kernel_call(
            attention_body,
            sds((owners, 3 * TURN, 128), BF16),
            1 << 32,
            [me_ref, range_ref] + blocks + [codes],
            [
                vmem((whole, rows), BF16),
                vmem((CHAN, quarter, rows), BF16),
                vmem((whole, rows // CHAN), BF16),
            ],
        )
    with jax.named_scope("exchange"):
        send, near1, near3 = lax.optimization_barrier((send, near1, near3))
        near2 = (
            lax.ppermute(near1[:split], "chan", turn(1)),
            lax.ppermute(near3[split:], "chan", turn(3)),
        )
        got = exchange(send)
        got, near2 = lax.optimization_barrier((got, near2))
        near_w = [near0, near1, near2[0], near2[1], near3]
        far_w = [far0] + [lax.ppermute(w, "range", swap) for w in near_w[1:]]
    with jax.named_scope("compact"):
        limit = (rows + (CHAN - 1) * owners) // CHAN
        limit = (limit + 15) // 16 * 16
        found = kernel_call(compact_body, sds((limit + INFO, whole), BF16), 1 << 28, [got])
        found = gather_chan(found)
        found, far_w = lax.optimization_barrier((found, far_w))
    with jax.named_scope("window"):
        win, third, place = kernel_call(
            window_body,
            (sds((512, whole), BF16), sds((256, whole), BF16), sds((8, owners * TURN), F32)),
            1 << 28,
            [me_ref, core_ref] + found,
            [vmem((CHAN, limit + INFO, whole), BF16)],
        )
        pairs = [(i * CHAN, (i + 1) * CHAN) for i in range(owners - 1)]
        pairs += [((i + 1) * CHAN + CHAN - 1, i * CHAN + CHAN - 1) for i in range(owners - 1)]
        halo = lax.ppermute(third, ("range", "chan"), pairs)
    with jax.named_scope("conv"):
        near_ranks = lax.dynamic_slice_in_dim(neighbours, me * 256, 256, 1)
        acc = kernel_call(
            conv_first_body,
            sds((whole, 256), F32),
            1 << 32,
            [me_ref, core_ref, win, near_ranks] + near_w + far_w,
            [vmem((whole, 256), F32)],
        )
        edge = sds((quarter, 256), BF16)
        thirds = kernel_call(
            conv_second_body,
            (edge, edge, edge, edge),
            1 << 32,
            [me_ref, core_ref, acc, halo, third, near_ranks] + near_w + far_w,
            [vmem((whole, 256), BF16)],
        )
    with jax.named_scope("turn_back"):
        thirds = [thirds[0]] + [lax.ppermute(thirds[k], "chan", turn(k)) for k in range(1, CHAN)]
    with jax.named_scope("back"):
        back = kernel_call(
            back_body,
            sds((owners, 2 * TURN, 128), BF16),
            1 << 30,
            [me_ref] + thirds + [place],
            [vmem((CHAN, quarter, 256), BF16)],
        )
        returned = exchange(back)
    with jax.named_scope("restore"):
        return kernel_call(restore_body, sds((quarter, rows), BF16), 1 << 30, [returned, codes])


def solution(mesh):
    in_specs = (
        P("chan", "range"),
        P("range"),
        P(None, "range"),
        P(None, None, "chan"),
        P(None, "chan"),
        P(None, "chan", None),
        P(None, "chan"),
        P("chan", None),
    )
    out_specs = P("chan", "range")
    return jax.shard_map(shards, mesh=mesh, in_specs=in_specs, out_specs=out_specs, check_vma=False)
```

time: 221 us -> 120 us (0.54)
  blocking collectives: 102 us -> 20.4 us
  between operations: 13.6 us -> 0.15 us
  waiting for transfers between devices: 21.7 us -> 28.7 us
  Pallas kernels: 32.4 us -> 26.1 us
  local copies, waits for them, and re-layouts: 7.98 us -> 5.22 us
  other arithmetic: 2.39 us -> 0 us
    all_gather x3 -> x0, blocking collectives: 78.8 us -> none  [the longest x1 51.2 us: shards(): tables = lax.all_gather(table, 'range', axis=0)]
    pallas_call x6 -> x10, Pallas kernels: 32.4 us -> 26.1 us  [kernel_call(): return call(*operands)]
    all_to_all x1, waiting for transfers between devices: 0.01 us -> 4.37 us  [exchange(): lax.all_to_all(parts, 'range', split_axis=0, concat_axis=0, tiled=True)]
    ppermute x7 -> x9, waiting for transfers between devices: 3.8 us -> 7.66 us  [the longest x1 5.78 us: shards(): lax.ppermute(near3[split:], 'chan', turn(3))]
    reshape x2 -> x0, local copies, waits for them, and re-layouts: 2.65 us -> none  [the longest x1 2.55 us: shards(): tables.reshape(owners, 2, owners, HALF)]
    all_to_all x1, blocking collectives: 22.9 us -> 20.4 us  [exchange(): lax.all_to_all(parts, 'range', split_axis=0, concat_axis=0, tiled=True)]
    ppermute x7 -> x9, starting transfers between devices: 12.5 us -> 11 us  [the longest x1 4.33 us: shards(): halo = lax.ppermute(third, ('range', 'chan'), pairs)]
    unnamed x16 -> x20, local copies, waits for them, and re-layouts: 3.82 us -> 5.18 us
  transfers between devices with their start and end apart: 18 -> 19, of which waited for: 10 -> 9; matrix products, arithmetic and copies ran while one was open for 3% -> 0% of each run, Pallas kernels for 6% -> 14%
where the time goes in v3:
time: 120 us
  starting transfers between devices  38.8 us (32%)
  waiting for transfers between devices  28.7 us (24%)
  Pallas kernels  26.1 us (22%)
  blocking collectives  20.4 us (17%)
  local copies, waits for them, and re-layouts  5.22 us (4%)
    pallas_call x10, Pallas kernels, kernel_call(): return call(*operands)  26.1 us
    all_to_all x1, blocking collectives, exchange(): lax.all_to_all(parts, 'range', split_axis=0, concat_axis=0, tiled=True)  20.4 us
    all_to_all x1, starting transfers between devices, exchange(): lax.all_to_all(parts, 'range', split_axis=0, concat_axis=0, tiled=True)  14.7 us
    ppermute x6, waiting for transfers between devices, gather_chan(): return [x] + [lax.ppermute(x, 'chan', turn(k)) for k in range(1, CHAN)]  14 us
    ppermute x6, starting transfers between devices, gather_chan(): return [x] + [lax.ppermute(x, 'chan', turn(k)) for k in range(1, CHAN)]  10.4 us
    ppermute x1, waiting for transfers between devices, shards(): lax.ppermute(near3[split:], 'chan', turn(3))  5.78 us
    unnamed x20, local copies, waits for them, and re-layouts  5.18 us
    all_to_all x1, waiting for transfers between devices, exchange(): lax.all_to_all(parts, 'range', split_axis=0, concat_axis=0, tiled=True)  4.37 us
  transfers between devices with their start and end apart: 19, of which 9 were waited for; matrix products, arithmetic and copies ran while one was open for 0% of the time, Pallas kernels for 14%

profile of v3, /device:TPU:1, one launch (start us, length us, event | category | flops | bytes accessed | tf_op | source)
XLA Modules:
  0.0 119.5 jit_solution(13147800303128606347)
XLA Ops:
  2.6 2.1 %collective-permute-start = (bf16[128,1024]{1,0:T(8,128)(2,1)S(1)}, bf16[128,1024]{1,0:T(8,128)(2,1)S(1)}, u32[]{:S(2)}, u32[]{:S(2)}) collective-permute-start(bf16[128,1024]{1,0:T(8,128)(2,1)S(1)} %gather_features.1.refs_0_), channel_id=1, source_target_pairs={{0,1},{1,2},{2,3},{3,0},{4,5},{5,6},{6,7},{7,4},{8,9},{9,10},{10,1... | collective-permute-start | bytes 786440 | tf_op jit(solution)/shard_map/gather_features/ppermute | solution.py:348
  4.7 2.5 %collective-permute-start.1 = (bf16[128,1024]{1,0:T(8,128)(2,1)S(1)}, bf16[128,1024]{1,0:T(8,128)(2,1)S(1)}, u32[]{:S(2)}, u32[]{:S(2)}) collective-permute-start(bf16[128,1024]{1,0:T(8,128)(2,1)S(1)} %gather_features.1.refs_0_), channel_id=1, source_target_pairs={{0,2},{1,3},{2,0},{3,1},{4,6},{5,7},{6,4},{7,5},{8,10},{9,11},{10,... | collective-permute-start | bytes 786440 | tf_op jit(solution)/shard_map/gather_features/ppermute | solution.py:348
  9.8 1.2 copy-done.1
  11.2 7.3 %collective-permute-done.1.refs_2_ = bf16[128,1024]{1,0:T(8,128)(2,1)S(1)} collective-permute-done((bf16[128,1024]{1,0:T(8,128)(2,1)S(1)}, bf16[128,1024]{1,0:T(8,128)(2,1)S(1)}, u32[]{:S(2)}, u32[]{:S(2)}) %collective-permute-start.1) | collective-permute-done | bytes 262176 | tf_op jit(solution)/shard_map/gather_features/ppermute | solution.py:348
  18.5 1.2 collective-permute-start.3
  19.7 1.5 %collective-permute-start.4 = (bf16[2240,128]{1,0:T(8,128)(2,1)S(1)}, bf16[2240,128]{1,0:T(8,128)(2,1)S(1)}, u32[]{:S(2)}, u32[]{:S(2)}) collective-permute-start(bf16[2240,128]{1,0:T(8,128)(2,1)S(1)} %get-tuple-element.43.refs_0_), channel_id=1, source_target_pairs={{0,3},{1,0},{2,1},{3,2},{4,7},{5,4},{6,5},{7,6},{8,11},{9,8},{10,9... | collective-permute-start | bytes 1720328 | tf_op jit(solution)/shard_map/gather_weights/ppermute | solution.py:399
  21.2 9.8 %attention.1 = bf16[64,24,128]{2,1,0:T(8,128)(2,1)} custom-call(s32[1]{0:T(128)} %bitcast.me_ref, s32[1]{0:T(128)} %bitcast.2.range_ref, bf16[128,1024]{1,0:T(8,128)(2,1)S(1)} %gather_features.1.refs_0_, bf16[128,1024]{1,0:T(8,128)(2,1)S(1)} %collective-permute-done.refs_1_, bf16[128,1024]{1,0:T(8,128)(2,1)S(1)} %collective-permute-done.1.refs_2_, ...), custom_call_target="tpu_custom_call" | custom-call | flops 4294967296 | bytes 1048576 | tf_op jit(solution)/shard_map/attention/pallas_call | solution.py:51
  31.0 1.7 %collective-permute-done.3.refs_1_ = bf16[2240,128]{1,0:T(8,128)(2,1)S(1)} collective-permute-done((bf16[2240,128]{1,0:T(8,128)(2,1)S(1)}, bf16[2240,128]{1,0:T(8,128)(2,1)S(1)}, u32[]{:S(2)}, u32[]{:S(2)}) %collective-permute-start.3) | collective-permute-done | bytes 573472 | tf_op jit(solution)/shard_map/gather_weights/ppermute | solution.py:398
  32.7 14.7 %all-to-all-start = ((bf16[64,24,128]{2,1,0:T(8,128)(2,1)}), bf16[64,24,128]{2,1,0:T(8,128)(2,1)S(1)}, u32[]{:S(2)}, u32[]{:S(2)}) async-start(bf16[64,24,128]{2,1,0:T(8,128)(2,1)} %attention.1), calls=%async_computation | async-start | bytes 786432 | tf_op jit(solution)/shard_map/exchange/all_to_all | solution.py:352
  49.0 1.9 %collective-permute-start.6 = (bf16[1088,128]{1,0:T(8,128)(2,1)S(1)}, bf16[1088,128]{1,0:T(8,128)(2,1)S(1)}, u32[]{:S(2)}, u32[]{:S(2)}) collective-permute-start(bf16[1088,128]{1,0:T(8,128)(2,1)S(1)} %slice.7), channel_id=1, source_target_pairs={{0,3},{1,0},{2,1},{3,2},{4,7},{5,4},{6,5},{7,6},{8,11},{9,8},{10,9... | collective-permute-start | bytes 835592 | tf_op jit(solution)/shard_map/exchange/ppermute | solution.py:416
  50.9 5.8 %collective-permute-done.6.refs_3_ = bf16[1088,128]{1,0:T(8,128)(2,1)S(1)} collective-permute-done((bf16[1088,128]{1,0:T(8,128)(2,1)S(1)}, bf16[1088,128]{1,0:T(8,128)(2,1)S(1)}, u32[]{:S(2)}, u32[]{:S(2)}) %collective-permute-start.6) | collective-permute-done | bytes 278560 | tf_op jit(solution)/shard_map/exchange/ppermute | solution.py:416
  57.6 4.4 %all-to-all-done.got_ref = bf16[64,24,128]{2,1,0:T(8,128)(2,1)S(1)} async-done(((bf16[64,24,128]{2,1,0:T(8,128)(2,1)}), bf16[64,24,128]{2,1,0:T(8,128)(2,1)S(1)}, u32[]{:S(2)}, u32[]{:S(2)}) %all-to-all-start) | async-done | bytes 393248 | tf_op jit(solution)/shard_map/exchange/all_to_all | solution.py:352
  64.4 3.0 %collective-permute-start.8 = (bf16[320,256]{1,0:T(8,128)(2,1)}, bf16[320,256]{1,0:T(8,128)(2,1)S(1)}, u32[]{:S(2)}, u32[]{:S(2)}) collective-permute-start(bf16[320,256]{1,0:T(8,128)(2,1)} %compact.1.c0), channel_id=1, source_target_pairs={{0,2},{1,3},{2,0},{3,1},{4,6},{5,7},{6,4},{7,5},{8,10},{9,11},{10,... | collective-permute-start | bytes 491528 | tf_op jit(solution)/shard_map/compact/ppermute | solution.py:348
  68.3 2.1 %collective-permute-done.7.c1 = bf16[320,256]{1,0:T(8,128)(2,1)S(1)} collective-permute-done((bf16[320,256]{1,0:T(8,128)(2,1)}, bf16[320,256]{1,0:T(8,128)(2,1)S(1)}, u32[]{:S(2)}, u32[]{:S(2)}) %collective-permute-start.7) | collective-permute-done | bytes 163872 | tf_op jit(solution)/shard_map/compact/ppermute | solution.py:348
  70.4 4.7 %collective-permute-done.8.c2 = bf16[320,256]{1,0:T(8,128)(2,1)S(1)} collective-permute-done((bf16[320,256]{1,0:T(8,128)(2,1)}, bf16[320,256]{1,0:T(8,128)(2,1)S(1)}, u32[]{:S(2)}, u32[]{:S(2)}) %collective-permute-start.8) | collective-permute-done | bytes 163872 | tf_op jit(solution)/shard_map/compact/ppermute | solution.py:348
  75.1 1.9 %window.1 = (bf16[512,256]{1,0:T(8,128)(2,1)S(1)}, bf16[256,256]{1,0:T(8,128)(2,1)S(1)}, f32[8,512]{1,0:T(8,128)S(1)}) custom-call(s32[1]{0:T(128)} %bitcast.me_ref, s32[1]{0:T(128)} %bitcast.1.core_ref, bf16[320,256]{1,0:T(8,128)(2,1)} %compact.1.c0, bf16[320,256]{1,0:T(8,128)(2,1)S(1)} %collective-permute-done.7.c1, ...), custom_call_target="tpu_custom_call" | custom-call | flops 268435456 | bytes 1048576 | tf_op jit(solution)/shard_map/window/pallas_call | solution.py:51
  77.0 4.3 %collective-permute-start.14 = (bf16[256,256]{1,0:T(8,128)(2,1)S(1)}, bf16[256,256]{1,0:T(8,128)(2,1)S(1)}, u32[]{:S(2)}, u32[]{:S(2)}) collective-permute-start(bf16[256,256]{1,0:T(8,128)(2,1)S(1)} %get-tuple-element.61.third_ref), channel_id=1, source_target_pairs={{0,4},{4,8},{8,12},{12,16},{16,20},{20,24},{24,28},{28,32},{32,36}... | collective-permute-start | bytes 393224 | tf_op jit(solution)/shard_map/window/ppermute | solution.py:438
  81.4 4.6 %conv.2.acc_ref = f32[256,256]{1,0:T(8,128)S(1)} custom-call(s32[1]{0:T(128)} %bitcast.me_ref, s32[1]{0:T(128)} %bitcast.1.core_ref, bf16[512,256]{1,0:T(8,128)(2,1)S(1)} %get-tuple-element.55.win_ref, s32[27,256]{1,0:T(8,128)S(1)} %constant_dynamic-slice_fusion.near_ref, bf16[2240,128]{1,0:T(8,128)(2,1)S(1)} %get-tuple-element.43.refs_0_, ...), custom_call_target="tpu_custom_call" | custom-call | flops 4294967296 | bytes 1048576 | tf_op jit(solution)/shard_map/conv/pallas_call | solution.py:51
  86.0 4.4 %conv.3 = (bf16[64,256]{1,0:T(8,128)(2,1)S(1)}, bf16[64,256]{1,0:T(8,128)(2,1)S(1)}, bf16[64,256]{1,0:T(8,128)(2,1)S(1)}, bf16[64,256]{1,0:T(8,128)(2,1)S(1)}) custom-call(s32[1]{0:T(128)} %bitcast.me_ref, s32[1]{0:T(128)} %bitcast.1.core_ref, f32[256,256]{1,0:T(8,128)S(1)} %conv.2.acc_ref, bf16[256,256]{1,0:T(8,128)(2,1)S(1)} %collective-permute-done.14.halo_ref, ...), custom_call_target="tpu_custom_call" | custom-call | flops 4294967296 | bytes 1048576 | tf_op jit(solution)/shard_map/conv/pallas_call | solution.py:51
  90.5 2.0 %collective-permute-start.16 = (bf16[64,256]{1,0:T(8,128)(2,1)S(1)}, bf16[64,256]{1,0:T(8,128)(2,1)S(1)}, u32[]{:S(2)}, u32[]{:S(2)}) collective-permute-start(bf16[64,256]{1,0:T(8,128)(2,1)S(1)} %get-tuple-element.64), channel_id=1, source_target_pairs={{0,2},{1,3},{2,0},{3,1},{4,6},{5,7},{6,4},{7,5},{8,10},{9,11},{10,... | collective-permute-start | bytes 98312 | tf_op jit(solution)/shard_map/turn_back/ppermute | solution.py:457
  93.2 1.9 %collective-permute-done.15.t1 = bf16[64,256]{1,0:T(8,128)(2,1)S(1)} collective-permute-done((bf16[64,256]{1,0:T(8,128)(2,1)S(1)}, bf16[64,256]{1,0:T(8,128)(2,1)S(1)}, u32[]{:S(2)}, u32[]{:S(2)}) %collective-permute-start.15) | collective-permute-done | bytes 32800 | tf_op jit(solution)/shard_map/turn_back/ppermute | solution.py:457
  95.8 1.6 %back.1 = bf16[64,16,128]{2,1,0:T(8,128)(2,1)S(1)} custom-call(s32[1]{0:T(128)} %bitcast.me_ref, bf16[64,256]{1,0:T(8,128)(2,1)S(1)} %get-tuple-element.62.t0, bf16[64,256]{1,0:T(8,128)(2,1)S(1)} %collective-permute-done.15.t1, bf16[64,256]{1,0:T(8,128)(2,1)S(1)} %collective-permute-done.16.t2, bf16[64,256]{1,0:T(8,128)(2,1)S(1)} %collective-permute-done.17.t3, ...), custom_call_target="tpu_custom_call" | custom-call | flops 1073741824 | bytes 1048576 | tf_op jit(solution)/shard_map/back/pallas_call | solution.py:51
  97.4 20.4 %all_to_all.10.got_ref = bf16[64,16,128]{2,1,0:T(8,128)(2,1)S(1)} all-to-all(bf16[64,16,128]{2,1,0:T(8,128)(2,1)S(1)} %back.1), channel_id=1, replica_groups=mesh['range'=64,'chan'=4] {'range'}, dimensions={0} | all-to-all | bytes 524288 | tf_op jit(solution)/shard_map/back/all_to_all | solution.py:352
  117.8 1.7 %restore.1 = bf16[64,1024]{1,0:T(8,128)(2,1)} custom-call(bf16[64,16,128]{2,1,0:T(8,128)(2,1)S(1)} %all_to_all.10.got_ref, s32[8,1024]{1,0:T(8,128)S(1)} %codes.1.refs_4_.codes_ref), custom_call_target="tpu_custom_call" | custom-call | flops 1073741824 | bytes 1048576 | tf_op jit(solution)/shard_map/restore/pallas_call | solution.py:51
  (48 shorter events, 12.9 us)
Async XLA Ops:
  0.0 68.3 %copy-start = (s32[27,1024]{1,0:T(8,128)S(1)}, s32[27,1024]{1,0:T(8,128)}, u32[]{:S(2)}) copy-start(s32[27,1024]{1,0:T(8,128)} %param.10) | copy-start | bytes 331780
  2.6 7.2 %copy-start.3 = (bf16[256,256]{1,0:T(8,128)(2,1)S(1)}, bf16[256,256]{1,0:T(8,128)(2,1)}, u32[]{:S(2)}) copy-start(bf16[256,256]{1,0:T(8,128)(2,1)} %up_ref.1) | copy-start | bytes 393220
  2.6 7.2 %copy-start.4 = (bf16[256,256]{1,0:T(8,128)(2,1)S(1)}, bf16[256,256]{1,0:T(8,128)(2,1)}, u32[]{:S(2)}) copy-start(bf16[256,256]{1,0:T(8,128)(2,1)} %down_ref.1) | copy-start | bytes 393220
  2.6 8.6 %collective-permute-start = (bf16[128,1024]{1,0:T(8,128)(2,1)S(1)}, bf16[128,1024]{1,0:T(8,128)(2,1)S(1)}, u32[]{:S(2)}, u32[]{:S(2)}) collective-permute-start(bf16[128,1024]{1,0:T(8,128)(2,1)S(1)} %gather_features.1.refs_0_), channel_id=1, source_target_pairs={{0,1},{1,2},{2,3},{3,0},{4,5},{5,6},{6,7},{7,4},{8,9},{9,10},{10,1... | collective-permute-start | bytes 786440 | tf_op jit(solution)/shard_map/gather_features/ppermute | solution.py:348
  4.7 13.8 %collective-permute-start.1 = (bf16[128,1024]{1,0:T(8,128)(2,1)S(1)}, bf16[128,1024]{1,0:T(8,128)(2,1)S(1)}, u32[]{:S(2)}, u32[]{:S(2)}) collective-permute-start(bf16[128,1024]{1,0:T(8,128)(2,1)S(1)} %gather_features.1.refs_0_), channel_id=1, source_target_pairs={{0,2},{1,3},{2,0},{3,1},{4,6},{5,7},{6,4},{7,5},{8,10},{9,11},{10,... | collective-permute-start | bytes 786440 | tf_op jit(solution)/shard_map/gather_features/ppermute | solution.py:348
  7.2 11.3 %collective-permute-start.2 = (bf16[128,1024]{1,0:T(8,128)(2,1)S(1)}, bf16[128,1024]{1,0:T(8,128)(2,1)S(1)}, u32[]{:S(2)}, u32[]{:S(2)}) collective-permute-start(bf16[128,1024]{1,0:T(8,128)(2,1)S(1)} %gather_features.1.refs_0_), channel_id=1, source_target_pairs={{0,3},{1,0},{2,1},{3,2},{4,7},{5,4},{6,5},{7,6},{8,11},{9,8},{10,9... | collective-permute-start | bytes 786440 | tf_op jit(solution)/shard_map/gather_features/ppermute | solution.py:348
  9.8 1.2 copy-start.1
  18.5 14.1 %collective-permute-start.3 = (bf16[2240,128]{1,0:T(8,128)(2,1)S(1)}, bf16[2240,128]{1,0:T(8,128)(2,1)S(1)}, u32[]{:S(2)}, u32[]{:S(2)}) collective-permute-start(bf16[2240,128]{1,0:T(8,128)(2,1)S(1)} %get-tuple-element.43.refs_0_), channel_id=1, source_target_pairs={{0,1},{1,2},{2,3},{3,0},{4,5},{5,6},{6,7},{7,4},{8,9},{9,10},{10,1... | collective-permute-start | bytes 1720328 | tf_op jit(solution)/shard_map/gather_weights/ppermute | solution.py:398
  19.7 13.0 %collective-permute-start.4 = (bf16[2240,128]{1,0:T(8,128)(2,1)S(1)}, bf16[2240,128]{1,0:T(8,128)(2,1)S(1)}, u32[]{:S(2)}, u32[]{:S(2)}) collective-permute-start(bf16[2240,128]{1,0:T(8,128)(2,1)S(1)} %get-tuple-element.43.refs_0_), channel_id=1, source_target_pairs={{0,3},{1,0},{2,1},{3,2},{4,7},{5,4},{6,5},{7,6},{8,11},{9,8},{10,9... | collective-permute-start | bytes 1720328 | tf_op jit(solution)/shard_map/gather_weights/ppermute | solution.py:399
  32.7 29.3 %all-to-all-start = ((bf16[64,24,128]{2,1,0:T(8,128)(2,1)}), bf16[64,24,128]{2,1,0:T(8,128)(2,1)S(1)}, u32[]{:S(2)}, u32[]{:S(2)}) async-start(bf16[64,24,128]{2,1,0:T(8,128)(2,1)} %attention.1), calls=%async_computation | async-start | bytes 786432 | tf_op jit(solution)/shard_map/exchange/all_to_all | solution.py:352
  47.3 17.1 %collective-permute-start.10 = (bf16[2240,128]{1,0:T(8,128)(2,1)S(1)}, bf16[2240,128]{1,0:T(8,128)(2,1)S(1)}, u32[]{:S(2)}, u32[]{:S(2)}) collective-permute-start(bf16[2240,128]{1,0:T(8,128)(2,1)S(1)} %collective-permute-done.3.refs_1_), channel_id=1, source_target_pairs={{0,4},{4,0},{8,12},{12,8},{16,20},{20,16},{24,28},{28,24},{32,36},... | collective-permute-start | bytes 1720328 | tf_op jit(solution)/shard_map/exchange/ppermute | solution.py:421
  47.9 19.6 %collective-permute-start.13 = (bf16[2240,128]{1,0:T(8,128)(2,1)S(1)}, bf16[2240,128]{1,0:T(8,128)(2,1)}, u32[]{:S(2)}, u32[]{:S(2)}) collective-permute-start(bf16[2240,128]{1,0:T(8,128)(2,1)S(1)} %collective-permute-done.4.refs_4_), channel_id=1, source_target_pairs={{0,4},{4,0},{8,12},{12,8},{16,20},{20,16},{24,28},{28,24},{32,36},... | collective-permute-start | bytes 1720328 | tf_op jit(solution)/shard_map/exchange/ppermute | solution.py:421
  48.0 9.6 %collective-permute-start.5 = (bf16[1152,128]{1,0:T(8,128)(2,1)S(1)}, bf16[1152,128]{1,0:T(8,128)(2,1)}, u32[]{:S(2)}, u32[]{:S(2)}) collective-permute-start(bf16[1152,128]{1,0:T(8,128)(2,1)S(1)} %slice.6), channel_id=1, source_target_pairs={{0,1},{1,2},{2,3},{3,0},{4,5},{5,6},{6,7},{7,4},{8,9},{9,10},{10,1... | collective-permute-start | bytes 884744 | tf_op jit(solution)/shard_map/exchange/ppermute | solution.py:415
  49.0 7.7 %collective-permute-start.6 = (bf16[1088,128]{1,0:T(8,128)(2,1)S(1)}, bf16[1088,128]{1,0:T(8,128)(2,1)S(1)}, u32[]{:S(2)}, u32[]{:S(2)}) collective-permute-start(bf16[1088,128]{1,0:T(8,128)(2,1)S(1)} %slice.7), channel_id=1, source_target_pairs={{0,3},{1,0},{2,1},{3,2},{4,7},{5,4},{6,5},{7,6},{8,11},{9,8},{10,9... | collective-permute-start | bytes 835592 | tf_op jit(solution)/shard_map/exchange/ppermute | solution.py:416
  61.9 13.2 %collective-permute-start.11 = (bf16[1152,128]{1,0:T(8,128)(2,1)}, bf16[1152,128]{1,0:T(8,128)(2,1)}, u32[]{:S(2)}, u32[]{:S(2)}) collective-permute-start(bf16[1152,128]{1,0:T(8,128)(2,1)} %collective-permute-done.5.refs_2_), channel_id=1, source_target_pairs={{0,4},{4,0},{8,12},{12,8},{16,20},{20,16},{24,28},{28,24},{32,36},... | collective-permute-start | bytes 884744 | tf_op jit(solution)/shard_map/exchange/ppermute | solution.py:421
  62.3 12.8 %collective-permute-start.12 = (bf16[1088,128]{1,0:T(8,128)(2,1)}, bf16[1088,128]{1,0:T(8,128)(2,1)}, u32[]{:S(2)}, u32[]{:S(2)}) collective-permute-start(bf16[1088,128]{1,0:T(8,128)(2,1)} %copy-done.8), channel_id=1, source_target_pairs={{0,4},{4,0},{8,12},{12,8},{16,20},{20,16},{24,28},{28,24},{32,36},... | collective-permute-start | bytes 835592 | tf_op jit(solution)/shard_map/exchange/ppermute | solution.py:421
  63.6 6.8 %collective-permute-start.7 = (bf16[320,256]{1,0:T(8,128)(2,1)}, bf16[320,256]{1,0:T(8,128)(2,1)S(1)}, u32[]{:S(2)}, u32[]{:S(2)}) collective-permute-start(bf16[320,256]{1,0:T(8,128)(2,1)} %compact.1.c0), channel_id=1, source_target_pairs={{0,1},{1,2},{2,3},{3,0},{4,5},{5,6},{6,7},{7,4},{8,9},{9,10},{10,1... | collective-permute-start | bytes 491528 | tf_op jit(solution)/shard_map/compact/ppermute | solution.py:348
  64.4 10.6 %collective-permute-start.8 = (bf16[320,256]{1,0:T(8,128)(2,1)}, bf16[320,256]{1,0:T(8,128)(2,1)S(1)}, u32[]{:S(2)}, u32[]{:S(2)}) collective-permute-start(bf16[320,256]{1,0:T(8,128)(2,1)} %compact.1.c0), channel_id=1, source_target_pairs={{0,2},{1,3},{2,0},{3,1},{4,6},{5,7},{6,4},{7,5},{8,10},{9,11},{10,... | collective-permute-start | bytes 491528 | tf_op jit(solution)/shard_map/compact/ppermute | solution.py:348
  67.5 7.6 %collective-permute-start.9 = (bf16[320,256]{1,0:T(8,128)(2,1)}, bf16[320,256]{1,0:T(8,128)(2,1)S(1)}, u32[]{:S(2)}, u32[]{:S(2)}) collective-permute-start(bf16[320,256]{1,0:T(8,128)(2,1)} %compact.1.c0), channel_id=1, source_target_pairs={{0,3},{1,0},{2,1},{3,2},{4,7},{5,4},{6,5},{7,6},{8,11},{9,8},{10,9... | collective-permute-start | bytes 491528 | tf_op jit(solution)/shard_map/compact/ppermute | solution.py:348
  68.3 13.1 %copy-start.9 = (bf16[1088,128]{1,0:T(8,128)(2,1)S(1)}, bf16[1088,128]{1,0:T(8,128)(2,1)}, u32[]{:S(2)}) copy-start(bf16[1088,128]{1,0:T(8,128)(2,1)} %copy-done.8) | copy-start | bytes 835588
  77.0 9.0 %collective-permute-start.14 = (bf16[256,256]{1,0:T(8,128)(2,1)S(1)}, bf16[256,256]{1,0:T(8,128)(2,1)S(1)}, u32[]{:S(2)}, u32[]{:S(2)}) collective-permute-start(bf16[256,256]{1,0:T(8,128)(2,1)S(1)} %get-tuple-element.61.third_ref), channel_id=1, source_target_pairs={{0,4},{4,8},{8,12},{12,16},{16,20},{20,24},{24,28},{28,32},{32,36}... | collective-permute-start | bytes 393224 | tf_op jit(solution)/shard_map/window/ppermute | solution.py:438
  90.4 4.6 %collective-permute-start.15 = (bf16[64,256]{1,0:T(8,128)(2,1)S(1)}, bf16[64,256]{1,0:T(8,128)(2,1)S(1)}, u32[]{:S(2)}, u32[]{:S(2)}) collective-permute-start(bf16[64,256]{1,0:T(8,128)(2,1)S(1)} %get-tuple-element.63), channel_id=1, source_target_pairs={{0,1},{1,2},{2,3},{3,0},{4,5},{5,6},{6,7},{7,4},{8,9},{9,10},{10,1... | collective-permute-start | bytes 98312 | tf_op jit(solution)/shard_map/turn_back/ppermute | solution.py:457
  90.5 4.5 %collective-permute-start.16 = (bf16[64,256]{1,0:T(8,128)(2,1)S(1)}, bf16[64,256]{1,0:T(8,128)(2,1)S(1)}, u32[]{:S(2)}, u32[]{:S(2)}) collective-permute-start(bf16[64,256]{1,0:T(8,128)(2,1)S(1)} %get-tuple-element.64), channel_id=1, source_target_pairs={{0,2},{1,3},{2,0},{3,1},{4,6},{5,7},{6,4},{7,5},{8,10},{9,11},{10,... | collective-permute-start | bytes 98312 | tf_op jit(solution)/shard_map/turn_back/ppermute | solution.py:457
  92.5 3.3 %collective-permute-start.17 = (bf16[64,256]{1,0:T(8,128)(2,1)S(1)}, bf16[64,256]{1,0:T(8,128)(2,1)S(1)}, u32[]{:S(2)}, u32[]{:S(2)}) collective-permute-start(bf16[64,256]{1,0:T(8,128)(2,1)S(1)} %get-tuple-element.65), channel_id=1, source_target_pairs={{0,3},{1,0},{2,1},{3,2},{4,7},{5,4},{6,5},{7,6},{8,11},{9,8},{10,9... | collective-permute-start | bytes 98312 | tf_op jit(solution)/shard_map/turn_back/ppermute | solution.py:457
  (5 other events, 4.0 us)

commit v4 on v3

--- a/solution.py
+++ b/solution.py
@@ -37,8 +37,9 @@
     return mask.astype(F32).astype(BF16)
 
 
-def kernel_call(body, outs, cost, operands, scratch=(), vmem=48, managed=False):
+def kernel_call(body, outs, cost, operands, scratch=(), vmem=24, managed=False):
     place = None if managed else pltpu.VMEM
+    vmem = 62 if managed else vmem
     specs = [pl.BlockSpec(memory_space=pltpu.SMEM if x.shape == (1,) else place) for x in operands]
     call = pl.pallas_call(
         body,
@@ -222,16 +223,9 @@
 
 
 def weight_reader(near_w, far_w, quarter):
-    split = near_w[2].shape[0]
-
-    def weight(k, section, at, size):
-        if k == 2:
-            piece = 2 if section < split else 3
-            section = section % split
-        else:
-            piece = (0, 1, None, 4)[k]
-        rows = pl.ds(pl.multiple_of(section + at, quarter), size)
-        return jnp.concatenate([near_w[piece][rows, :], far_w[piece][rows, :]], axis=1)
+    def weight(k, at, size):
+        rows = pl.ds(pl.multiple_of(at, quarter), size)
+        return jnp.concatenate([near_w[k][rows, :], far_w[k][rows, :]], axis=1)
 
     return weight
 
@@ -249,7 +243,7 @@
     group = 3
 
     def kernel(j):
-        return jnp.concatenate([weight(k, j * quarter, 0, quarter) for k in range(CHAN)], axis=0)
+        return jnp.concatenate([weight(k, j * quarter, quarter) for k in range(CHAN)], axis=0)
 
     for start in range(0, KER, group):
         js = range(start, start + group)
@@ -261,7 +255,7 @@
 
 
 def conv_first_body(me_ref, core_ref, win_ref, near_ref, *refs):
-    near_w, far_w, out_ref, turned = refs[0:5], refs[5:10], refs[10], refs[11]
+    near_w, far_w, out_ref, turned = refs[0:4], refs[4:8], refs[8], refs[9]
     me, core = me_ref[0], core_ref[0]
     quarter = 64
     turned[...] = win_ref[0:256, :].astype(F32).T
@@ -275,7 +269,7 @@
 
 
 def conv_second_body(me_ref, core_ref, acc_ref, halo_ref, third_ref, near_ref, *refs):
-    near_w, far_w, outs, norm_ref = refs[0:5], refs[5:10], refs[10:14], refs[14]
+    near_w, far_w, outs, norm_ref = refs[0:4], refs[4:8], refs[8:12], refs[12]
     me, core = me_ref[0], core_ref[0]
     quarter = 64
     whole = CHAN * quarter
@@ -293,10 +287,10 @@
     up_at = KER * quarter
     down_at = up_at + whole
     for k in range(CHAN):
-        up = [weight(k, up_at, x, half) for x in (lo, hi)]
+        up = [weight(k, up_at + x, half) for x in (lo, hi)]
         hidden = dot(jnp.concatenate(up, axis=0), norm_ref[...])
         hidden = (0.5 * hidden * (1.0 + lax.erf(hidden * (2.0 ** -0.5)))).astype(BF16)
-        down = [weight(k, down_at, sender(me, p) * quarter, quarter) for p in range(CHAN)]
+        down = [weight(k, down_at + sender(me, p) * quarter, quarter) for p in range(CHAN)]
         total += dot(jnp.concatenate(down, axis=0), hidden)
     third = total.astype(BF16)
     for k in range(CHAN):
@@ -382,21 +376,18 @@
             sds((8, rows), I32),
             1 << 20,
             [me_ref, hilbert_rank[None, :]],
-            managed=True,
         )
     with jax.named_scope("gather_weights"):
         size = KER * quarter + 2 * up_weight.shape[1]
-        split = (size // quarter + 1) // 2 * quarter
         near0, far0 = kernel_call(
             pack_body,
             (sds((size, 128), BF16), sds((size, 128), BF16)),
             1 << 20,
             [core_ref, conv_weight.reshape(KER * quarter, whole), up_weight, down_weight],
-            managed=True,
         )
         blocks, codes, near0, far0 = lax.optimization_barrier((blocks, codes, near0, far0))
-        near1 = lax.ppermute(near0, "chan", turn(1))
-        near3 = lax.ppermute(near0, "chan", turn(3))
+        near_w = gather_chan(near0)
+        far_w = [far0] + [lax.ppermute(w, "range", swap) for w in near_w[1:]]
     with jax.named_scope("attention"):
         send = kernel_call(
             attention_body,
@@ -410,15 +401,8 @@
             ],
         )
     with jax.named_scope("exchange"):
-        send, near1, near3 = lax.optimization_barrier((send, near1, near3))
-        near2 = (
-            lax.ppermute(near1[:split], "chan", turn(1)),
-            lax.ppermute(near3[split:], "chan", turn(3)),
-        )
         got = exchange(send)
-        got, near2 = lax.optimization_barrier((got, near2))
-        near_w = [near0, near1, near2[0], near2[1], near3]
-        far_w = [far0] + [lax.ppermute(w, "range", swap) for w in near_w[1:]]
+        got, far_w = lax.optimization_barrier((got, far_w))
     with jax.named_scope("compact"):
         limit = (rows + (CHAN - 1) * owners) // CHAN
         limit = (limit + 15) // 16 * 16

time: 120 us -> 115 us (0.958)
  starting transfers between devices: 38.8 us -> 34.2 us
  waiting for transfers between devices: 28.7 us -> 31.5 us
  local copies, waits for them, and re-layouts: 5.22 us -> 3.53 us
  blocking collectives: 20.4 us -> 18.8 us
    all_to_all x1, waiting for transfers between devices: 4.37 us -> 13.5 us  [exchange(): lax.all_to_all(parts, 'range', split_axis=0, concat_axis=0, tiled=True)]
    ppermute x4 -> x0, waiting for transfers between devices: 7.65 us -> none  [the longest x1 5.78 us: shards(): lax.ppermute(near3[split:], 'chan', turn(3))]
    ppermute x4 -> x0, starting transfers between devices: 5.52 us -> none  [the longest x1 1.91 us: shards(): lax.ppermute(near3[split:], 'chan', turn(3))]
    ppermute x6 -> x9, starting transfers between devices: 10.4 us -> 12.5 us  [gather_chan(): return [x] + [lax.ppermute(x, 'chan', turn(k)) for k in range(1, CHAN)]]
    all_to_all x1, blocking collectives: 20.4 us -> 18.8 us  [exchange(): lax.all_to_all(parts, 'range', split_axis=0, concat_axis=0, tiled=True)]
    unnamed x20 -> x16, local copies, waits for them, and re-layouts: 5.18 us -> 3.53 us
    ppermute x6 -> x9, waiting for transfers between devices: 14 us -> 15.6 us  [gather_chan(): return [x] + [lax.ppermute(x, 'chan', turn(k)) for k in range(1, CHAN)]]
  transfers between devices with their start and end apart: 19 -> 17, of which waited for: 9 -> 8; matrix products, arithmetic and copies ran while one was open for 0% -> 0% of each run, Pallas kernels for 14% -> 14%
where the time goes in v4:
time: 115 us
  starting transfers between devices  34.2 us (30%)
  waiting for transfers between devices  31.5 us (27%)
  Pallas kernels  26.8 us (23%)
  blocking collectives  18.8 us (16%)
  local copies, waits for them, and re-layouts  3.53 us (3%)
    pallas_call x10, Pallas kernels, kernel_call(): return call(*operands)  26.8 us
    all_to_all x1, blocking collectives, exchange(): lax.all_to_all(parts, 'range', split_axis=0, concat_axis=0, tiled=True)  18.8 us
    ppermute x9, waiting for transfers between devices, gather_chan(): return [x] + [lax.ppermute(x, 'chan', turn(k)) for k in range(1, CHAN)]  15.6 us
    all_to_all x1, starting transfers between devices, exchange(): lax.all_to_all(parts, 'range', split_axis=0, concat_axis=0, tiled=True)  14.3 us
    all_to_all x1, waiting for transfers between devices, exchange(): lax.all_to_all(parts, 'range', split_axis=0, concat_axis=0, tiled=True)  13.5 us
    ppermute x9, starting transfers between devices, gather_chan(): return [x] + [lax.ppermute(x, 'chan', turn(k)) for k in range(1, CHAN)]  12.5 us
    ppermute x1, starting transfers between devices, shards(): halo = lax.ppermute(third, ('range', 'chan'), pairs)  3.66 us
    unnamed x16, local copies, waits for them, and re-layouts  3.53 us
  transfers between devices with their start and end apart: 17, of which 8 were waited for; matrix products, arithmetic and copies ran while one was open for 0% of the time, Pallas kernels for 14%

profile of v4, /device:TPU:1, one launch (start us, length us, event | category | flops | bytes accessed | tf_op | source)
XLA Modules:
  0.0 115.0 jit_solution(4811734468991831136)
XLA Ops:
  0.0 1.7 %gather_features.1.refs_0_ = bf16[128,1024]{1,0:T(8,128)(2,1)} custom-call(bf16[64,1024]{1,0:T(8,128)(2,1)} %x_ref.1, bf16[192,256]{1,0:T(8,128)(2,1)} %bitcast.11, bf16[64,256]{1,0:T(8,128)(2,1)} %bitcast.12), custom_call_target="tpu_custom_call" | custom-call | flops 1048576 | bytes 1048576 | tf_op jit(solution)/shard_map/gather_features/pallas_call | solution.py:52
  1.8 2.0 %collective-permute-start = (bf16[128,1024]{1,0:T(8,128)(2,1)}, bf16[128,1024]{1,0:T(8,128)(2,1)S(1)}, u32[]{:S(2)}, u32[]{:S(2)}) collective-permute-start(bf16[128,1024]{1,0:T(8,128)(2,1)} %gather_features.1.refs_0_), channel_id=1, source_target_pairs={{0,1},{1,2},{2,3},{3,0},{4,5},{5,6},{6,7},{7,4},{8,9},{9,10},{10,1... | collective-permute-start | bytes 786440 | tf_op jit(solution)/shard_map/gather_features/ppermute | solution.py:342
  3.8 2.5 %collective-permute-start.1 = (bf16[128,1024]{1,0:T(8,128)(2,1)}, bf16[128,1024]{1,0:T(8,128)(2,1)S(1)}, u32[]{:S(2)}, u32[]{:S(2)}) collective-permute-start(bf16[128,1024]{1,0:T(8,128)(2,1)} %gather_features.1.refs_0_), channel_id=1, source_target_pairs={{0,2},{1,3},{2,0},{3,1},{4,6},{5,7},{6,4},{7,5},{8,10},{9,11},{10,... | collective-permute-start | bytes 786440 | tf_op jit(solution)/shard_map/gather_features/ppermute | solution.py:342
  6.2 1.2 %collective-permute-start.2 = (bf16[128,1024]{1,0:T(8,128)(2,1)}, bf16[128,1024]{1,0:T(8,128)(2,1)S(1)}, u32[]{:S(2)}, u32[]{:S(2)}) collective-permute-start(bf16[128,1024]{1,0:T(8,128)(2,1)} %gather_features.1.refs_0_), channel_id=1, source_target_pairs={{0,3},{1,0},{2,1},{3,2},{4,7},{5,4},{6,5},{7,6},{8,11},{9,8},{10,9... | collective-permute-start | bytes 786440 | tf_op jit(solution)/shard_map/gather_features/ppermute | solution.py:342
  8.9 1.2 %copy-done.1 = bf16[27,64,256]{2,1,0:T(8,128)(2,1)S(1)} copy-done((bf16[27,64,256]{2,1,0:T(8,128)(2,1)S(1)}, bf16[27,64,256]{2,1,0:T(8,128)(2,1)}, u32[]{:S(2)}) %copy-start.1) | copy-done | bytes 884760
  10.3 7.5 %collective-permute-done.1.refs_2_ = bf16[128,1024]{1,0:T(8,128)(2,1)S(1)} collective-permute-done((bf16[128,1024]{1,0:T(8,128)(2,1)}, bf16[128,1024]{1,0:T(8,128)(2,1)S(1)}, u32[]{:S(2)}, u32[]{:S(2)}) %collective-permute-start.1) | collective-permute-done | bytes 262176 | tf_op jit(solution)/shard_map/gather_features/ppermute | solution.py:342
  18.5 1.0 collective-permute-start.3
  19.5 2.3 %collective-permute-start.5 = (bf16[2240,128]{1,0:T(8,128)(2,1)S(1)}, bf16[2240,128]{1,0:T(8,128)(2,1)S(1)}, u32[]{:S(2)}, u32[]{:S(2)}) collective-permute-start(bf16[2240,128]{1,0:T(8,128)(2,1)S(1)} %get-tuple-element.42.refs_0_), channel_id=1, source_target_pairs={{0,2},{1,3},{2,0},{3,1},{4,6},{5,7},{6,4},{7,5},{8,10},{9,11},{10,... | collective-permute-start | bytes 1720328 | tf_op jit(solution)/shard_map/gather_weights/ppermute | solution.py:342
  23.6 9.8 %attention.1 = bf16[64,24,128]{2,1,0:T(8,128)(2,1)} custom-call(s32[1]{0:T(128)} %bitcast.me_ref, s32[1]{0:T(128)} %bitcast.2.range_ref, bf16[128,1024]{1,0:T(8,128)(2,1)S(1)} %copy-done.2, bf16[128,1024]{1,0:T(8,128)(2,1)S(1)} %collective-permute-done.refs_1_, bf16[128,1024]{1,0:T(8,128)(2,1)S(1)} %collective-permute-done.1.refs_2_, ...), custom_call_target="tpu_custom_call" | custom-call | flops 4294967296 | bytes 1048576 | tf_op jit(solution)/shard_map/attention/pallas_call | solution.py:52
  33.4 14.3 %all-to-all-start = ((bf16[64,24,128]{2,1,0:T(8,128)(2,1)}), bf16[64,24,128]{2,1,0:T(8,128)(2,1)S(1)}, u32[]{:S(2)}, u32[]{:S(2)}) async-start(bf16[64,24,128]{2,1,0:T(8,128)(2,1)} %attention.1), calls=%async_computation | async-start | bytes 786432 | tf_op jit(solution)/shard_map/exchange/all_to_all | solution.py:346
  48.8 13.5 %all-to-all-done.got_ref = bf16[64,24,128]{2,1,0:T(8,128)(2,1)S(1)} async-done(((bf16[64,24,128]{2,1,0:T(8,128)(2,1)}), bf16[64,24,128]{2,1,0:T(8,128)(2,1)S(1)}, u32[]{:S(2)}, u32[]{:S(2)}) %all-to-all-start) | async-done | bytes 393248 | tf_op jit(solution)/shard_map/exchange/all_to_all | solution.py:346
  63.5 2.0 %collective-permute-start.11 = (bf16[320,256]{1,0:T(8,128)(2,1)S(1)}, bf16[320,256]{1,0:T(8,128)(2,1)S(1)}, u32[]{:S(2)}, u32[]{:S(2)}) collective-permute-start(bf16[320,256]{1,0:T(8,128)(2,1)S(1)} %compact.1.c0), channel_id=1, source_target_pairs={{0,3},{1,0},{2,1},{3,2},{4,7},{5,4},{6,5},{7,6},{8,11},{9,8},{10,9... | collective-permute-start | bytes 491528 | tf_op jit(solution)/shard_map/compact/ppermute | solution.py:342
  65.5 4.3 %collective-permute-done.10.c2 = bf16[320,256]{1,0:T(8,128)(2,1)S(1)} collective-permute-done((bf16[320,256]{1,0:T(8,128)(2,1)S(1)}, bf16[320,256]{1,0:T(8,128)(2,1)S(1)}, u32[]{:S(2)}, u32[]{:S(2)}) %collective-permute-start.10) | collective-permute-done | bytes 163872 | tf_op jit(solution)/shard_map/compact/ppermute | solution.py:342
  69.8 1.0 collective-permute-done.11.c3
  70.8 2.8 %collective-permute-done.9.c1 = bf16[320,256]{1,0:T(8,128)(2,1)S(1)} collective-permute-done((bf16[320,256]{1,0:T(8,128)(2,1)S(1)}, bf16[320,256]{1,0:T(8,128)(2,1)S(1)}, u32[]{:S(2)}, u32[]{:S(2)}) %collective-permute-start.9) | collective-permute-done | bytes 163872 | tf_op jit(solution)/shard_map/compact/ppermute | solution.py:342
  73.6 1.0 window.1
  74.6 3.7 %collective-permute-start.12 = (bf16[256,256]{1,0:T(8,128)(2,1)S(1)}, bf16[256,256]{1,0:T(8,128)(2,1)S(1)}, u32[]{:S(2)}, u32[]{:S(2)}) collective-permute-start(bf16[256,256]{1,0:T(8,128)(2,1)S(1)} %get-tuple-element.57.third_ref), channel_id=1, source_target_pairs={{0,4},{4,8},{8,12},{12,16},{16,20},{20,24},{24,28},{28,32},{32,36}... | collective-permute-start | bytes 393224 | tf_op jit(solution)/shard_map/window/ppermute | solution.py:422
  78.3 4.9 %conv.2.acc_ref = f32[256,256]{1,0:T(8,128)S(1)} custom-call(s32[1]{0:T(128)} %bitcast.me_ref, s32[1]{0:T(128)} %bitcast.1.core_ref, bf16[512,256]{1,0:T(8,128)(2,1)S(1)} %get-tuple-element.52.win_ref, s32[27,256]{1,0:T(8,128)S(1)} %constant_dynamic-slice_fusion.near_ref, bf16[2240,128]{1,0:T(8,128)(2,1)S(1)} %get-tuple-element.42.refs_0_, ...), custom_call_target="tpu_custom_call" | custom-call | flops 4294967296 | bytes 1048576 | tf_op jit(solution)/shard_map/conv/pallas_call | solution.py:52
  83.1 4.6 %conv.3 = (bf16[64,256]{1,0:T(8,128)(2,1)S(1)}, bf16[64,256]{1,0:T(8,128)(2,1)S(1)}, bf16[64,256]{1,0:T(8,128)(2,1)S(1)}, bf16[64,256]{1,0:T(8,128)(2,1)S(1)}) custom-call(s32[1]{0:T(128)} %bitcast.me_ref, s32[1]{0:T(128)} %bitcast.1.core_ref, f32[256,256]{1,0:T(8,128)S(1)} %conv.2.acc_ref, bf16[256,256]{1,0:T(8,128)(2,1)S(1)} %collective-permute-done.12.halo_ref, ...), custom_call_target="tpu_custom_call" | custom-call | flops 4294967296 | bytes 1048576 | tf_op jit(solution)/shard_map/conv/pallas_call | solution.py:52
  88.5 2.0 %collective-permute-start.15 = (bf16[64,256]{1,0:T(8,128)(2,1)S(1)}, bf16[64,256]{1,0:T(8,128)(2,1)S(1)}, u32[]{:S(2)}, u32[]{:S(2)}) collective-permute-start(bf16[64,256]{1,0:T(8,128)(2,1)S(1)} %get-tuple-element.61), channel_id=1, source_target_pairs={{0,3},{1,0},{2,1},{3,2},{4,7},{5,4},{6,5},{7,6},{8,11},{9,8},{10,9... | collective-permute-start | bytes 98312 | tf_op jit(solution)/shard_map/turn_back/ppermute | solution.py:441
  90.5 1.3 %collective-permute-done.13.t1 = bf16[64,256]{1,0:T(8,128)(2,1)S(1)} collective-permute-done((bf16[64,256]{1,0:T(8,128)(2,1)S(1)}, bf16[64,256]{1,0:T(8,128)(2,1)S(1)}, u32[]{:S(2)}, u32[]{:S(2)}) %collective-permute-start.13) | collective-permute-done | bytes 32800 | tf_op jit(solution)/shard_map/turn_back/ppermute | solution.py:441
  93.0 1.6 %back.1 = bf16[64,16,128]{2,1,0:T(8,128)(2,1)S(1)} custom-call(s32[1]{0:T(128)} %bitcast.me_ref, bf16[64,256]{1,0:T(8,128)(2,1)S(1)} %get-tuple-element.58.t0, bf16[64,256]{1,0:T(8,128)(2,1)S(1)} %collective-permute-done.13.t1, bf16[64,256]{1,0:T(8,128)(2,1)S(1)} %collective-permute-done.14.t2, bf16[64,256]{1,0:T(8,128)(2,1)S(1)} %collective-permute-done.15.t3, ...), custom_call_target="tpu_custom_call" | custom-call | flops 1073741824 | bytes 1048576 | tf_op jit(solution)/shard_map/back/pallas_call | solution.py:52
  94.6 18.8 %all_to_all.10.got_ref = bf16[64,16,128]{2,1,0:T(8,128)(2,1)S(1)} all-to-all(bf16[64,16,128]{2,1,0:T(8,128)(2,1)S(1)} %back.1), channel_id=1, replica_groups=mesh['range'=64,'chan'=4] {'range'}, dimensions={0} | all-to-all | bytes 524288 | tf_op jit(solution)/shard_map/back/all_to_all | solution.py:346
  113.3 1.7 %restore.1 = bf16[64,1024]{1,0:T(8,128)(2,1)} custom-call(bf16[64,16,128]{2,1,0:T(8,128)(2,1)S(1)} %all_to_all.10.got_ref, s32[8,1024]{1,0:T(8,128)S(1)} %codes.1.refs_4_.codes_ref), custom_call_target="tpu_custom_call" | custom-call | flops 1073741824 | bytes 1048576 | tf_op jit(solution)/shard_map/restore/pallas_call | solution.py:52
  (38 shorter events, 8.3 us)
Async XLA Ops:
  0.0 65.5 %copy-start = (s32[27,1024]{1,0:T(8,128)S(1)}, s32[27,1024]{1,0:T(8,128)}, u32[]{:S(2)}) copy-start(s32[27,1024]{1,0:T(8,128)} %param.10) | copy-start | bytes 331780
  0.0 8.8 %copy-start.3 = (bf16[256,256]{1,0:T(8,128)(2,1)S(1)}, bf16[256,256]{1,0:T(8,128)(2,1)}, u32[]{:S(2)}) copy-start(bf16[256,256]{1,0:T(8,128)(2,1)} %up_ref.1) | copy-start | bytes 393220
  0.0 8.8 %copy-start.4 = (bf16[256,256]{1,0:T(8,128)(2,1)S(1)}, bf16[256,256]{1,0:T(8,128)(2,1)}, u32[]{:S(2)}) copy-start(bf16[256,256]{1,0:T(8,128)(2,1)} %down_ref.1) | copy-start | bytes 393220
  1.8 8.5 %collective-permute-start = (bf16[128,1024]{1,0:T(8,128)(2,1)}, bf16[128,1024]{1,0:T(8,128)(2,1)S(1)}, u32[]{:S(2)}, u32[]{:S(2)}) collective-permute-start(bf16[128,1024]{1,0:T(8,128)(2,1)} %gather_features.1.refs_0_), channel_id=1, source_target_pairs={{0,1},{1,2},{2,3},{3,0},{4,5},{5,6},{6,7},{7,4},{8,9},{9,10},{10,1... | collective-permute-start | bytes 786440 | tf_op jit(solution)/shard_map/gather_features/ppermute | solution.py:342
  3.8 14.0 %collective-permute-start.1 = (bf16[128,1024]{1,0:T(8,128)(2,1)}, bf16[128,1024]{1,0:T(8,128)(2,1)S(1)}, u32[]{:S(2)}, u32[]{:S(2)}) collective-permute-start(bf16[128,1024]{1,0:T(8,128)(2,1)} %gather_features.1.refs_0_), channel_id=1, source_target_pairs={{0,2},{1,3},{2,0},{3,1},{4,6},{5,7},{6,4},{7,5},{8,10},{9,11},{10,... | collective-permute-start | bytes 786440 | tf_op jit(solution)/shard_map/gather_features/ppermute | solution.py:342
  6.2 11.5 %collective-permute-start.2 = (bf16[128,1024]{1,0:T(8,128)(2,1)}, bf16[128,1024]{1,0:T(8,128)(2,1)S(1)}, u32[]{:S(2)}, u32[]{:S(2)}) collective-permute-start(bf16[128,1024]{1,0:T(8,128)(2,1)} %gather_features.1.refs_0_), channel_id=1, source_target_pairs={{0,3},{1,0},{2,1},{3,2},{4,7},{5,4},{6,5},{7,6},{8,11},{9,8},{10,9... | collective-permute-start | bytes 786440 | tf_op jit(solution)/shard_map/gather_features/ppermute | solution.py:342
  8.9 1.2 %copy-start.1 = (bf16[27,64,256]{2,1,0:T(8,128)(2,1)S(1)}, bf16[27,64,256]{2,1,0:T(8,128)(2,1)}, u32[]{:S(2)}) copy-start(bf16[27,64,256]{2,1,0:T(8,128)(2,1)} %param.13) | copy-start | bytes 2654212
  10.0 12.7 %copy-start.2 = (bf16[128,1024]{1,0:T(8,128)(2,1)S(1)}, bf16[128,1024]{1,0:T(8,128)(2,1)}, u32[]{:S(2)}) copy-start(bf16[128,1024]{1,0:T(8,128)(2,1)} %gather_features.1.refs_0_) | copy-start | bytes 786436
  17.8 0.7 copy-start.6
  18.5 29.2 %collective-permute-start.3 = (bf16[2240,128]{1,0:T(8,128)(2,1)S(1)}, bf16[2240,128]{1,0:T(8,128)(2,1)S(1)}, u32[]{:S(2)}, u32[]{:S(2)}) collective-permute-start(bf16[2240,128]{1,0:T(8,128)(2,1)S(1)} %get-tuple-element.42.refs_0_), channel_id=1, source_target_pairs={{0,1},{1,2},{2,3},{3,0},{4,5},{5,6},{6,7},{7,4},{8,9},{9,10},{10,1... | collective-permute-start | bytes 1720328 | tf_op jit(solution)/shard_map/gather_weights/ppermute | solution.py:342
  19.5 28.8 %collective-permute-start.5 = (bf16[2240,128]{1,0:T(8,128)(2,1)S(1)}, bf16[2240,128]{1,0:T(8,128)(2,1)S(1)}, u32[]{:S(2)}, u32[]{:S(2)}) collective-permute-start(bf16[2240,128]{1,0:T(8,128)(2,1)S(1)} %get-tuple-element.42.refs_0_), channel_id=1, source_target_pairs={{0,2},{1,3},{2,0},{3,1},{4,6},{5,7},{6,4},{7,5},{8,10},{9,11},{10,... | collective-permute-start | bytes 1720328 | tf_op jit(solution)/shard_map/gather_weights/ppermute | solution.py:342
  21.8 26.6 %collective-permute-start.7 = (bf16[2240,128]{1,0:T(8,128)(2,1)S(1)}, bf16[2240,128]{1,0:T(8,128)(2,1)}, u32[]{:S(2)}, u32[]{:S(2)}) collective-permute-start(bf16[2240,128]{1,0:T(8,128)(2,1)S(1)} %get-tuple-element.42.refs_0_), channel_id=1, source_target_pairs={{0,3},{1,0},{2,1},{3,2},{4,7},{5,4},{6,5},{7,6},{8,11},{9,8},{10,9... | collective-permute-start | bytes 1720328 | tf_op jit(solution)/shard_map/gather_weights/ppermute | solution.py:342
  22.7 1.0 copy-start.7
  33.4 28.9 %all-to-all-start = ((bf16[64,24,128]{2,1,0:T(8,128)(2,1)}), bf16[64,24,128]{2,1,0:T(8,128)(2,1)S(1)}, u32[]{:S(2)}, u32[]{:S(2)}) async-start(bf16[64,24,128]{2,1,0:T(8,128)(2,1)} %attention.1), calls=%async_computation | async-start | bytes 786432 | tf_op jit(solution)/shard_map/exchange/all_to_all | solution.py:346
  47.8 14.6 %collective-permute-start.4 = (bf16[2240,128]{1,0:T(8,128)(2,1)S(1)}, bf16[2240,128]{1,0:T(8,128)(2,1)}, u32[]{:S(2)}, u32[]{:S(2)}) collective-permute-start(bf16[2240,128]{1,0:T(8,128)(2,1)S(1)} %collective-permute-done.3.refs_1_), channel_id=1, source_target_pairs={{0,4},{4,0},{8,12},{12,8},{16,20},{20,16},{24,28},{28,24},{32,36},... | collective-permute-start | bytes 1720328 | tf_op jit(solution)/shard_map/gather_weights/ppermute | solution.py:390
  48.3 14.1 %collective-permute-start.6 = (bf16[2240,128]{1,0:T(8,128)(2,1)S(1)}, bf16[2240,128]{1,0:T(8,128)(2,1)}, u32[]{:S(2)}, u32[]{:S(2)}) collective-permute-start(bf16[2240,128]{1,0:T(8,128)(2,1)S(1)} %collective-permute-done.5.refs_2_), channel_id=1, source_target_pairs={{0,4},{4,0},{8,12},{12,8},{16,20},{20,16},{24,28},{28,24},{32,36},... | collective-permute-start | bytes 1720328 | tf_op jit(solution)/shard_map/gather_weights/ppermute | solution.py:390
  48.4 14.0 %collective-permute-start.8 = (bf16[2240,128]{1,0:T(8,128)(2,1)}, bf16[2240,128]{1,0:T(8,128)(2,1)}, u32[]{:S(2)}, u32[]{:S(2)}) collective-permute-start(bf16[2240,128]{1,0:T(8,128)(2,1)} %collective-permute-done.7.refs_3_), channel_id=1, source_target_pairs={{0,4},{4,0},{8,12},{12,8},{16,20},{20,16},{24,28},{28,24},{32,36},... | collective-permute-start | bytes 1720328 | tf_op jit(solution)/shard_map/gather_weights/ppermute | solution.py:390
  62.8 6.9 %collective-permute-start.10 = (bf16[320,256]{1,0:T(8,128)(2,1)S(1)}, bf16[320,256]{1,0:T(8,128)(2,1)S(1)}, u32[]{:S(2)}, u32[]{:S(2)}) collective-permute-start(bf16[320,256]{1,0:T(8,128)(2,1)S(1)} %compact.1.c0), channel_id=1, source_target_pairs={{0,2},{1,3},{2,0},{3,1},{4,6},{5,7},{6,4},{7,5},{8,10},{9,11},{10,... | collective-permute-start | bytes 491528 | tf_op jit(solution)/shard_map/compact/ppermute | solution.py:342
  63.5 7.3 %collective-permute-start.11 = (bf16[320,256]{1,0:T(8,128)(2,1)S(1)}, bf16[320,256]{1,0:T(8,128)(2,1)S(1)}, u32[]{:S(2)}, u32[]{:S(2)}) collective-permute-start(bf16[320,256]{1,0:T(8,128)(2,1)S(1)} %compact.1.c0), channel_id=1, source_target_pairs={{0,3},{1,0},{2,1},{3,2},{4,7},{5,4},{6,5},{7,6},{8,11},{9,8},{10,9... | collective-permute-start | bytes 491528 | tf_op jit(solution)/shard_map/compact/ppermute | solution.py:342
  65.5 8.1 %collective-permute-start.9 = (bf16[320,256]{1,0:T(8,128)(2,1)S(1)}, bf16[320,256]{1,0:T(8,128)(2,1)S(1)}, u32[]{:S(2)}, u32[]{:S(2)}) collective-permute-start(bf16[320,256]{1,0:T(8,128)(2,1)S(1)} %compact.1.c0), channel_id=1, source_target_pairs={{0,1},{1,2},{2,3},{3,0},{4,5},{5,6},{6,7},{7,4},{8,9},{9,10},{10,1... | collective-permute-start | bytes 491528 | tf_op jit(solution)/shard_map/compact/ppermute | solution.py:342
  74.6 8.5 %collective-permute-start.12 = (bf16[256,256]{1,0:T(8,128)(2,1)S(1)}, bf16[256,256]{1,0:T(8,128)(2,1)S(1)}, u32[]{:S(2)}, u32[]{:S(2)}) collective-permute-start(bf16[256,256]{1,0:T(8,128)(2,1)S(1)} %get-tuple-element.57.third_ref), channel_id=1, source_target_pairs={{0,4},{4,8},{8,12},{12,16},{16,20},{20,24},{24,28},{28,32},{32,36}... | collective-permute-start | bytes 393224 | tf_op jit(solution)/shard_map/window/ppermute | solution.py:422
  87.8 4.1 %collective-permute-start.13 = (bf16[64,256]{1,0:T(8,128)(2,1)S(1)}, bf16[64,256]{1,0:T(8,128)(2,1)S(1)}, u32[]{:S(2)}, u32[]{:S(2)}) collective-permute-start(bf16[64,256]{1,0:T(8,128)(2,1)S(1)} %get-tuple-element.59), channel_id=1, source_target_pairs={{0,1},{1,2},{2,3},{3,0},{4,5},{5,6},{6,7},{7,4},{8,9},{9,10},{10,1... | collective-permute-start | bytes 98312 | tf_op jit(solution)/shard_map/turn_back/ppermute | solution.py:441
  87.9 4.4 %collective-permute-start.14 = (bf16[64,256]{1,0:T(8,128)(2,1)S(1)}, bf16[64,256]{1,0:T(8,128)(2,1)S(1)}, u32[]{:S(2)}, u32[]{:S(2)}) collective-permute-start(bf16[64,256]{1,0:T(8,128)(2,1)S(1)} %get-tuple-element.60), channel_id=1, source_target_pairs={{0,2},{1,3},{2,0},{3,1},{4,6},{5,7},{6,4},{7,5},{8,10},{9,11},{10,... | collective-permute-start | bytes 98312 | tf_op jit(solution)/shard_map/turn_back/ppermute | solution.py:441
  88.5 4.4 %collective-permute-start.15 = (bf16[64,256]{1,0:T(8,128)(2,1)S(1)}, bf16[64,256]{1,0:T(8,128)(2,1)S(1)}, u32[]{:S(2)}, u32[]{:S(2)}) collective-permute-start(bf16[64,256]{1,0:T(8,128)(2,1)S(1)} %get-tuple-element.61), channel_id=1, source_target_pairs={{0,3},{1,0},{2,1},{3,2},{4,7},{5,4},{6,5},{7,6},{8,11},{9,8},{10,9... | collective-permute-start | bytes 98312 | tf_op jit(solution)/shard_map/turn_back/ppermute | solution.py:441
  (1 other events, 0.7 us)

commit v5 on v4

--- a/solution.py
+++ b/solution.py
@@ -122,13 +122,20 @@
     keys = dot(weight(1), norm).astype(BF16)
     vals = dot(weight(2), norm).astype(BF16)
     ones = hot(iota((HD, rows), 0) == 0)
-    for lo in range(0, width, HD):
+
+    def scored(lo):
         at = slice(lo, lo + HD)
         scores = dot(q[at], keys[at], TN)
-        top = jnp.max(scores, axis=1, keepdims=True)
+        return scores, jnp.max(scores, axis=1, keepdims=True)
+
+    scores, top = scored(0)
+    for lo in range(0, width, HD):
+        later = scored(lo + HD) if lo + HD < width else (None, None)
+        at = slice(lo, lo + HD)
         expo = jnp.exp(scores - top).astype(BF16)
         res = dot(jnp.concatenate([vals[at], ones], axis=0), expo, NT)
         heads[at, :] = (res[0:HD] / res[HD : HD + 1]).astype(BF16)
+        scores, top = later
     first = (own + dot(weight(3), heads[...])).astype(BF16)
 
     target = digits[2:3] * TURN + digits[3:4]

time: 115 us -> 113 us (0.983)
  Pallas kernels: 26.8 us -> 24 us
  starting transfers between devices: 34.2 us -> 36.1 us
  waiting for transfers between devices: 31.5 us -> 29.6 us
    pallas_call x10, Pallas kernels: 26.8 us -> 24 us  [kernel_call(): return call(*operands)]
    all_to_all x1, waiting for transfers between devices: 13.5 us -> 11.5 us  [exchange(): lax.all_to_all(parts, 'range', split_axis=0, concat_axis=0, tiled=True)]
    ppermute x3, starting transfers between devices: 1.05 us -> 2.97 us  [shards(): far_w = [far0] + [lax.ppermute(w, 'range', swap) for w in near_w[1:]]]
  transfers between devices with their start and end apart: 17 -> 17, of which waited for: 8 -> 9; matrix products, arithmetic and copies ran while one was open for 0% -> 0% of each run, Pallas kernels for 14% -> 12%
where the time goes in v5:
time: 113 us; the launch traced here: 112 us
  starting transfers between devices  36.1 us (32%)
  waiting for transfers between devices  29.6 us (26%)
  Pallas kernels  24 us (21%)
  blocking collectives  18.8 us (17%)
  local copies, waits for them, and re-layouts  3.53 us (3%)
    pallas_call x10, Pallas kernels, kernel_call(): return call(*operands)  24 us
    all_to_all x1, blocking collectives, exchange(): lax.all_to_all(parts, 'range', split_axis=0, concat_axis=0, tiled=True)  18.8 us
    ppermute x9, waiting for transfers between devices, gather_chan(): return [x] + [lax.ppermute(x, 'chan', turn(k)) for k in range(1, CHAN)]  15.7 us
    all_to_all x1, starting transfers between devices, exchange(): lax.all_to_all(parts, 'range', split_axis=0, concat_axis=0, tiled=True)  14.3 us
    ppermute x9, starting transfers between devices, gather_chan(): return [x] + [lax.ppermute(x, 'chan', turn(k)) for k in range(1, CHAN)]  12.5 us
    all_to_all x1, waiting for transfers between devices, exchange(): lax.all_to_all(parts, 'range', split_axis=0, concat_axis=0, tiled=True)  11.5 us
    ppermute x1, starting transfers between devices, shards(): halo = lax.ppermute(third, ('range', 'chan'), pairs)  3.66 us
    unnamed x16, local copies, waits for them, and re-layouts  3.53 us
  transfers between devices with their start and end apart: 17, of which 9 were waited for; matrix products, arithmetic and copies ran while one was open for 0% of the time, Pallas kernels for 12%

profile of v5, /device:TPU:1, one launch (start us, length us, event | category | flops | bytes accessed | tf_op | source)
XLA Modules:
  0.0 112.3 jit_solution(4153460522293689309)
XLA Ops:
  0.0 1.7 %gather_features.1.refs_0_ = bf16[128,1024]{1,0:T(8,128)(2,1)} custom-call(bf16[64,1024]{1,0:T(8,128)(2,1)} %x_ref.1, bf16[192,256]{1,0:T(8,128)(2,1)} %bitcast.11, bf16[64,256]{1,0:T(8,128)(2,1)} %bitcast.12), custom_call_target="tpu_custom_call" | custom-call | flops 1048576 | bytes 1048576 | tf_op jit(solution)/shard_map/gather_features/pallas_call | solution.py:52
  1.8 2.0 %collective-permute-start = (bf16[128,1024]{1,0:T(8,128)(2,1)}, bf16[128,1024]{1,0:T(8,128)(2,1)S(1)}, u32[]{:S(2)}, u32[]{:S(2)}) collective-permute-start(bf16[128,1024]{1,0:T(8,128)(2,1)} %gather_features.1.refs_0_), channel_id=1, source_target_pairs={{0,1},{1,2},{2,3},{3,0},{4,5},{5,6},{6,7},{7,4},{8,9},{9,10},{10,1... | collective-permute-start | bytes 786440 | tf_op jit(solution)/shard_map/gather_features/ppermute | solution.py:349
  3.8 2.5 %collective-permute-start.1 = (bf16[128,1024]{1,0:T(8,128)(2,1)}, bf16[128,1024]{1,0:T(8,128)(2,1)S(1)}, u32[]{:S(2)}, u32[]{:S(2)}) collective-permute-start(bf16[128,1024]{1,0:T(8,128)(2,1)} %gather_features.1.refs_0_), channel_id=1, source_target_pairs={{0,2},{1,3},{2,0},{3,1},{4,6},{5,7},{6,4},{7,5},{8,10},{9,11},{10,... | collective-permute-start | bytes 786440 | tf_op jit(solution)/shard_map/gather_features/ppermute | solution.py:349
  6.2 1.2 %collective-permute-start.2 = (bf16[128,1024]{1,0:T(8,128)(2,1)}, bf16[128,1024]{1,0:T(8,128)(2,1)S(1)}, u32[]{:S(2)}, u32[]{:S(2)}) collective-permute-start(bf16[128,1024]{1,0:T(8,128)(2,1)} %gather_features.1.refs_0_), channel_id=1, source_target_pairs={{0,3},{1,0},{2,1},{3,2},{4,7},{5,4},{6,5},{7,6},{8,11},{9,8},{10,9... | collective-permute-start | bytes 786440 | tf_op jit(solution)/shard_map/gather_features/ppermute | solution.py:349
  8.9 1.2 %copy-done.1 = bf16[27,64,256]{2,1,0:T(8,128)(2,1)S(1)} copy-done((bf16[27,64,256]{2,1,0:T(8,128)(2,1)S(1)}, bf16[27,64,256]{2,1,0:T(8,128)(2,1)}, u32[]{:S(2)}) %copy-start.1) | copy-done | bytes 884760
  10.3 7.5 %collective-permute-done.1.refs_2_ = bf16[128,1024]{1,0:T(8,128)(2,1)S(1)} collective-permute-done((bf16[128,1024]{1,0:T(8,128)(2,1)}, bf16[128,1024]{1,0:T(8,128)(2,1)S(1)}, u32[]{:S(2)}, u32[]{:S(2)}) %collective-permute-start.1) | collective-permute-done | bytes 262176 | tf_op jit(solution)/shard_map/gather_features/ppermute | solution.py:349
  19.5 2.3 %collective-permute-start.5 = (bf16[2240,128]{1,0:T(8,128)(2,1)S(1)}, bf16[2240,128]{1,0:T(8,128)(2,1)S(1)}, u32[]{:S(2)}, u32[]{:S(2)}) collective-permute-start(bf16[2240,128]{1,0:T(8,128)(2,1)S(1)} %get-tuple-element.42.refs_0_), channel_id=1, source_target_pairs={{0,2},{1,3},{2,0},{3,1},{4,6},{5,7},{6,4},{7,5},{8,10},{9,11},{10,... | collective-permute-start | bytes 1720328 | tf_op jit(solution)/shard_map/gather_weights/ppermute | solution.py:349
  23.6 7.1 %attention.1 = bf16[64,24,128]{2,1,0:T(8,128)(2,1)} custom-call(s32[1]{0:T(128)} %bitcast.me_ref, s32[1]{0:T(128)} %bitcast.2.range_ref, bf16[128,1024]{1,0:T(8,128)(2,1)S(1)} %copy-done.2, bf16[128,1024]{1,0:T(8,128)(2,1)S(1)} %collective-permute-done.refs_1_, bf16[128,1024]{1,0:T(8,128)(2,1)S(1)} %collective-permute-done.1.refs_2_, ...), custom_call_target="tpu_custom_call" | custom-call | flops 4294967296 | bytes 1048576 | tf_op jit(solution)/shard_map/attention/pallas_call | solution.py:52
  30.7 14.3 %all-to-all-start = ((bf16[64,24,128]{2,1,0:T(8,128)(2,1)}), bf16[64,24,128]{2,1,0:T(8,128)(2,1)S(1)}, u32[]{:S(2)}, u32[]{:S(2)}) async-start(bf16[64,24,128]{2,1,0:T(8,128)(2,1)} %attention.1), calls=%async_computation | async-start | bytes 786432 | tf_op jit(solution)/shard_map/exchange/all_to_all | solution.py:353
  45.9 2.1 %collective-permute-start.6 = (bf16[2240,128]{1,0:T(8,128)(2,1)S(1)}, bf16[2240,128]{1,0:T(8,128)(2,1)}, u32[]{:S(2)}, u32[]{:S(2)}) collective-permute-start(bf16[2240,128]{1,0:T(8,128)(2,1)S(1)} %collective-permute-done.5.refs_2_), channel_id=1, source_target_pairs={{0,4},{4,0},{8,12},{12,8},{16,20},{20,16},{24,28},{28,24},{32,36},... | collective-permute-start | bytes 1720328 | tf_op jit(solution)/shard_map/gather_weights/ppermute | solution.py:397
  48.1 11.5 %all-to-all-done.got_ref = bf16[64,24,128]{2,1,0:T(8,128)(2,1)S(1)} async-done(((bf16[64,24,128]{2,1,0:T(8,128)(2,1)}), bf16[64,24,128]{2,1,0:T(8,128)(2,1)S(1)}, u32[]{:S(2)}, u32[]{:S(2)}) %all-to-all-start) | async-done | bytes 393248 | tf_op jit(solution)/shard_map/exchange/all_to_all | solution.py:353
  60.8 2.0 %collective-permute-start.11 = (bf16[320,256]{1,0:T(8,128)(2,1)S(1)}, bf16[320,256]{1,0:T(8,128)(2,1)S(1)}, u32[]{:S(2)}, u32[]{:S(2)}) collective-permute-start(bf16[320,256]{1,0:T(8,128)(2,1)S(1)} %compact.1.c0), channel_id=1, source_target_pairs={{0,3},{1,0},{2,1},{3,2},{4,7},{5,4},{6,5},{7,6},{8,11},{9,8},{10,9... | collective-permute-start | bytes 491528 | tf_op jit(solution)/shard_map/compact/ppermute | solution.py:349
  62.8 4.3 %collective-permute-done.10.c2 = bf16[320,256]{1,0:T(8,128)(2,1)S(1)} collective-permute-done((bf16[320,256]{1,0:T(8,128)(2,1)S(1)}, bf16[320,256]{1,0:T(8,128)(2,1)S(1)}, u32[]{:S(2)}, u32[]{:S(2)}) %collective-permute-start.10) | collective-permute-done | bytes 163872 | tf_op jit(solution)/shard_map/compact/ppermute | solution.py:349
  67.1 1.0 collective-permute-done.11.c3
  68.0 2.8 %collective-permute-done.9.c1 = bf16[320,256]{1,0:T(8,128)(2,1)S(1)} collective-permute-done((bf16[320,256]{1,0:T(8,128)(2,1)S(1)}, bf16[320,256]{1,0:T(8,128)(2,1)S(1)}, u32[]{:S(2)}, u32[]{:S(2)}) %collective-permute-start.9) | collective-permute-done | bytes 163872 | tf_op jit(solution)/shard_map/compact/ppermute | solution.py:349
  70.8 1.0 window.1
  71.9 3.7 %collective-permute-start.12 = (bf16[256,256]{1,0:T(8,128)(2,1)S(1)}, bf16[256,256]{1,0:T(8,128)(2,1)S(1)}, u32[]{:S(2)}, u32[]{:S(2)}) collective-permute-start(bf16[256,256]{1,0:T(8,128)(2,1)S(1)} %get-tuple-element.57.third_ref), channel_id=1, source_target_pairs={{0,4},{4,8},{8,12},{12,16},{16,20},{20,24},{24,28},{28,32},{32,36}... | collective-permute-start | bytes 393224 | tf_op jit(solution)/shard_map/window/ppermute | solution.py:429
  75.5 4.9 %conv.2.acc_ref = f32[256,256]{1,0:T(8,128)S(1)} custom-call(s32[1]{0:T(128)} %bitcast.me_ref, s32[1]{0:T(128)} %bitcast.1.core_ref, bf16[512,256]{1,0:T(8,128)(2,1)S(1)} %get-tuple-element.52.win_ref, s32[27,256]{1,0:T(8,128)S(1)} %constant_dynamic-slice_fusion.near_ref, bf16[2240,128]{1,0:T(8,128)(2,1)S(1)} %get-tuple-element.42.refs_0_, ...), custom_call_target="tpu_custom_call" | custom-call | flops 4294967296 | bytes 1048576 | tf_op jit(solution)/shard_map/conv/pallas_call | solution.py:52
  80.4 4.6 %conv.3 = (bf16[64,256]{1,0:T(8,128)(2,1)S(1)}, bf16[64,256]{1,0:T(8,128)(2,1)S(1)}, bf16[64,256]{1,0:T(8,128)(2,1)S(1)}, bf16[64,256]{1,0:T(8,128)(2,1)S(1)}) custom-call(s32[1]{0:T(128)} %bitcast.me_ref, s32[1]{0:T(128)} %bitcast.1.core_ref, f32[256,256]{1,0:T(8,128)S(1)} %conv.2.acc_ref, bf16[256,256]{1,0:T(8,128)(2,1)S(1)} %collective-permute-done.12.halo_ref, ...), custom_call_target="tpu_custom_call" | custom-call | flops 4294967296 | bytes 1048576 | tf_op jit(solution)/shard_map/conv/pallas_call | solution.py:52
  85.8 2.0 %collective-permute-start.15 = (bf16[64,256]{1,0:T(8,128)(2,1)S(1)}, bf16[64,256]{1,0:T(8,128)(2,1)S(1)}, u32[]{:S(2)}, u32[]{:S(2)}) collective-permute-start(bf16[64,256]{1,0:T(8,128)(2,1)S(1)} %get-tuple-element.61), channel_id=1, source_target_pairs={{0,3},{1,0},{2,1},{3,2},{4,7},{5,4},{6,5},{7,6},{8,11},{9,8},{10,9... | collective-permute-start | bytes 98312 | tf_op jit(solution)/shard_map/turn_back/ppermute | solution.py:448
  87.8 1.3 %collective-permute-done.13.t1 = bf16[64,256]{1,0:T(8,128)(2,1)S(1)} collective-permute-done((bf16[64,256]{1,0:T(8,128)(2,1)S(1)}, bf16[64,256]{1,0:T(8,128)(2,1)S(1)}, u32[]{:S(2)}, u32[]{:S(2)}) %collective-permute-start.13) | collective-permute-done | bytes 32800 | tf_op jit(solution)/shard_map/turn_back/ppermute | solution.py:448
  90.3 1.6 %back.1 = bf16[64,16,128]{2,1,0:T(8,128)(2,1)S(1)} custom-call(s32[1]{0:T(128)} %bitcast.me_ref, bf16[64,256]{1,0:T(8,128)(2,1)S(1)} %get-tuple-element.58.t0, bf16[64,256]{1,0:T(8,128)(2,1)S(1)} %collective-permute-done.13.t1, bf16[64,256]{1,0:T(8,128)(2,1)S(1)} %collective-permute-done.14.t2, bf16[64,256]{1,0:T(8,128)(2,1)S(1)} %collective-permute-done.15.t3, ...), custom_call_target="tpu_custom_call" | custom-call | flops 1073741824 | bytes 1048576 | tf_op jit(solution)/shard_map/back/pallas_call | solution.py:52
  91.8 18.8 %all_to_all.10.got_ref = bf16[64,16,128]{2,1,0:T(8,128)(2,1)S(1)} all-to-all(bf16[64,16,128]{2,1,0:T(8,128)(2,1)S(1)} %back.1), channel_id=1, replica_groups=mesh['range'=64,'chan'=4] {'range'}, dimensions={0} | all-to-all | bytes 524288 | tf_op jit(solution)/shard_map/back/all_to_all | solution.py:353
  110.6 1.7 %restore.1 = bf16[64,1024]{1,0:T(8,128)(2,1)} custom-call(bf16[64,16,128]{2,1,0:T(8,128)(2,1)S(1)} %all_to_all.10.got_ref, s32[8,1024]{1,0:T(8,128)S(1)} %codes.1.refs_4_.codes_ref), custom_call_target="tpu_custom_call" | custom-call | flops 1073741824 | bytes 1048576 | tf_op jit(solution)/shard_map/restore/pallas_call | solution.py:52
  (38 shorter events, 9.2 us)
Async XLA Ops:
  0.0 62.7 %copy-start = (s32[27,1024]{1,0:T(8,128)S(1)}, s32[27,1024]{1,0:T(8,128)}, u32[]{:S(2)}) copy-start(s32[27,1024]{1,0:T(8,128)} %param.10) | copy-start | bytes 331780
  0.0 8.8 %copy-start.3 = (bf16[256,256]{1,0:T(8,128)(2,1)S(1)}, bf16[256,256]{1,0:T(8,128)(2,1)}, u32[]{:S(2)}) copy-start(bf16[256,256]{1,0:T(8,128)(2,1)} %up_ref.1) | copy-start | bytes 393220
  0.0 8.8 %copy-start.4 = (bf16[256,256]{1,0:T(8,128)(2,1)S(1)}, bf16[256,256]{1,0:T(8,128)(2,1)}, u32[]{:S(2)}) copy-start(bf16[256,256]{1,0:T(8,128)(2,1)} %down_ref.1) | copy-start | bytes 393220
  1.8 8.5 %collective-permute-start = (bf16[128,1024]{1,0:T(8,128)(2,1)}, bf16[128,1024]{1,0:T(8,128)(2,1)S(1)}, u32[]{:S(2)}, u32[]{:S(2)}) collective-permute-start(bf16[128,1024]{1,0:T(8,128)(2,1)} %gather_features.1.refs_0_), channel_id=1, source_target_pairs={{0,1},{1,2},{2,3},{3,0},{4,5},{5,6},{6,7},{7,4},{8,9},{9,10},{10,1... | collective-permute-start | bytes 786440 | tf_op jit(solution)/shard_map/gather_features/ppermute | solution.py:349
  3.8 14.0 %collective-permute-start.1 = (bf16[128,1024]{1,0:T(8,128)(2,1)}, bf16[128,1024]{1,0:T(8,128)(2,1)S(1)}, u32[]{:S(2)}, u32[]{:S(2)}) collective-permute-start(bf16[128,1024]{1,0:T(8,128)(2,1)} %gather_features.1.refs_0_), channel_id=1, source_target_pairs={{0,2},{1,3},{2,0},{3,1},{4,6},{5,7},{6,4},{7,5},{8,10},{9,11},{10,... | collective-permute-start | bytes 786440 | tf_op jit(solution)/shard_map/gather_features/ppermute | solution.py:349
  6.2 11.5 %collective-permute-start.2 = (bf16[128,1024]{1,0:T(8,128)(2,1)}, bf16[128,1024]{1,0:T(8,128)(2,1)S(1)}, u32[]{:S(2)}, u32[]{:S(2)}) collective-permute-start(bf16[128,1024]{1,0:T(8,128)(2,1)} %gather_features.1.refs_0_), channel_id=1, source_target_pairs={{0,3},{1,0},{2,1},{3,2},{4,7},{5,4},{6,5},{7,6},{8,11},{9,8},{10,9... | collective-permute-start | bytes 786440 | tf_op jit(solution)/shard_map/gather_features/ppermute | solution.py:349
  8.9 1.2 %copy-start.1 = (bf16[27,64,256]{2,1,0:T(8,128)(2,1)S(1)}, bf16[27,64,256]{2,1,0:T(8,128)(2,1)}, u32[]{:S(2)}) copy-start(bf16[27,64,256]{2,1,0:T(8,128)(2,1)} %param.13) | copy-start | bytes 2654212
  10.0 12.7 %copy-start.2 = (bf16[128,1024]{1,0:T(8,128)(2,1)S(1)}, bf16[128,1024]{1,0:T(8,128)(2,1)}, u32[]{:S(2)}) copy-start(bf16[128,1024]{1,0:T(8,128)(2,1)} %gather_features.1.refs_0_) | copy-start | bytes 786436
  17.8 0.7 copy-start.6
  18.5 26.5 %collective-permute-start.3 = (bf16[2240,128]{1,0:T(8,128)(2,1)S(1)}, bf16[2240,128]{1,0:T(8,128)(2,1)S(1)}, u32[]{:S(2)}, u32[]{:S(2)}) collective-permute-start(bf16[2240,128]{1,0:T(8,128)(2,1)S(1)} %get-tuple-element.42.refs_0_), channel_id=1, source_target_pairs={{0,1},{1,2},{2,3},{3,0},{4,5},{5,6},{6,7},{7,4},{8,9},{9,10},{10,1... | collective-permute-start | bytes 1720328 | tf_op jit(solution)/shard_map/gather_weights/ppermute | solution.py:349
  19.5 26.4 %collective-permute-start.5 = (bf16[2240,128]{1,0:T(8,128)(2,1)S(1)}, bf16[2240,128]{1,0:T(8,128)(2,1)S(1)}, u32[]{:S(2)}, u32[]{:S(2)}) collective-permute-start(bf16[2240,128]{1,0:T(8,128)(2,1)S(1)} %get-tuple-element.42.refs_0_), channel_id=1, source_target_pairs={{0,2},{1,3},{2,0},{3,1},{4,6},{5,7},{6,4},{7,5},{8,10},{9,11},{10,... | collective-permute-start | bytes 1720328 | tf_op jit(solution)/shard_map/gather_weights/ppermute | solution.py:349
  21.8 26.2 %collective-permute-start.7 = (bf16[2240,128]{1,0:T(8,128)(2,1)S(1)}, bf16[2240,128]{1,0:T(8,128)(2,1)}, u32[]{:S(2)}, u32[]{:S(2)}) collective-permute-start(bf16[2240,128]{1,0:T(8,128)(2,1)S(1)} %get-tuple-element.42.refs_0_), channel_id=1, source_target_pairs={{0,3},{1,0},{2,1},{3,2},{4,7},{5,4},{6,5},{7,6},{8,11},{9,8},{10,9... | collective-permute-start | bytes 1720328 | tf_op jit(solution)/shard_map/gather_weights/ppermute | solution.py:349
  22.7 1.0 copy-start.7
  30.7 28.9 %all-to-all-start = ((bf16[64,24,128]{2,1,0:T(8,128)(2,1)}), bf16[64,24,128]{2,1,0:T(8,128)(2,1)S(1)}, u32[]{:S(2)}, u32[]{:S(2)}) async-start(bf16[64,24,128]{2,1,0:T(8,128)(2,1)} %attention.1), calls=%async_computation | async-start | bytes 786432 | tf_op jit(solution)/shard_map/exchange/all_to_all | solution.py:353
  45.0 14.6 %collective-permute-start.4 = (bf16[2240,128]{1,0:T(8,128)(2,1)S(1)}, bf16[2240,128]{1,0:T(8,128)(2,1)}, u32[]{:S(2)}, u32[]{:S(2)}) collective-permute-start(bf16[2240,128]{1,0:T(8,128)(2,1)S(1)} %collective-permute-done.3.refs_1_), channel_id=1, source_target_pairs={{0,4},{4,0},{8,12},{12,8},{16,20},{20,16},{24,28},{28,24},{32,36},... | collective-permute-start | bytes 1720328 | tf_op jit(solution)/shard_map/gather_weights/ppermute | solution.py:397
  45.9 13.8 %collective-permute-start.6 = (bf16[2240,128]{1,0:T(8,128)(2,1)S(1)}, bf16[2240,128]{1,0:T(8,128)(2,1)}, u32[]{:S(2)}, u32[]{:S(2)}) collective-permute-start(bf16[2240,128]{1,0:T(8,128)(2,1)S(1)} %collective-permute-done.5.refs_2_), channel_id=1, source_target_pairs={{0,4},{4,0},{8,12},{12,8},{16,20},{20,16},{24,28},{28,24},{32,36},... | collective-permute-start | bytes 1720328 | tf_op jit(solution)/shard_map/gather_weights/ppermute | solution.py:397
  48.0 11.6 %collective-permute-start.8 = (bf16[2240,128]{1,0:T(8,128)(2,1)}, bf16[2240,128]{1,0:T(8,128)(2,1)}, u32[]{:S(2)}, u32[]{:S(2)}) collective-permute-start(bf16[2240,128]{1,0:T(8,128)(2,1)} %collective-permute-done.7.refs_3_), channel_id=1, source_target_pairs={{0,4},{4,0},{8,12},{12,8},{16,20},{20,16},{24,28},{28,24},{32,36},... | collective-permute-start | bytes 1720328 | tf_op jit(solution)/shard_map/gather_weights/ppermute | solution.py:397
  60.1 6.9 %collective-permute-start.10 = (bf16[320,256]{1,0:T(8,128)(2,1)S(1)}, bf16[320,256]{1,0:T(8,128)(2,1)S(1)}, u32[]{:S(2)}, u32[]{:S(2)}) collective-permute-start(bf16[320,256]{1,0:T(8,128)(2,1)S(1)} %compact.1.c0), channel_id=1, source_target_pairs={{0,2},{1,3},{2,0},{3,1},{4,6},{5,7},{6,4},{7,5},{8,10},{9,11},{10,... | collective-permute-start | bytes 491528 | tf_op jit(solution)/shard_map/compact/ppermute | solution.py:349
  60.8 7.3 %collective-permute-start.11 = (bf16[320,256]{1,0:T(8,128)(2,1)S(1)}, bf16[320,256]{1,0:T(8,128)(2,1)S(1)}, u32[]{:S(2)}, u32[]{:S(2)}) collective-permute-start(bf16[320,256]{1,0:T(8,128)(2,1)S(1)} %compact.1.c0), channel_id=1, source_target_pairs={{0,3},{1,0},{2,1},{3,2},{4,7},{5,4},{6,5},{7,6},{8,11},{9,8},{10,9... | collective-permute-start | bytes 491528 | tf_op jit(solution)/shard_map/compact/ppermute | solution.py:349
  62.7 8.1 %collective-permute-start.9 = (bf16[320,256]{1,0:T(8,128)(2,1)S(1)}, bf16[320,256]{1,0:T(8,128)(2,1)S(1)}, u32[]{:S(2)}, u32[]{:S(2)}) collective-permute-start(bf16[320,256]{1,0:T(8,128)(2,1)S(1)} %compact.1.c0), channel_id=1, source_target_pairs={{0,1},{1,2},{2,3},{3,0},{4,5},{5,6},{6,7},{7,4},{8,9},{9,10},{10,1... | collective-permute-start | bytes 491528 | tf_op jit(solution)/shard_map/compact/ppermute | solution.py:349
  71.9 8.5 %collective-permute-start.12 = (bf16[256,256]{1,0:T(8,128)(2,1)S(1)}, bf16[256,256]{1,0:T(8,128)(2,1)S(1)}, u32[]{:S(2)}, u32[]{:S(2)}) collective-permute-start(bf16[256,256]{1,0:T(8,128)(2,1)S(1)} %get-tuple-element.57.third_ref), channel_id=1, source_target_pairs={{0,4},{4,8},{8,12},{12,16},{16,20},{20,24},{24,28},{28,32},{32,36}... | collective-permute-start | bytes 393224 | tf_op jit(solution)/shard_map/window/ppermute | solution.py:429
  85.1 4.1 %collective-permute-start.13 = (bf16[64,256]{1,0:T(8,128)(2,1)S(1)}, bf16[64,256]{1,0:T(8,128)(2,1)S(1)}, u32[]{:S(2)}, u32[]{:S(2)}) collective-permute-start(bf16[64,256]{1,0:T(8,128)(2,1)S(1)} %get-tuple-element.59), channel_id=1, source_target_pairs={{0,1},{1,2},{2,3},{3,0},{4,5},{5,6},{6,7},{7,4},{8,9},{9,10},{10,1... | collective-permute-start | bytes 98312 | tf_op jit(solution)/shard_map/turn_back/ppermute | solution.py:448
  85.2 4.4 %collective-permute-start.14 = (bf16[64,256]{1,0:T(8,128)(2,1)S(1)}, bf16[64,256]{1,0:T(8,128)(2,1)S(1)}, u32[]{:S(2)}, u32[]{:S(2)}) collective-permute-start(bf16[64,256]{1,0:T(8,128)(2,1)S(1)} %get-tuple-element.60), channel_id=1, source_target_pairs={{0,2},{1,3},{2,0},{3,1},{4,6},{5,7},{6,4},{7,5},{8,10},{9,11},{10,... | collective-permute-start | bytes 98312 | tf_op jit(solution)/shard_map/turn_back/ppermute | solution.py:448
  85.8 4.4 %collective-permute-start.15 = (bf16[64,256]{1,0:T(8,128)(2,1)S(1)}, bf16[64,256]{1,0:T(8,128)(2,1)S(1)}, u32[]{:S(2)}, u32[]{:S(2)}) collective-permute-start(bf16[64,256]{1,0:T(8,128)(2,1)S(1)} %get-tuple-element.61), channel_id=1, source_target_pairs={{0,3},{1,0},{2,1},{3,2},{4,7},{5,4},{6,5},{7,6},{8,11},{9,8},{10,9... | collective-permute-start | bytes 98312 | tf_op jit(solution)/shard_map/turn_back/ppermute | solution.py:448
  (1 other events, 0.7 us)

commit v6 on v5

--- a/solution.py
+++ b/solution.py
@@ -310,23 +310,12 @@
     for k, ref in enumerate((t0, t1, t2, t3)):
         tmp[sender(me, k)] = ref[...]
     third = jnp.concatenate([tmp[q] for q in range(CHAN)], axis=1)
-    zero = jnp.zeros_like(third)
-    low = jnp.concatenate([third, zero], axis=0)
-    high = jnp.concatenate([zero, third], axis=0)
-    column = place_ref[...].T
-    slots = column.shape[0]
-    block = 256
-    rank = iota((block, third.shape[1]), 1).astype(F32)
-    for start in range(0, slots, block):
-        res = []
-        for odd in range(2):
-            part = 0.0
-            for half, rhs in enumerate((low, high)):
-                i = 2 * half + odd
-                part += dot(hot(rank == column[start : start + block, i : i + 1]), rhs, NT)
-            res.append(part.reshape(block // TURN, TURN, 128))
-        owner = start // TURN
-        out_ref[owner : owner + block // TURN] = jnp.concatenate(res, axis=1).astype(BF16)
+    slots = place_ref.shape[1]
+    rank = iota((third.shape[1], slots), 0).astype(F32)
+    res = [dot(third, hot(rank == place_ref[i : i + 1, :])) for i in range(CHAN)]
+    res = [jnp.concatenate([res[i], res[i + 2]], axis=0).T for i in range(2)]
+    res = [x.reshape(slots // TURN, TURN, x.shape[1]) for x in res]
+    out_ref[...] = jnp.concatenate(res, axis=1).astype(BF16)
 
 
 def restore_body(got_ref, codes_ref, out_ref):
@@ -335,9 +324,8 @@
     code = codes_ref[0:1, :]
     res = 0.0
     for half in range(2):
-        for start in range(0, got.shape[1], 256):
-            match = hot(iota((256, rows), 0) + (start + half * rows) == code)
-            res += dot(got[half * width : (half + 1) * width, start : start + 256], match)
+        match = hot(iota((got.shape[1], rows), 0) + half * rows == code)
+        res += dot(got[half * width : (half + 1) * width], match)
     out_ref[...] = res.astype(BF16)
 
 

time: 113 us -> 112 us (level)
  no operation moved by 1% of the time
where the time goes in v6:
time: 112 us
  starting transfers between devices  36.1 us (32%)
  waiting for transfers between devices  29.6 us (26%)
  Pallas kernels  23.3 us (21%)
  blocking collectives  18.8 us (17%)
  local copies, waits for them, and re-layouts  3.53 us (3%)
    pallas_call x10, Pallas kernels, kernel_call(): return call(*operands)  23.3 us
    all_to_all x1, blocking collectives, exchange(): lax.all_to_all(parts, 'range', split_axis=0, concat_axis=0, tiled=True)  18.8 us
    ppermute x9, waiting for transfers between devices, gather_chan(): return [x] + [lax.ppermute(x, 'chan', turn(k)) for k in range(1, CHAN)]  15.7 us
    all_to_all x1, starting transfers between devices, exchange(): lax.all_to_all(parts, 'range', split_axis=0, concat_axis=0, tiled=True)  14.3 us
    ppermute x9, starting transfers between devices, gather_chan(): return [x] + [lax.ppermute(x, 'chan', turn(k)) for k in range(1, CHAN)]  12.5 us
    all_to_all x1, waiting for transfers between devices, exchange(): lax.all_to_all(parts, 'range', split_axis=0, concat_axis=0, tiled=True)  11.5 us
    ppermute x1, starting transfers between devices, shards(): halo = lax.ppermute(third, ('range', 'chan'), pairs)  3.66 us
    unnamed x16, local copies, waits for them, and re-layouts  3.53 us
  transfers between devices with their start and end apart: 17, of which 9 were waited for; matrix products, arithmetic and copies ran while one was open for 0% of the time, Pallas kernels for 12%

profile of v6, /device:TPU:1, one launch (start us, length us, event | category | flops | bytes accessed | tf_op | source)
XLA Modules:
  0.0 111.5 jit_solution(2466217636263407784)
XLA Ops:
  0.0 1.7 %gather_features.1.refs_0_ = bf16[128,1024]{1,0:T(8,128)(2,1)} custom-call(bf16[64,1024]{1,0:T(8,128)(2,1)} %x_ref.1, bf16[192,256]{1,0:T(8,128)(2,1)} %bitcast.11, bf16[64,256]{1,0:T(8,128)(2,1)} %bitcast.12), custom_call_target="tpu_custom_call" | custom-call | flops 1048576 | bytes 1048576 | tf_op jit(solution)/shard_map/gather_features/pallas_call | solution.py:52
  1.8 2.0 %collective-permute-start = (bf16[128,1024]{1,0:T(8,128)(2,1)}, bf16[128,1024]{1,0:T(8,128)(2,1)S(1)}, u32[]{:S(2)}, u32[]{:S(2)}) collective-permute-start(bf16[128,1024]{1,0:T(8,128)(2,1)} %gather_features.1.refs_0_), channel_id=1, source_target_pairs={{0,1},{1,2},{2,3},{3,0},{4,5},{5,6},{6,7},{7,4},{8,9},{9,10},{10,1... | collective-permute-start | bytes 786440 | tf_op jit(solution)/shard_map/gather_features/ppermute | solution.py:337
  3.8 2.5 %collective-permute-start.1 = (bf16[128,1024]{1,0:T(8,128)(2,1)}, bf16[128,1024]{1,0:T(8,128)(2,1)S(1)}, u32[]{:S(2)}, u32[]{:S(2)}) collective-permute-start(bf16[128,1024]{1,0:T(8,128)(2,1)} %gather_features.1.refs_0_), channel_id=1, source_target_pairs={{0,2},{1,3},{2,0},{3,1},{4,6},{5,7},{6,4},{7,5},{8,10},{9,11},{10,... | collective-permute-start | bytes 786440 | tf_op jit(solution)/shard_map/gather_features/ppermute | solution.py:337
  6.2 1.2 %collective-permute-start.2 = (bf16[128,1024]{1,0:T(8,128)(2,1)}, bf16[128,1024]{1,0:T(8,128)(2,1)S(1)}, u32[]{:S(2)}, u32[]{:S(2)}) collective-permute-start(bf16[128,1024]{1,0:T(8,128)(2,1)} %gather_features.1.refs_0_), channel_id=1, source_target_pairs={{0,3},{1,0},{2,1},{3,2},{4,7},{5,4},{6,5},{7,6},{8,11},{9,8},{10,9... | collective-permute-start | bytes 786440 | tf_op jit(solution)/shard_map/gather_features/ppermute | solution.py:337
  8.9 1.2 %copy-done.1 = bf16[27,64,256]{2,1,0:T(8,128)(2,1)S(1)} copy-done((bf16[27,64,256]{2,1,0:T(8,128)(2,1)S(1)}, bf16[27,64,256]{2,1,0:T(8,128)(2,1)}, u32[]{:S(2)}) %copy-start.1) | copy-done | bytes 884760
  10.3 7.5 %collective-permute-done.1.refs_2_ = bf16[128,1024]{1,0:T(8,128)(2,1)S(1)} collective-permute-done((bf16[128,1024]{1,0:T(8,128)(2,1)}, bf16[128,1024]{1,0:T(8,128)(2,1)S(1)}, u32[]{:S(2)}, u32[]{:S(2)}) %collective-permute-start.1) | collective-permute-done | bytes 262176 | tf_op jit(solution)/shard_map/gather_features/ppermute | solution.py:337
  18.5 1.0 collective-permute-start.3
  19.5 2.3 %collective-permute-start.5 = (bf16[2240,128]{1,0:T(8,128)(2,1)S(1)}, bf16[2240,128]{1,0:T(8,128)(2,1)S(1)}, u32[]{:S(2)}, u32[]{:S(2)}) collective-permute-start(bf16[2240,128]{1,0:T(8,128)(2,1)S(1)} %get-tuple-element.42.refs_0_), channel_id=1, source_target_pairs={{0,2},{1,3},{2,0},{3,1},{4,6},{5,7},{6,4},{7,5},{8,10},{9,11},{10,... | collective-permute-start | bytes 1720328 | tf_op jit(solution)/shard_map/gather_weights/ppermute | solution.py:337
  23.6 7.1 %attention.1 = bf16[64,24,128]{2,1,0:T(8,128)(2,1)} custom-call(s32[1]{0:T(128)} %bitcast.me_ref, s32[1]{0:T(128)} %bitcast.2.range_ref, bf16[128,1024]{1,0:T(8,128)(2,1)S(1)} %copy-done.2, bf16[128,1024]{1,0:T(8,128)(2,1)S(1)} %collective-permute-done.refs_1_, bf16[128,1024]{1,0:T(8,128)(2,1)S(1)} %collective-permute-done.1.refs_2_, ...), custom_call_target="tpu_custom_call" | custom-call | flops 4294967296 | bytes 1048576 | tf_op jit(solution)/shard_map/attention/pallas_call | solution.py:52
  30.7 14.3 %all-to-all-start = ((bf16[64,24,128]{2,1,0:T(8,128)(2,1)}), bf16[64,24,128]{2,1,0:T(8,128)(2,1)S(1)}, u32[]{:S(2)}, u32[]{:S(2)}) async-start(bf16[64,24,128]{2,1,0:T(8,128)(2,1)} %attention.1), calls=%async_computation | async-start | bytes 786432 | tf_op jit(solution)/shard_map/exchange/all_to_all | solution.py:341
  45.9 2.1 %collective-permute-start.6 = (bf16[2240,128]{1,0:T(8,128)(2,1)S(1)}, bf16[2240,128]{1,0:T(8,128)(2,1)}, u32[]{:S(2)}, u32[]{:S(2)}) collective-permute-start(bf16[2240,128]{1,0:T(8,128)(2,1)S(1)} %collective-permute-done.5.refs_2_), channel_id=1, source_target_pairs={{0,4},{4,0},{8,12},{12,8},{16,20},{20,16},{24,28},{28,24},{32,36},... | collective-permute-start | bytes 1720328 | tf_op jit(solution)/shard_map/gather_weights/ppermute | solution.py:385
  48.1 11.5 %all-to-all-done.got_ref = bf16[64,24,128]{2,1,0:T(8,128)(2,1)S(1)} async-done(((bf16[64,24,128]{2,1,0:T(8,128)(2,1)}), bf16[64,24,128]{2,1,0:T(8,128)(2,1)S(1)}, u32[]{:S(2)}, u32[]{:S(2)}) %all-to-all-start) | async-done | bytes 393248 | tf_op jit(solution)/shard_map/exchange/all_to_all | solution.py:341
  60.8 2.0 %collective-permute-start.11 = (bf16[320,256]{1,0:T(8,128)(2,1)S(1)}, bf16[320,256]{1,0:T(8,128)(2,1)S(1)}, u32[]{:S(2)}, u32[]{:S(2)}) collective-permute-start(bf16[320,256]{1,0:T(8,128)(2,1)S(1)} %compact.1.c0), channel_id=1, source_target_pairs={{0,3},{1,0},{2,1},{3,2},{4,7},{5,4},{6,5},{7,6},{8,11},{9,8},{10,9... | collective-permute-start | bytes 491528 | tf_op jit(solution)/shard_map/compact/ppermute | solution.py:337
  62.8 4.3 %collective-permute-done.10.c2 = bf16[320,256]{1,0:T(8,128)(2,1)S(1)} collective-permute-done((bf16[320,256]{1,0:T(8,128)(2,1)S(1)}, bf16[320,256]{1,0:T(8,128)(2,1)S(1)}, u32[]{:S(2)}, u32[]{:S(2)}) %collective-permute-start.10) | collective-permute-done | bytes 163872 | tf_op jit(solution)/shard_map/compact/ppermute | solution.py:337
  67.1 1.0 collective-permute-done.11.c3
  68.0 2.8 %collective-permute-done.9.c1 = bf16[320,256]{1,0:T(8,128)(2,1)S(1)} collective-permute-done((bf16[320,256]{1,0:T(8,128)(2,1)S(1)}, bf16[320,256]{1,0:T(8,128)(2,1)S(1)}, u32[]{:S(2)}, u32[]{:S(2)}) %collective-permute-start.9) | collective-permute-done | bytes 163872 | tf_op jit(solution)/shard_map/compact/ppermute | solution.py:337
  70.8 1.0 window.1
  71.9 3.7 %collective-permute-start.12 = (bf16[256,256]{1,0:T(8,128)(2,1)S(1)}, bf16[256,256]{1,0:T(8,128)(2,1)S(1)}, u32[]{:S(2)}, u32[]{:S(2)}) collective-permute-start(bf16[256,256]{1,0:T(8,128)(2,1)S(1)} %get-tuple-element.57.third_ref), channel_id=1, source_target_pairs={{0,4},{4,8},{8,12},{12,16},{16,20},{20,24},{24,28},{28,32},{32,36}... | collective-permute-start | bytes 393224 | tf_op jit(solution)/shard_map/window/ppermute | solution.py:417
  75.5 4.9 %conv.2.acc_ref = f32[256,256]{1,0:T(8,128)S(1)} custom-call(s32[1]{0:T(128)} %bitcast.me_ref, s32[1]{0:T(128)} %bitcast.1.core_ref, bf16[512,256]{1,0:T(8,128)(2,1)S(1)} %get-tuple-element.52.win_ref, s32[27,256]{1,0:T(8,128)S(1)} %constant_dynamic-slice_fusion.near_ref, bf16[2240,128]{1,0:T(8,128)(2,1)S(1)} %get-tuple-element.42.refs_0_, ...), custom_call_target="tpu_custom_call" | custom-call | flops 4294967296 | bytes 1048576 | tf_op jit(solution)/shard_map/conv/pallas_call | solution.py:52
  80.4 4.6 %conv.3 = (bf16[64,256]{1,0:T(8,128)(2,1)S(1)}, bf16[64,256]{1,0:T(8,128)(2,1)S(1)}, bf16[64,256]{1,0:T(8,128)(2,1)S(1)}, bf16[64,256]{1,0:T(8,128)(2,1)S(1)}) custom-call(s32[1]{0:T(128)} %bitcast.me_ref, s32[1]{0:T(128)} %bitcast.1.core_ref, f32[256,256]{1,0:T(8,128)S(1)} %conv.2.acc_ref, bf16[256,256]{1,0:T(8,128)(2,1)S(1)} %collective-permute-done.12.halo_ref, ...), custom_call_target="tpu_custom_call" | custom-call | flops 4294967296 | bytes 1048576 | tf_op jit(solution)/shard_map/conv/pallas_call | solution.py:52
  85.8 2.0 %collective-permute-start.15 = (bf16[64,256]{1,0:T(8,128)(2,1)S(1)}, bf16[64,256]{1,0:T(8,128)(2,1)S(1)}, u32[]{:S(2)}, u32[]{:S(2)}) collective-permute-start(bf16[64,256]{1,0:T(8,128)(2,1)S(1)} %get-tuple-element.61), channel_id=1, source_target_pairs={{0,3},{1,0},{2,1},{3,2},{4,7},{5,4},{6,5},{7,6},{8,11},{9,8},{10,9... | collective-permute-start | bytes 98312 | tf_op jit(solution)/shard_map/turn_back/ppermute | solution.py:436
  87.8 1.3 %collective-permute-done.13.t1 = bf16[64,256]{1,0:T(8,128)(2,1)S(1)} collective-permute-done((bf16[64,256]{1,0:T(8,128)(2,1)S(1)}, bf16[64,256]{1,0:T(8,128)(2,1)S(1)}, u32[]{:S(2)}, u32[]{:S(2)}) %collective-permute-start.13) | collective-permute-done | bytes 32800 | tf_op jit(solution)/shard_map/turn_back/ppermute | solution.py:436
  91.2 18.8 %all_to_all.10.got_ref = bf16[64,16,128]{2,1,0:T(8,128)(2,1)S(1)} all-to-all(bf16[64,16,128]{2,1,0:T(8,128)(2,1)S(1)} %back.1), channel_id=1, replica_groups=mesh['range'=64,'chan'=4] {'range'}, dimensions={0} | all-to-all | bytes 524288 | tf_op jit(solution)/shard_map/back/all_to_all | solution.py:341
  109.9 1.6 %restore.1 = bf16[64,1024]{1,0:T(8,128)(2,1)} custom-call(bf16[64,16,128]{2,1,0:T(8,128)(2,1)S(1)} %all_to_all.10.got_ref, s32[8,1024]{1,0:T(8,128)S(1)} %codes.1.refs_4_.codes_ref), custom_call_target="tpu_custom_call" | custom-call | flops 1073741824 | bytes 1048576 | tf_op jit(solution)/shard_map/restore/pallas_call | solution.py:52
  (38 shorter events, 9.2 us)
Async XLA Ops:
  0.0 62.7 %copy-start = (s32[27,1024]{1,0:T(8,128)S(1)}, s32[27,1024]{1,0:T(8,128)}, u32[]{:S(2)}) copy-start(s32[27,1024]{1,0:T(8,128)} %param.10) | copy-start | bytes 331780
  0.0 8.8 %copy-start.3 = (bf16[256,256]{1,0:T(8,128)(2,1)S(1)}, bf16[256,256]{1,0:T(8,128)(2,1)}, u32[]{:S(2)}) copy-start(bf16[256,256]{1,0:T(8,128)(2,1)} %up_ref.1) | copy-start | bytes 393220
  0.0 8.8 %copy-start.4 = (bf16[256,256]{1,0:T(8,128)(2,1)S(1)}, bf16[256,256]{1,0:T(8,128)(2,1)}, u32[]{:S(2)}) copy-start(bf16[256,256]{1,0:T(8,128)(2,1)} %down_ref.1) | copy-start | bytes 393220
  1.8 8.5 %collective-permute-start = (bf16[128,1024]{1,0:T(8,128)(2,1)}, bf16[128,1024]{1,0:T(8,128)(2,1)S(1)}, u32[]{:S(2)}, u32[]{:S(2)}) collective-permute-start(bf16[128,1024]{1,0:T(8,128)(2,1)} %gather_features.1.refs_0_), channel_id=1, source_target_pairs={{0,1},{1,2},{2,3},{3,0},{4,5},{5,6},{6,7},{7,4},{8,9},{9,10},{10,1... | collective-permute-start | bytes 786440 | tf_op jit(solution)/shard_map/gather_features/ppermute | solution.py:337
  3.8 14.0 %collective-permute-start.1 = (bf16[128,1024]{1,0:T(8,128)(2,1)}, bf16[128,1024]{1,0:T(8,128)(2,1)S(1)}, u32[]{:S(2)}, u32[]{:S(2)}) collective-permute-start(bf16[128,1024]{1,0:T(8,128)(2,1)} %gather_features.1.refs_0_), channel_id=1, source_target_pairs={{0,2},{1,3},{2,0},{3,1},{4,6},{5,7},{6,4},{7,5},{8,10},{9,11},{10,... | collective-permute-start | bytes 786440 | tf_op jit(solution)/shard_map/gather_features/ppermute | solution.py:337
  6.2 11.5 %collective-permute-start.2 = (bf16[128,1024]{1,0:T(8,128)(2,1)}, bf16[128,1024]{1,0:T(8,128)(2,1)S(1)}, u32[]{:S(2)}, u32[]{:S(2)}) collective-permute-start(bf16[128,1024]{1,0:T(8,128)(2,1)} %gather_features.1.refs_0_), channel_id=1, source_target_pairs={{0,3},{1,0},{2,1},{3,2},{4,7},{5,4},{6,5},{7,6},{8,11},{9,8},{10,9... | collective-permute-start | bytes 786440 | tf_op jit(solution)/shard_map/gather_features/ppermute | solution.py:337
  8.9 1.2 %copy-start.1 = (bf16[27,64,256]{2,1,0:T(8,128)(2,1)S(1)}, bf16[27,64,256]{2,1,0:T(8,128)(2,1)}, u32[]{:S(2)}) copy-start(bf16[27,64,256]{2,1,0:T(8,128)(2,1)} %param.13) | copy-start | bytes 2654212
  10.0 12.7 %copy-start.2 = (bf16[128,1024]{1,0:T(8,128)(2,1)S(1)}, bf16[128,1024]{1,0:T(8,128)(2,1)}, u32[]{:S(2)}) copy-start(bf16[128,1024]{1,0:T(8,128)(2,1)} %gather_features.1.refs_0_) | copy-start | bytes 786436
  17.8 0.7 copy-start.6
  18.5 26.5 %collective-permute-start.3 = (bf16[2240,128]{1,0:T(8,128)(2,1)S(1)}, bf16[2240,128]{1,0:T(8,128)(2,1)S(1)}, u32[]{:S(2)}, u32[]{:S(2)}) collective-permute-start(bf16[2240,128]{1,0:T(8,128)(2,1)S(1)} %get-tuple-element.42.refs_0_), channel_id=1, source_target_pairs={{0,1},{1,2},{2,3},{3,0},{4,5},{5,6},{6,7},{7,4},{8,9},{9,10},{10,1... | collective-permute-start | bytes 1720328 | tf_op jit(solution)/shard_map/gather_weights/ppermute | solution.py:337
  19.5 26.4 %collective-permute-start.5 = (bf16[2240,128]{1,0:T(8,128)(2,1)S(1)}, bf16[2240,128]{1,0:T(8,128)(2,1)S(1)}, u32[]{:S(2)}, u32[]{:S(2)}) collective-permute-start(bf16[2240,128]{1,0:T(8,128)(2,1)S(1)} %get-tuple-element.42.refs_0_), channel_id=1, source_target_pairs={{0,2},{1,3},{2,0},{3,1},{4,6},{5,7},{6,4},{7,5},{8,10},{9,11},{10,... | collective-permute-start | bytes 1720328 | tf_op jit(solution)/shard_map/gather_weights/ppermute | solution.py:337
  21.8 26.2 %collective-permute-start.7 = (bf16[2240,128]{1,0:T(8,128)(2,1)S(1)}, bf16[2240,128]{1,0:T(8,128)(2,1)}, u32[]{:S(2)}, u32[]{:S(2)}) collective-permute-start(bf16[2240,128]{1,0:T(8,128)(2,1)S(1)} %get-tuple-element.42.refs_0_), channel_id=1, source_target_pairs={{0,3},{1,0},{2,1},{3,2},{4,7},{5,4},{6,5},{7,6},{8,11},{9,8},{10,9... | collective-permute-start | bytes 1720328 | tf_op jit(solution)/shard_map/gather_weights/ppermute | solution.py:337
  22.7 1.0 copy-start.7
  30.7 28.9 %all-to-all-start = ((bf16[64,24,128]{2,1,0:T(8,128)(2,1)}), bf16[64,24,128]{2,1,0:T(8,128)(2,1)S(1)}, u32[]{:S(2)}, u32[]{:S(2)}) async-start(bf16[64,24,128]{2,1,0:T(8,128)(2,1)} %attention.1), calls=%async_computation | async-start | bytes 786432 | tf_op jit(solution)/shard_map/exchange/all_to_all | solution.py:341
  45.0 14.6 %collective-permute-start.4 = (bf16[2240,128]{1,0:T(8,128)(2,1)S(1)}, bf16[2240,128]{1,0:T(8,128)(2,1)}, u32[]{:S(2)}, u32[]{:S(2)}) collective-permute-start(bf16[2240,128]{1,0:T(8,128)(2,1)S(1)} %collective-permute-done.3.refs_1_), channel_id=1, source_target_pairs={{0,4},{4,0},{8,12},{12,8},{16,20},{20,16},{24,28},{28,24},{32,36},... | collective-permute-start | bytes 1720328 | tf_op jit(solution)/shard_map/gather_weights/ppermute | solution.py:385
  45.9 13.8 %collective-permute-start.6 = (bf16[2240,128]{1,0:T(8,128)(2,1)S(1)}, bf16[2240,128]{1,0:T(8,128)(2,1)}, u32[]{:S(2)}, u32[]{:S(2)}) collective-permute-start(bf16[2240,128]{1,0:T(8,128)(2,1)S(1)} %collective-permute-done.5.refs_2_), channel_id=1, source_target_pairs={{0,4},{4,0},{8,12},{12,8},{16,20},{20,16},{24,28},{28,24},{32,36},... | collective-permute-start | bytes 1720328 | tf_op jit(solution)/shard_map/gather_weights/ppermute | solution.py:385
  48.0 11.6 %collective-permute-start.8 = (bf16[2240,128]{1,0:T(8,128)(2,1)}, bf16[2240,128]{1,0:T(8,128)(2,1)}, u32[]{:S(2)}, u32[]{:S(2)}) collective-permute-start(bf16[2240,128]{1,0:T(8,128)(2,1)} %collective-permute-done.7.refs_3_), channel_id=1, source_target_pairs={{0,4},{4,0},{8,12},{12,8},{16,20},{20,16},{24,28},{28,24},{32,36},... | collective-permute-start | bytes 1720328 | tf_op jit(solution)/shard_map/gather_weights/ppermute | solution.py:385
  60.1 6.9 %collective-permute-start.10 = (bf16[320,256]{1,0:T(8,128)(2,1)S(1)}, bf16[320,256]{1,0:T(8,128)(2,1)S(1)}, u32[]{:S(2)}, u32[]{:S(2)}) collective-permute-start(bf16[320,256]{1,0:T(8,128)(2,1)S(1)} %compact.1.c0), channel_id=1, source_target_pairs={{0,2},{1,3},{2,0},{3,1},{4,6},{5,7},{6,4},{7,5},{8,10},{9,11},{10,... | collective-permute-start | bytes 491528 | tf_op jit(solution)/shard_map/compact/ppermute | solution.py:337
  60.8 7.3 %collective-permute-start.11 = (bf16[320,256]{1,0:T(8,128)(2,1)S(1)}, bf16[320,256]{1,0:T(8,128)(2,1)S(1)}, u32[]{:S(2)}, u32[]{:S(2)}) collective-permute-start(bf16[320,256]{1,0:T(8,128)(2,1)S(1)} %compact.1.c0), channel_id=1, source_target_pairs={{0,3},{1,0},{2,1},{3,2},{4,7},{5,4},{6,5},{7,6},{8,11},{9,8},{10,9... | collective-permute-start | bytes 491528 | tf_op jit(solution)/shard_map/compact/ppermute | solution.py:337
  62.7 8.1 %collective-permute-start.9 = (bf16[320,256]{1,0:T(8,128)(2,1)S(1)}, bf16[320,256]{1,0:T(8,128)(2,1)S(1)}, u32[]{:S(2)}, u32[]{:S(2)}) collective-permute-start(bf16[320,256]{1,0:T(8,128)(2,1)S(1)} %compact.1.c0), channel_id=1, source_target_pairs={{0,1},{1,2},{2,3},{3,0},{4,5},{5,6},{6,7},{7,4},{8,9},{9,10},{10,1... | collective-permute-start | bytes 491528 | tf_op jit(solution)/shard_map/compact/ppermute | solution.py:337
  71.9 8.5 %collective-permute-start.12 = (bf16[256,256]{1,0:T(8,128)(2,1)S(1)}, bf16[256,256]{1,0:T(8,128)(2,1)S(1)}, u32[]{:S(2)}, u32[]{:S(2)}) collective-permute-start(bf16[256,256]{1,0:T(8,128)(2,1)S(1)} %get-tuple-element.57.third_ref), channel_id=1, source_target_pairs={{0,4},{4,8},{8,12},{12,16},{16,20},{20,24},{24,28},{28,32},{32,36}... | collective-permute-start | bytes 393224 | tf_op jit(solution)/shard_map/window/ppermute | solution.py:417
  85.1 4.1 %collective-permute-start.13 = (bf16[64,256]{1,0:T(8,128)(2,1)S(1)}, bf16[64,256]{1,0:T(8,128)(2,1)S(1)}, u32[]{:S(2)}, u32[]{:S(2)}) collective-permute-start(bf16[64,256]{1,0:T(8,128)(2,1)S(1)} %get-tuple-element.59), channel_id=1, source_target_pairs={{0,1},{1,2},{2,3},{3,0},{4,5},{5,6},{6,7},{7,4},{8,9},{9,10},{10,1... | collective-permute-start | bytes 98312 | tf_op jit(solution)/shard_map/turn_back/ppermute | solution.py:436
  85.2 4.4 %collective-permute-start.14 = (bf16[64,256]{1,0:T(8,128)(2,1)S(1)}, bf16[64,256]{1,0:T(8,128)(2,1)S(1)}, u32[]{:S(2)}, u32[]{:S(2)}) collective-permute-start(bf16[64,256]{1,0:T(8,128)(2,1)S(1)} %get-tuple-element.60), channel_id=1, source_target_pairs={{0,2},{1,3},{2,0},{3,1},{4,6},{5,7},{6,4},{7,5},{8,10},{9,11},{10,... | collective-permute-start | bytes 98312 | tf_op jit(solution)/shard_map/turn_back/ppermute | solution.py:436
  85.8 4.4 %collective-permute-start.15 = (bf16[64,256]{1,0:T(8,128)(2,1)S(1)}, bf16[64,256]{1,0:T(8,128)(2,1)S(1)}, u32[]{:S(2)}, u32[]{:S(2)}) collective-permute-start(bf16[64,256]{1,0:T(8,128)(2,1)S(1)} %get-tuple-element.61), channel_id=1, source_target_pairs={{0,3},{1,0},{2,1},{3,2},{4,7},{5,4},{6,5},{7,6},{8,11},{9,8},{10,9... | collective-permute-start | bytes 98312 | tf_op jit(solution)/shard_map/turn_back/ppermute | solution.py:436
  (1 other events, 0.7 us)

commit v7 on v6

--- a/solution.py
+++ b/solution.py
@@ -380,7 +380,8 @@
             1 << 20,
             [core_ref, conv_weight.reshape(KER * quarter, whole), up_weight, down_weight],
         )
-        blocks, codes, near0, far0 = lax.optimization_barrier((blocks, codes, near0, far0))
+        early = (blocks[1], blocks[2], codes, near0, far0)
+        blocks[1], blocks[2], codes, near0, far0 = lax.optimization_barrier(early)
         near_w = gather_chan(near0)
         far_w = [far0] + [lax.ppermute(w, "range", swap) for w in near_w[1:]]
     with jax.named_scope("attention"):

time: 112 us -> 110 us (0.982)
  waiting for transfers between devices: 29.6 us -> 27.9 us
  local copies, waits for them, and re-layouts: 3.53 us -> 1.87 us
    all_to_all x1, waiting for transfers between devices: 11.5 us -> 9.67 us  [exchange(): lax.all_to_all(parts, 'range', split_axis=0, concat_axis=0, tiled=True)]
    unnamed x16 -> x12, local copies, waits for them, and re-layouts: 3.53 us -> 1.86 us
  transfers between devices with their start and end apart: 17 -> 17, of which waited for: 9 -> 8; matrix products, arithmetic and copies ran while one was open for 0% -> 0% of each run, Pallas kernels for 12% -> 13%
where the time goes in v7:
time: 110 us
  starting transfers between devices  36 us (33%)
  waiting for transfers between devices  27.9 us (25%)
  Pallas kernels  24.2 us (22%)
  blocking collectives  19.5 us (18%)
  local copies, waits for them, and re-layouts  1.87 us (2%)
    pallas_call x10, Pallas kernels, kernel_call(): return call(*operands)  24.2 us
    all_to_all x1, blocking collectives, exchange(): lax.all_to_all(parts, 'range', split_axis=0, concat_axis=0, tiled=True)  19.5 us
    ppermute x9, waiting for transfers between devices, gather_chan(): return [x] + [lax.ppermute(x, 'chan', turn(k)) for k in range(1, CHAN)]  15.9 us
    all_to_all x1, starting transfers between devices, exchange(): lax.all_to_all(parts, 'range', split_axis=0, concat_axis=0, tiled=True)  14 us
    ppermute x9, starting transfers between devices, gather_chan(): return [x] + [lax.ppermute(x, 'chan', turn(k)) for k in range(1, CHAN)]  12.3 us
    all_to_all x1, waiting for transfers between devices, exchange(): lax.all_to_all(parts, 'range', split_axis=0, concat_axis=0, tiled=True)  9.67 us
    ppermute x1, starting transfers between devices, shards(): halo = lax.ppermute(third, ('range', 'chan'), pairs)  3.8 us
    ppermute x3, starting transfers between devices, shards(): far_w = [far0] + [lax.ppermute(w, 'range', swap) for w in near_w[1:]]  3.19 us
  transfers between devices with their start and end apart: 17, of which 8 were waited for; matrix products, arithmetic and copies ran while one was open for 0% of the time, Pallas kernels for 13%

profile of v7, /device:TPU:1, one launch (start us, length us, event | category | flops | bytes accessed | tf_op | source)
XLA Modules:
  0.0 109.5 jit_solution(6021422656007779999)
XLA Ops:
  0.0 1.7 %gather_features.1.refs_0_ = bf16[128,1024]{1,0:T(8,128)(2,1)} custom-call(bf16[64,1024]{1,0:T(8,128)(2,1)} %x_ref.1, bf16[192,256]{1,0:T(8,128)(2,1)} %bitcast.11, bf16[64,256]{1,0:T(8,128)(2,1)} %bitcast.12), custom_call_target="tpu_custom_call" | custom-call | flops 1048576 | bytes 1048576 | tf_op jit(solution)/shard_map/gather_features/pallas_call | solution.py:52
  1.8 2.0 %collective-permute-start = (bf16[128,1024]{1,0:T(8,128)(2,1)}, bf16[128,1024]{1,0:T(8,128)(2,1)S(1)}, u32[]{:S(2)}, u32[]{:S(2)}) collective-permute-start(bf16[128,1024]{1,0:T(8,128)(2,1)} %gather_features.1.refs_0_), channel_id=1, source_target_pairs={{0,1},{1,2},{2,3},{3,0},{4,5},{5,6},{6,7},{7,4},{8,9},{9,10},{10,1... | collective-permute-start | bytes 786440 | tf_op jit(solution)/shard_map/gather_features/ppermute | solution.py:337
  3.8 2.5 %collective-permute-start.1 = (bf16[128,1024]{1,0:T(8,128)(2,1)}, bf16[128,1024]{1,0:T(8,128)(2,1)S(1)}, u32[]{:S(2)}, u32[]{:S(2)}) collective-permute-start(bf16[128,1024]{1,0:T(8,128)(2,1)} %gather_features.1.refs_0_), channel_id=1, source_target_pairs={{0,2},{1,3},{2,0},{3,1},{4,6},{5,7},{6,4},{7,5},{8,10},{9,11},{10,... | collective-permute-start | bytes 786440 | tf_op jit(solution)/shard_map/gather_features/ppermute | solution.py:337
  6.2 1.2 %collective-permute-start.2 = (bf16[128,1024]{1,0:T(8,128)(2,1)}, bf16[128,1024]{1,0:T(8,128)(2,1)}, u32[]{:S(2)}, u32[]{:S(2)}) collective-permute-start(bf16[128,1024]{1,0:T(8,128)(2,1)} %gather_features.1.refs_0_), channel_id=1, source_target_pairs={{0,3},{1,0},{2,1},{3,2},{4,7},{5,4},{6,5},{7,6},{8,11},{9,8},{10,9... | collective-permute-start | bytes 786440 | tf_op jit(solution)/shard_map/gather_features/ppermute | solution.py:337
  8.9 1.2 %copy-done.1 = bf16[27,64,256]{2,1,0:T(8,128)(2,1)S(1)} copy-done((bf16[27,64,256]{2,1,0:T(8,128)(2,1)S(1)}, bf16[27,64,256]{2,1,0:T(8,128)(2,1)}, u32[]{:S(2)}) %copy-start.1) | copy-done | bytes 884760
  10.3 7.5 %collective-permute-done.1.refs_2_ = bf16[128,1024]{1,0:T(8,128)(2,1)S(1)} collective-permute-done((bf16[128,1024]{1,0:T(8,128)(2,1)}, bf16[128,1024]{1,0:T(8,128)(2,1)S(1)}, u32[]{:S(2)}, u32[]{:S(2)}) %collective-permute-start.1) | collective-permute-done | bytes 262176 | tf_op jit(solution)/shard_map/gather_features/ppermute | solution.py:337
  18.0 2.4 %collective-permute-start.7 = (bf16[2240,128]{1,0:T(8,128)(2,1)S(1)}, bf16[2240,128]{1,0:T(8,128)(2,1)}, u32[]{:S(2)}, u32[]{:S(2)}) collective-permute-start(bf16[2240,128]{1,0:T(8,128)(2,1)S(1)} %get-tuple-element.38.refs_0_), channel_id=1, source_target_pairs={{0,3},{1,0},{2,1},{3,2},{4,7},{5,4},{6,5},{7,6},{8,11},{9,8},{10,9... | collective-permute-start | bytes 1720328 | tf_op jit(solution)/shard_map/gather_weights/ppermute | solution.py:337
  20.5 8.0 %attention.1 = bf16[64,24,128]{2,1,0:T(8,128)(2,1)} custom-call(s32[1]{0:T(128)} %bitcast.me_ref, s32[1]{0:T(128)} %bitcast.2.range_ref, bf16[128,1024]{1,0:T(8,128)(2,1)S(1)} %copy-done.2, bf16[128,1024]{1,0:T(8,128)(2,1)S(1)} %collective-permute-done.refs_1_, bf16[128,1024]{1,0:T(8,128)(2,1)S(1)} %collective-permute-done.1.refs_2_, ...), custom_call_target="tpu_custom_call" | custom-call | flops 4294967296 | bytes 1048576 | tf_op jit(solution)/shard_map/attention/pallas_call | solution.py:52
  28.5 14.0 %all-to-all-start = ((bf16[64,24,128]{2,1,0:T(8,128)(2,1)}), bf16[64,24,128]{2,1,0:T(8,128)(2,1)S(1)}, u32[]{:S(2)}, u32[]{:S(2)}) async-start(bf16[64,24,128]{2,1,0:T(8,128)(2,1)} %attention.1), calls=%async_computation | async-start | bytes 786432 | tf_op jit(solution)/shard_map/exchange/all_to_all | solution.py:341
  42.5 1.7 %collective-permute-done.3.refs_1_ = bf16[2240,128]{1,0:T(8,128)(2,1)S(1)} collective-permute-done((bf16[2240,128]{1,0:T(8,128)(2,1)S(1)}, bf16[2240,128]{1,0:T(8,128)(2,1)S(1)}, u32[]{:S(2)}, u32[]{:S(2)}) %collective-permute-start.3) | collective-permute-done | bytes 573472 | tf_op jit(solution)/shard_map/gather_weights/ppermute | solution.py:337
  44.2 2.5 %collective-permute-start.4 = (bf16[2240,128]{1,0:T(8,128)(2,1)S(1)}, bf16[2240,128]{1,0:T(8,128)(2,1)}, u32[]{:S(2)}, u32[]{:S(2)}) collective-permute-start(bf16[2240,128]{1,0:T(8,128)(2,1)S(1)} %collective-permute-done.3.refs_1_), channel_id=1, source_target_pairs={{0,4},{4,0},{8,12},{12,8},{16,20},{20,16},{24,28},{28,24},{32,36},... | collective-permute-start | bytes 1720328 | tf_op jit(solution)/shard_map/gather_weights/ppermute | solution.py:386
  47.4 9.7 %all-to-all-done.got_ref = bf16[64,24,128]{2,1,0:T(8,128)(2,1)S(1)} async-done(((bf16[64,24,128]{2,1,0:T(8,128)(2,1)}), bf16[64,24,128]{2,1,0:T(8,128)(2,1)S(1)}, u32[]{:S(2)}, u32[]{:S(2)}) %all-to-all-start) | async-done | bytes 393248 | tf_op jit(solution)/shard_map/exchange/all_to_all | solution.py:341
  57.5 2.5 %collective-permute-start.10 = (bf16[320,256]{1,0:T(8,128)(2,1)S(1)}, bf16[320,256]{1,0:T(8,128)(2,1)S(1)}, u32[]{:S(2)}, u32[]{:S(2)}) collective-permute-start(bf16[320,256]{1,0:T(8,128)(2,1)S(1)} %compact.1.c0), channel_id=1, source_target_pairs={{0,2},{1,3},{2,0},{3,1},{4,6},{5,7},{6,4},{7,5},{8,10},{9,11},{10,... | collective-permute-start | bytes 491528 | tf_op jit(solution)/shard_map/compact/ppermute | solution.py:337
  60.4 1.1 %collective-permute-start.9 = (bf16[320,256]{1,0:T(8,128)(2,1)S(1)}, bf16[320,256]{1,0:T(8,128)(2,1)S(1)}, u32[]{:S(2)}, u32[]{:S(2)}) collective-permute-start(bf16[320,256]{1,0:T(8,128)(2,1)S(1)} %compact.1.c0), channel_id=1, source_target_pairs={{0,1},{1,2},{2,3},{3,0},{4,5},{5,6},{6,7},{7,4},{8,9},{9,10},{10,1... | collective-permute-start | bytes 491528 | tf_op jit(solution)/shard_map/compact/ppermute | solution.py:337
  61.5 3.0 %collective-permute-done.10.c2 = bf16[320,256]{1,0:T(8,128)(2,1)S(1)} collective-permute-done((bf16[320,256]{1,0:T(8,128)(2,1)S(1)}, bf16[320,256]{1,0:T(8,128)(2,1)S(1)}, u32[]{:S(2)}, u32[]{:S(2)}) %collective-permute-start.10) | collective-permute-done | bytes 163872 | tf_op jit(solution)/shard_map/compact/ppermute | solution.py:337
  64.5 1.7 %collective-permute-done.11.c3 = bf16[320,256]{1,0:T(8,128)(2,1)S(1)} collective-permute-done((bf16[320,256]{1,0:T(8,128)(2,1)S(1)}, bf16[320,256]{1,0:T(8,128)(2,1)S(1)}, u32[]{:S(2)}, u32[]{:S(2)}) %collective-permute-start.11) | collective-permute-done | bytes 163872 | tf_op jit(solution)/shard_map/compact/ppermute | solution.py:337
  66.2 2.0 %collective-permute-done.9.c1 = bf16[320,256]{1,0:T(8,128)(2,1)S(1)} collective-permute-done((bf16[320,256]{1,0:T(8,128)(2,1)S(1)}, bf16[320,256]{1,0:T(8,128)(2,1)S(1)}, u32[]{:S(2)}, u32[]{:S(2)}) %collective-permute-start.9) | collective-permute-done | bytes 163872 | tf_op jit(solution)/shard_map/compact/ppermute | solution.py:337
  69.2 3.8 %collective-permute-start.12 = (bf16[256,256]{1,0:T(8,128)(2,1)S(1)}, bf16[256,256]{1,0:T(8,128)(2,1)S(1)}, u32[]{:S(2)}, u32[]{:S(2)}) collective-permute-start(bf16[256,256]{1,0:T(8,128)(2,1)S(1)} %get-tuple-element.53.third_ref), channel_id=1, source_target_pairs={{0,4},{4,8},{8,12},{12,16},{16,20},{20,24},{24,28},{28,32},{32,36}... | collective-permute-start | bytes 393224 | tf_op jit(solution)/shard_map/window/ppermute | solution.py:418
  73.0 4.9 %conv.2.acc_ref = f32[256,256]{1,0:T(8,128)S(1)} custom-call(s32[1]{0:T(128)} %bitcast.me_ref, s32[1]{0:T(128)} %bitcast.1.core_ref, bf16[512,256]{1,0:T(8,128)(2,1)S(1)} %get-tuple-element.48.win_ref, s32[27,256]{1,0:T(8,128)S(1)} %constant_dynamic-slice_fusion.near_ref, bf16[2240,128]{1,0:T(8,128)(2,1)S(1)} %get-tuple-element.38.refs_0_, ...), custom_call_target="tpu_custom_call" | custom-call | flops 4294967296 | bytes 1048576 | tf_op jit(solution)/shard_map/conv/pallas_call | solution.py:52
  77.9 4.6 %conv.3 = (bf16[64,256]{1,0:T(8,128)(2,1)S(1)}, bf16[64,256]{1,0:T(8,128)(2,1)S(1)}, bf16[64,256]{1,0:T(8,128)(2,1)S(1)}, bf16[64,256]{1,0:T(8,128)(2,1)S(1)}) custom-call(s32[1]{0:T(128)} %bitcast.me_ref, s32[1]{0:T(128)} %bitcast.1.core_ref, f32[256,256]{1,0:T(8,128)S(1)} %conv.2.acc_ref, bf16[256,256]{1,0:T(8,128)(2,1)S(1)} %collective-permute-done.12.halo_ref, ...), custom_call_target="tpu_custom_call" | custom-call | flops 4294967296 | bytes 1048576 | tf_op jit(solution)/shard_map/conv/pallas_call | solution.py:52
  83.3 2.0 %collective-permute-start.15 = (bf16[64,256]{1,0:T(8,128)(2,1)S(1)}, bf16[64,256]{1,0:T(8,128)(2,1)S(1)}, u32[]{:S(2)}, u32[]{:S(2)}) collective-permute-start(bf16[64,256]{1,0:T(8,128)(2,1)S(1)} %get-tuple-element.57), channel_id=1, source_target_pairs={{0,3},{1,0},{2,1},{3,2},{4,7},{5,4},{6,5},{7,6},{8,11},{9,8},{10,9... | collective-permute-start | bytes 98312 | tf_op jit(solution)/shard_map/turn_back/ppermute | solution.py:437
  85.3 1.9 %collective-permute-done.13.t1 = bf16[64,256]{1,0:T(8,128)(2,1)S(1)} collective-permute-done((bf16[64,256]{1,0:T(8,128)(2,1)S(1)}, bf16[64,256]{1,0:T(8,128)(2,1)S(1)}, u32[]{:S(2)}, u32[]{:S(2)}) %collective-permute-start.13) | collective-permute-done | bytes 32800 | tf_op jit(solution)/shard_map/turn_back/ppermute | solution.py:437
  88.5 19.5 %all_to_all.10.got_ref = bf16[64,16,128]{2,1,0:T(8,128)(2,1)S(1)} all-to-all(bf16[64,16,128]{2,1,0:T(8,128)(2,1)S(1)} %back.1), channel_id=1, replica_groups=mesh['range'=64,'chan'=4] {'range'}, dimensions={0} | all-to-all | bytes 524288 | tf_op jit(solution)/shard_map/back/all_to_all | solution.py:341
  108.0 1.6 %restore.1 = bf16[64,1024]{1,0:T(8,128)(2,1)} custom-call(bf16[64,16,128]{2,1,0:T(8,128)(2,1)S(1)} %all_to_all.10.got_ref, s32[8,1024]{1,0:T(8,128)S(1)} %codes.1.refs_4_.codes_ref), custom_call_target="tpu_custom_call" | custom-call | flops 1073741824 | bytes 1048576 | tf_op jit(solution)/shard_map/restore/pallas_call | solution.py:52
  (34 shorter events, 6.6 us)
Async XLA Ops:
  0.0 61.5 %copy-start = (s32[27,1024]{1,0:T(8,128)S(1)}, s32[27,1024]{1,0:T(8,128)}, u32[]{:S(2)}) copy-start(s32[27,1024]{1,0:T(8,128)} %param.10) | copy-start | bytes 331780
  0.0 8.8 %copy-start.3 = (bf16[256,256]{1,0:T(8,128)(2,1)S(1)}, bf16[256,256]{1,0:T(8,128)(2,1)}, u32[]{:S(2)}) copy-start(bf16[256,256]{1,0:T(8,128)(2,1)} %up_ref.1) | copy-start | bytes 393220
  0.0 8.8 %copy-start.4 = (bf16[256,256]{1,0:T(8,128)(2,1)S(1)}, bf16[256,256]{1,0:T(8,128)(2,1)}, u32[]{:S(2)}) copy-start(bf16[256,256]{1,0:T(8,128)(2,1)} %down_ref.1) | copy-start | bytes 393220
  1.8 8.5 %collective-permute-start = (bf16[128,1024]{1,0:T(8,128)(2,1)}, bf16[128,1024]{1,0:T(8,128)(2,1)S(1)}, u32[]{:S(2)}, u32[]{:S(2)}) collective-permute-start(bf16[128,1024]{1,0:T(8,128)(2,1)} %gather_features.1.refs_0_), channel_id=1, source_target_pairs={{0,1},{1,2},{2,3},{3,0},{4,5},{5,6},{6,7},{7,4},{8,9},{9,10},{10,1... | collective-permute-start | bytes 786440 | tf_op jit(solution)/shard_map/gather_features/ppermute | solution.py:337
  3.8 14.0 %collective-permute-start.1 = (bf16[128,1024]{1,0:T(8,128)(2,1)}, bf16[128,1024]{1,0:T(8,128)(2,1)S(1)}, u32[]{:S(2)}, u32[]{:S(2)}) collective-permute-start(bf16[128,1024]{1,0:T(8,128)(2,1)} %gather_features.1.refs_0_), channel_id=1, source_target_pairs={{0,2},{1,3},{2,0},{3,1},{4,6},{5,7},{6,4},{7,5},{8,10},{9,11},{10,... | collective-permute-start | bytes 786440 | tf_op jit(solution)/shard_map/gather_features/ppermute | solution.py:337
  6.2 14.2 %collective-permute-start.2 = (bf16[128,1024]{1,0:T(8,128)(2,1)}, bf16[128,1024]{1,0:T(8,128)(2,1)}, u32[]{:S(2)}, u32[]{:S(2)}) collective-permute-start(bf16[128,1024]{1,0:T(8,128)(2,1)} %gather_features.1.refs_0_), channel_id=1, source_target_pairs={{0,3},{1,0},{2,1},{3,2},{4,7},{5,4},{6,5},{7,6},{8,11},{9,8},{10,9... | collective-permute-start | bytes 786440 | tf_op jit(solution)/shard_map/gather_features/ppermute | solution.py:337
  7.4 0.7 copy-start.5
  8.9 1.2 %copy-start.1 = (bf16[27,64,256]{2,1,0:T(8,128)(2,1)S(1)}, bf16[27,64,256]{2,1,0:T(8,128)(2,1)}, u32[]{:S(2)}) copy-start(bf16[27,64,256]{2,1,0:T(8,128)(2,1)} %param.13) | copy-start | bytes 2654212
  10.0 10.4 %copy-start.2 = (bf16[128,1024]{1,0:T(8,128)(2,1)S(1)}, bf16[128,1024]{1,0:T(8,128)(2,1)}, u32[]{:S(2)}) copy-start(bf16[128,1024]{1,0:T(8,128)(2,1)} %gather_features.1.refs_0_) | copy-start | bytes 786436
  17.8 26.4 %collective-permute-start.3 = (bf16[2240,128]{1,0:T(8,128)(2,1)S(1)}, bf16[2240,128]{1,0:T(8,128)(2,1)S(1)}, u32[]{:S(2)}, u32[]{:S(2)}) collective-permute-start(bf16[2240,128]{1,0:T(8,128)(2,1)S(1)} %get-tuple-element.38.refs_0_), channel_id=1, source_target_pairs={{0,1},{1,2},{2,3},{3,0},{4,5},{5,6},{6,7},{7,4},{8,9},{9,10},{10,1... | collective-permute-start | bytes 1720328 | tf_op jit(solution)/shard_map/gather_weights/ppermute | solution.py:337
  17.8 28.9 %collective-permute-start.5 = (bf16[2240,128]{1,0:T(8,128)(2,1)S(1)}, bf16[2240,128]{1,0:T(8,128)(2,1)S(1)}, u32[]{:S(2)}, u32[]{:S(2)}) collective-permute-start(bf16[2240,128]{1,0:T(8,128)(2,1)S(1)} %get-tuple-element.38.refs_0_), channel_id=1, source_target_pairs={{0,2},{1,3},{2,0},{3,1},{4,6},{5,7},{6,4},{7,5},{8,10},{9,11},{10,... | collective-permute-start | bytes 1720328 | tf_op jit(solution)/shard_map/gather_weights/ppermute | solution.py:337
  18.0 28.7 %collective-permute-start.7 = (bf16[2240,128]{1,0:T(8,128)(2,1)S(1)}, bf16[2240,128]{1,0:T(8,128)(2,1)}, u32[]{:S(2)}, u32[]{:S(2)}) collective-permute-start(bf16[2240,128]{1,0:T(8,128)(2,1)S(1)} %get-tuple-element.38.refs_0_), channel_id=1, source_target_pairs={{0,3},{1,0},{2,1},{3,2},{4,7},{5,4},{6,5},{7,6},{8,11},{9,8},{10,9... | collective-permute-start | bytes 1720328 | tf_op jit(solution)/shard_map/gather_weights/ppermute | solution.py:337
  28.5 28.6 %all-to-all-start = ((bf16[64,24,128]{2,1,0:T(8,128)(2,1)}), bf16[64,24,128]{2,1,0:T(8,128)(2,1)S(1)}, u32[]{:S(2)}, u32[]{:S(2)}) async-start(bf16[64,24,128]{2,1,0:T(8,128)(2,1)} %attention.1), calls=%async_computation | async-start | bytes 786432 | tf_op jit(solution)/shard_map/exchange/all_to_all | solution.py:341
  44.2 12.9 %collective-permute-start.4 = (bf16[2240,128]{1,0:T(8,128)(2,1)S(1)}, bf16[2240,128]{1,0:T(8,128)(2,1)}, u32[]{:S(2)}, u32[]{:S(2)}) collective-permute-start(bf16[2240,128]{1,0:T(8,128)(2,1)S(1)} %collective-permute-done.3.refs_1_), channel_id=1, source_target_pairs={{0,4},{4,0},{8,12},{12,8},{16,20},{20,16},{24,28},{28,24},{32,36},... | collective-permute-start | bytes 1720328 | tf_op jit(solution)/shard_map/gather_weights/ppermute | solution.py:386
  46.7 10.4 %collective-permute-start.6 = (bf16[2240,128]{1,0:T(8,128)(2,1)S(1)}, bf16[2240,128]{1,0:T(8,128)(2,1)}, u32[]{:S(2)}, u32[]{:S(2)}) collective-permute-start(bf16[2240,128]{1,0:T(8,128)(2,1)S(1)} %collective-permute-done.5.refs_2_), channel_id=1, source_target_pairs={{0,4},{4,0},{8,12},{12,8},{16,20},{20,16},{24,28},{28,24},{32,36},... | collective-permute-start | bytes 1720328 | tf_op jit(solution)/shard_map/gather_weights/ppermute | solution.py:386
  46.7 10.4 %collective-permute-start.8 = (bf16[2240,128]{1,0:T(8,128)(2,1)}, bf16[2240,128]{1,0:T(8,128)(2,1)}, u32[]{:S(2)}, u32[]{:S(2)}) collective-permute-start(bf16[2240,128]{1,0:T(8,128)(2,1)} %collective-permute-done.7.refs_3_), channel_id=1, source_target_pairs={{0,4},{4,0},{8,12},{12,8},{16,20},{20,16},{24,28},{28,24},{32,36},... | collective-permute-start | bytes 1720328 | tf_op jit(solution)/shard_map/gather_weights/ppermute | solution.py:386
  57.5 6.9 %collective-permute-start.10 = (bf16[320,256]{1,0:T(8,128)(2,1)S(1)}, bf16[320,256]{1,0:T(8,128)(2,1)S(1)}, u32[]{:S(2)}, u32[]{:S(2)}) collective-permute-start(bf16[320,256]{1,0:T(8,128)(2,1)S(1)} %compact.1.c0), channel_id=1, source_target_pairs={{0,2},{1,3},{2,0},{3,1},{4,6},{5,7},{6,4},{7,5},{8,10},{9,11},{10,... | collective-permute-start | bytes 491528 | tf_op jit(solution)/shard_map/compact/ppermute | solution.py:337
  60.0 6.2 %collective-permute-start.11 = (bf16[320,256]{1,0:T(8,128)(2,1)S(1)}, bf16[320,256]{1,0:T(8,128)(2,1)S(1)}, u32[]{:S(2)}, u32[]{:S(2)}) collective-permute-start(bf16[320,256]{1,0:T(8,128)(2,1)S(1)} %compact.1.c0), channel_id=1, source_target_pairs={{0,3},{1,0},{2,1},{3,2},{4,7},{5,4},{6,5},{7,6},{8,11},{9,8},{10,9... | collective-permute-start | bytes 491528 | tf_op jit(solution)/shard_map/compact/ppermute | solution.py:337
  60.4 7.8 %collective-permute-start.9 = (bf16[320,256]{1,0:T(8,128)(2,1)S(1)}, bf16[320,256]{1,0:T(8,128)(2,1)S(1)}, u32[]{:S(2)}, u32[]{:S(2)}) collective-permute-start(bf16[320,256]{1,0:T(8,128)(2,1)S(1)} %compact.1.c0), channel_id=1, source_target_pairs={{0,1},{1,2},{2,3},{3,0},{4,5},{5,6},{6,7},{7,4},{8,9},{9,10},{10,1... | collective-permute-start | bytes 491528 | tf_op jit(solution)/shard_map/compact/ppermute | solution.py:337
  69.2 8.7 %collective-permute-start.12 = (bf16[256,256]{1,0:T(8,128)(2,1)S(1)}, bf16[256,256]{1,0:T(8,128)(2,1)S(1)}, u32[]{:S(2)}, u32[]{:S(2)}) collective-permute-start(bf16[256,256]{1,0:T(8,128)(2,1)S(1)} %get-tuple-element.53.third_ref), channel_id=1, source_target_pairs={{0,4},{4,8},{8,12},{12,16},{16,20},{20,24},{24,28},{28,32},{32,36}... | collective-permute-start | bytes 393224 | tf_op jit(solution)/shard_map/window/ppermute | solution.py:418
  82.6 4.7 %collective-permute-start.13 = (bf16[64,256]{1,0:T(8,128)(2,1)S(1)}, bf16[64,256]{1,0:T(8,128)(2,1)S(1)}, u32[]{:S(2)}, u32[]{:S(2)}) collective-permute-start(bf16[64,256]{1,0:T(8,128)(2,1)S(1)} %get-tuple-element.55), channel_id=1, source_target_pairs={{0,1},{1,2},{2,3},{3,0},{4,5},{5,6},{6,7},{7,4},{8,9},{9,10},{10,1... | collective-permute-start | bytes 98312 | tf_op jit(solution)/shard_map/turn_back/ppermute | solution.py:437
  82.6 4.6 %collective-permute-start.14 = (bf16[64,256]{1,0:T(8,128)(2,1)S(1)}, bf16[64,256]{1,0:T(8,128)(2,1)S(1)}, u32[]{:S(2)}, u32[]{:S(2)}) collective-permute-start(bf16[64,256]{1,0:T(8,128)(2,1)S(1)} %get-tuple-element.56), channel_id=1, source_target_pairs={{0,2},{1,3},{2,0},{3,1},{4,6},{5,7},{6,4},{7,5},{8,10},{9,11},{10,... | collective-permute-start | bytes 98312 | tf_op jit(solution)/shard_map/turn_back/ppermute | solution.py:437
  83.3 4.3 %collective-permute-start.15 = (bf16[64,256]{1,0:T(8,128)(2,1)S(1)}, bf16[64,256]{1,0:T(8,128)(2,1)S(1)}, u32[]{:S(2)}, u32[]{:S(2)}) collective-permute-start(bf16[64,256]{1,0:T(8,128)(2,1)S(1)} %get-tuple-element.57), channel_id=1, source_target_pairs={{0,3},{1,0},{2,1},{3,2},{4,7},{5,4},{6,5},{7,6},{8,11},{9,8},{10,9... | collective-permute-start | bytes 98312 | tf_op jit(solution)/shard_map/turn_back/ppermute | solution.py:437

commit v8 on v6

--- a/solution.py
+++ b/solution.py
@@ -380,7 +380,8 @@
             1 << 20,
             [core_ref, conv_weight.reshape(KER * quarter, whole), up_weight, down_weight],
         )
-        blocks, codes, near0, far0 = lax.optimization_barrier((blocks, codes, near0, far0))
+        early = (blocks[2], codes, near0, far0)
+        blocks[2], codes, near0, far0 = lax.optimization_barrier(early)
         near_w = gather_chan(near0)
         far_w = [far0] + [lax.ppermute(w, "range", swap) for w in near_w[1:]]
     with jax.named_scope("attention"):

time: 112 us -> 109 us (0.973)
  waiting for transfers between devices: 29.6 us -> 22.3 us
  starting transfers between devices: 36.1 us -> 39.4 us
  blocking collectives: 18.8 us -> 21 us
  local copies, waits for them, and re-layouts: 3.53 us -> 1.87 us
    ppermute x9, waiting for transfers between devices: 15.7 us -> 9.02 us  [gather_chan(): return [x] + [lax.ppermute(x, 'chan', turn(k)) for k in range(1, CHAN)]]
    ppermute x9, starting transfers between devices: 12.5 us -> 15.4 us  [gather_chan(): return [x] + [lax.ppermute(x, 'chan', turn(k)) for k in range(1, CHAN)]]
    all_to_all x1, blocking collectives: 18.8 us -> 21 us  [exchange(): lax.all_to_all(parts, 'range', split_axis=0, concat_axis=0, tiled=True)]
    unnamed x16 -> x12, local copies, waits for them, and re-layouts: 3.53 us -> 1.86 us
  transfers between devices with their start and end apart: 17 -> 17, of which waited for: 9 -> 10; matrix products, arithmetic and copies ran while one was open for 0% -> 0% of each run, Pallas kernels for 12% -> 13%
where the time goes in v8:
time: 109 us
  starting transfers between devices  39.4 us (36%)
  Pallas kernels  24.2 us (22%)
  waiting for transfers between devices  22.3 us (20%)
  blocking collectives  21 us (19%)
  local copies, waits for them, and re-layouts  1.87 us (2%)
    pallas_call x10, Pallas kernels, kernel_call(): return call(*operands)  24.2 us
    all_to_all x1, blocking collectives, exchange(): lax.all_to_all(parts, 'range', split_axis=0, concat_axis=0, tiled=True)  21 us
    ppermute x9, starting transfers between devices, gather_chan(): return [x] + [lax.ppermute(x, 'chan', turn(k)) for k in range(1, CHAN)]  15.4 us
    all_to_all x1, starting transfers between devices, exchange(): lax.all_to_all(parts, 'range', split_axis=0, concat_axis=0, tiled=True)  13.8 us
    all_to_all x1, waiting for transfers between devices, exchange(): lax.all_to_all(parts, 'range', split_axis=0, concat_axis=0, tiled=True)  10.8 us
    ppermute x9, waiting for transfers between devices, gather_chan(): return [x] + [lax.ppermute(x, 'chan', turn(k)) for k in range(1, CHAN)]  9.02 us
    ppermute x1, starting transfers between devices, shards(): halo = lax.ppermute(third, ('range', 'chan'), pairs)  4.2 us
    ppermute x3, starting transfers between devices, shards(): far_w = [far0] + [lax.ppermute(w, 'range', swap) for w in near_w[1:]]  3.23 us
  transfers between devices with their start and end apart: 17, of which 10 were waited for; matrix products, arithmetic and copies ran while one was open for 0% of the time, Pallas kernels for 13%

profile of v8, /device:TPU:1, one launch (start us, length us, event | category | flops | bytes accessed | tf_op | source)
XLA Modules:
  0.0 108.9 jit_solution(6588752381672637859)
XLA Ops:
  0.0 1.7 %gather_features.1.refs_0_ = bf16[128,1024]{1,0:T(8,128)(2,1)} custom-call(bf16[64,1024]{1,0:T(8,128)(2,1)} %x_ref.1, bf16[192,256]{1,0:T(8,128)(2,1)} %bitcast.11, bf16[64,256]{1,0:T(8,128)(2,1)} %bitcast.12), custom_call_target="tpu_custom_call" | custom-call | flops 1048576 | bytes 1048576 | tf_op jit(solution)/shard_map/gather_features/pallas_call | solution.py:52
  1.8 3.6 %collective-permute-start.1 = (bf16[128,1024]{1,0:T(8,128)(2,1)}, bf16[128,1024]{1,0:T(8,128)(2,1)S(1)}, u32[]{:S(2)}, u32[]{:S(2)}) collective-permute-start(bf16[128,1024]{1,0:T(8,128)(2,1)} %gather_features.1.refs_0_), channel_id=1, source_target_pairs={{0,2},{1,3},{2,0},{3,1},{4,6},{5,7},{6,4},{7,5},{8,10},{9,11},{10,... | collective-permute-start | bytes 786440 | tf_op jit(solution)/shard_map/gather_features/ppermute | solution.py:337
  5.6 2.4 %collective-permute-start.2 = (bf16[128,1024]{1,0:T(8,128)(2,1)}, bf16[128,1024]{1,0:T(8,128)(2,1)}, u32[]{:S(2)}, u32[]{:S(2)}) collective-permute-start(bf16[128,1024]{1,0:T(8,128)(2,1)} %gather_features.1.refs_0_), channel_id=1, source_target_pairs={{0,3},{1,0},{2,1},{3,2},{4,7},{5,4},{6,5},{7,6},{8,11},{9,8},{10,9... | collective-permute-start | bytes 786440 | tf_op jit(solution)/shard_map/gather_features/ppermute | solution.py:337
  9.5 1.2 %copy-done.1 = bf16[27,64,256]{2,1,0:T(8,128)(2,1)S(1)} copy-done((bf16[27,64,256]{2,1,0:T(8,128)(2,1)S(1)}, bf16[27,64,256]{2,1,0:T(8,128)(2,1)}, u32[]{:S(2)}) %copy-start.1) | copy-done | bytes 884760
  10.9 1.8 %collective-permute-start.3 = (bf16[2240,128]{1,0:T(8,128)(2,1)S(1)}, bf16[2240,128]{1,0:T(8,128)(2,1)S(1)}, u32[]{:S(2)}, u32[]{:S(2)}) collective-permute-start(bf16[2240,128]{1,0:T(8,128)(2,1)S(1)} %get-tuple-element.36.refs_0_), channel_id=1, source_target_pairs={{0,1},{1,2},{2,3},{3,0},{4,5},{5,6},{6,7},{7,4},{8,9},{9,10},{10,1... | collective-permute-start | bytes 1720328 | tf_op jit(solution)/shard_map/gather_weights/ppermute | solution.py:337
  12.7 2.4 %collective-permute-start.5 = (bf16[2240,128]{1,0:T(8,128)(2,1)S(1)}, bf16[2240,128]{1,0:T(8,128)(2,1)S(1)}, u32[]{:S(2)}, u32[]{:S(2)}) collective-permute-start(bf16[2240,128]{1,0:T(8,128)(2,1)S(1)} %get-tuple-element.36.refs_0_), channel_id=1, source_target_pairs={{0,2},{1,3},{2,0},{3,1},{4,6},{5,7},{6,4},{7,5},{8,10},{9,11},{10,... | collective-permute-start | bytes 1720328 | tf_op jit(solution)/shard_map/gather_weights/ppermute | solution.py:337
  15.2 1.2 %collective-permute-start.7 = (bf16[2240,128]{1,0:T(8,128)(2,1)S(1)}, bf16[2240,128]{1,0:T(8,128)(2,1)}, u32[]{:S(2)}, u32[]{:S(2)}) collective-permute-start(bf16[2240,128]{1,0:T(8,128)(2,1)S(1)} %get-tuple-element.36.refs_0_), channel_id=1, source_target_pairs={{0,3},{1,0},{2,1},{3,2},{4,7},{5,4},{6,5},{7,6},{8,11},{9,8},{10,9... | collective-permute-start | bytes 1720328 | tf_op jit(solution)/shard_map/gather_weights/ppermute | solution.py:337
  17.8 8.0 %attention.1 = bf16[64,24,128]{2,1,0:T(8,128)(2,1)} custom-call(s32[1]{0:T(128)} %bitcast.me_ref, s32[1]{0:T(128)} %bitcast.2.range_ref, bf16[128,1024]{1,0:T(8,128)(2,1)S(1)} %copy-done.2, bf16[128,1024]{1,0:T(8,128)(2,1)S(1)} %collective-permute-done.refs_1_, bf16[128,1024]{1,0:T(8,128)(2,1)S(1)} %collective-permute-done.1.refs_2_, ...), custom_call_target="tpu_custom_call" | custom-call | flops 4294967296 | bytes 1048576 | tf_op jit(solution)/shard_map/attention/pallas_call | solution.py:52
  25.8 13.8 %all-to-all-start = ((bf16[64,24,128]{2,1,0:T(8,128)(2,1)}), bf16[64,24,128]{2,1,0:T(8,128)(2,1)S(1)}, u32[]{:S(2)}, u32[]{:S(2)}) async-start(bf16[64,24,128]{2,1,0:T(8,128)(2,1)} %attention.1), calls=%async_computation | async-start | bytes 786432 | tf_op jit(solution)/shard_map/exchange/all_to_all | solution.py:341
  41.0 2.0 %collective-permute-start.6 = (bf16[2240,128]{1,0:T(8,128)(2,1)S(1)}, bf16[2240,128]{1,0:T(8,128)(2,1)}, u32[]{:S(2)}, u32[]{:S(2)}) collective-permute-start(bf16[2240,128]{1,0:T(8,128)(2,1)S(1)} %collective-permute-done.5.refs_2_), channel_id=1, source_target_pairs={{0,4},{4,0},{8,12},{12,8},{16,20},{20,16},{24,28},{28,24},{32,36},... | collective-permute-start | bytes 1720328 | tf_op jit(solution)/shard_map/gather_weights/ppermute | solution.py:386
  43.5 10.8 %all-to-all-done.got_ref = bf16[64,24,128]{2,1,0:T(8,128)(2,1)S(1)} async-done(((bf16[64,24,128]{2,1,0:T(8,128)(2,1)}), bf16[64,24,128]{2,1,0:T(8,128)(2,1)S(1)}, u32[]{:S(2)}, u32[]{:S(2)}) %all-to-all-start) | async-done | bytes 393248 | tf_op jit(solution)/shard_map/exchange/all_to_all | solution.py:341
  54.8 1.8 %collective-permute-start.10 = (bf16[320,256]{1,0:T(8,128)(2,1)S(1)}, bf16[320,256]{1,0:T(8,128)(2,1)S(1)}, u32[]{:S(2)}, u32[]{:S(2)}) collective-permute-start(bf16[320,256]{1,0:T(8,128)(2,1)S(1)} %compact.1.c0), channel_id=1, source_target_pairs={{0,2},{1,3},{2,0},{3,1},{4,6},{5,7},{6,4},{7,5},{8,10},{9,11},{10,... | collective-permute-start | bytes 491528 | tf_op jit(solution)/shard_map/compact/ppermute | solution.py:337
  56.6 1.9 %collective-permute-start.11 = (bf16[320,256]{1,0:T(8,128)(2,1)S(1)}, bf16[320,256]{1,0:T(8,128)(2,1)S(1)}, u32[]{:S(2)}, u32[]{:S(2)}) collective-permute-start(bf16[320,256]{1,0:T(8,128)(2,1)S(1)} %compact.1.c0), channel_id=1, source_target_pairs={{0,3},{1,0},{2,1},{3,2},{4,7},{5,4},{6,5},{7,6},{8,11},{9,8},{10,9... | collective-permute-start | bytes 491528 | tf_op jit(solution)/shard_map/compact/ppermute | solution.py:337
  58.4 3.3 %collective-permute-done.10.c2 = bf16[320,256]{1,0:T(8,128)(2,1)S(1)} collective-permute-done((bf16[320,256]{1,0:T(8,128)(2,1)S(1)}, bf16[320,256]{1,0:T(8,128)(2,1)S(1)}, u32[]{:S(2)}, u32[]{:S(2)}) %collective-permute-start.10) | collective-permute-done | bytes 163872 | tf_op jit(solution)/shard_map/compact/ppermute | solution.py:337
  61.7 3.6 %collective-permute-done.11.c3 = bf16[320,256]{1,0:T(8,128)(2,1)S(1)} collective-permute-done((bf16[320,256]{1,0:T(8,128)(2,1)S(1)}, bf16[320,256]{1,0:T(8,128)(2,1)S(1)}, u32[]{:S(2)}, u32[]{:S(2)}) %collective-permute-start.11) | collective-permute-done | bytes 163872 | tf_op jit(solution)/shard_map/compact/ppermute | solution.py:337
  65.4 1.0 window.1
  66.5 4.2 %collective-permute-start.12 = (bf16[256,256]{1,0:T(8,128)(2,1)S(1)}, bf16[256,256]{1,0:T(8,128)(2,1)S(1)}, u32[]{:S(2)}, u32[]{:S(2)}) collective-permute-start(bf16[256,256]{1,0:T(8,128)(2,1)S(1)} %get-tuple-element.51.third_ref), channel_id=1, source_target_pairs={{0,4},{4,8},{8,12},{12,16},{16,20},{20,24},{24,28},{28,32},{32,36}... | collective-permute-start | bytes 393224 | tf_op jit(solution)/shard_map/window/ppermute | solution.py:418
  70.7 4.9 %conv.2.acc_ref = f32[256,256]{1,0:T(8,128)S(1)} custom-call(s32[1]{0:T(128)} %bitcast.me_ref, s32[1]{0:T(128)} %bitcast.1.core_ref, bf16[512,256]{1,0:T(8,128)(2,1)S(1)} %get-tuple-element.46.win_ref, s32[27,256]{1,0:T(8,128)S(1)} %constant_dynamic-slice_fusion.near_ref, bf16[2240,128]{1,0:T(8,128)(2,1)S(1)} %get-tuple-element.36.refs_0_, ...), custom_call_target="tpu_custom_call" | custom-call | flops 4294967296 | bytes 1048576 | tf_op jit(solution)/shard_map/conv/pallas_call | solution.py:52
  75.5 4.6 %conv.3 = (bf16[64,256]{1,0:T(8,128)(2,1)S(1)}, bf16[64,256]{1,0:T(8,128)(2,1)S(1)}, bf16[64,256]{1,0:T(8,128)(2,1)S(1)}, bf16[64,256]{1,0:T(8,128)(2,1)S(1)}) custom-call(s32[1]{0:T(128)} %bitcast.me_ref, s32[1]{0:T(128)} %bitcast.1.core_ref, f32[256,256]{1,0:T(8,128)S(1)} %conv.2.acc_ref, bf16[256,256]{1,0:T(8,128)(2,1)S(1)} %collective-permute-done.12.halo_ref, ...), custom_call_target="tpu_custom_call" | custom-call | flops 4294967296 | bytes 1048576 | tf_op jit(solution)/shard_map/conv/pallas_call | solution.py:52
  80.3 2.4 %collective-permute-start.14 = (bf16[64,256]{1,0:T(8,128)(2,1)S(1)}, bf16[64,256]{1,0:T(8,128)(2,1)S(1)}, u32[]{:S(2)}, u32[]{:S(2)}) collective-permute-start(bf16[64,256]{1,0:T(8,128)(2,1)S(1)} %get-tuple-element.54), channel_id=1, source_target_pairs={{0,2},{1,3},{2,0},{3,1},{4,6},{5,7},{6,4},{7,5},{8,10},{9,11},{10,... | collective-permute-start | bytes 98312 | tf_op jit(solution)/shard_map/turn_back/ppermute | solution.py:437
  83.0 1.7 %collective-permute-done.13.t1 = bf16[64,256]{1,0:T(8,128)(2,1)S(1)} collective-permute-done((bf16[64,256]{1,0:T(8,128)(2,1)S(1)}, bf16[64,256]{1,0:T(8,128)(2,1)S(1)}, u32[]{:S(2)}, u32[]{:S(2)}) %collective-permute-start.13) | collective-permute-done | bytes 32800 | tf_op jit(solution)/shard_map/turn_back/ppermute | solution.py:437
  85.4 0.9 back.1
  86.3 21.0 %all_to_all.10.got_ref = bf16[64,16,128]{2,1,0:T(8,128)(2,1)S(1)} all-to-all(bf16[64,16,128]{2,1,0:T(8,128)(2,1)S(1)} %back.1), channel_id=1, replica_groups=mesh['range'=64,'chan'=4] {'range'}, dimensions={0} | all-to-all | bytes 524288 | tf_op jit(solution)/shard_map/back/all_to_all | solution.py:341
  107.4 1.6 %restore.1 = bf16[64,1024]{1,0:T(8,128)(2,1)} custom-call(bf16[64,16,128]{2,1,0:T(8,128)(2,1)S(1)} %all_to_all.10.got_ref, s32[8,1024]{1,0:T(8,128)S(1)} %codes.1.refs_4_.codes_ref), custom_call_target="tpu_custom_call" | custom-call | flops 1073741824 | bytes 1048576 | tf_op jit(solution)/shard_map/restore/pallas_call | solution.py:52
  (34 shorter events, 6.9 us)
Async XLA Ops:
  0.0 58.4 %copy-start = (s32[27,1024]{1,0:T(8,128)S(1)}, s32[27,1024]{1,0:T(8,128)}, u32[]{:S(2)}) copy-start(s32[27,1024]{1,0:T(8,128)} %param.10) | copy-start | bytes 331780
  0.0 9.4 %copy-start.3 = (bf16[256,256]{1,0:T(8,128)(2,1)S(1)}, bf16[256,256]{1,0:T(8,128)(2,1)}, u32[]{:S(2)}) copy-start(bf16[256,256]{1,0:T(8,128)(2,1)} %up_ref.1) | copy-start | bytes 393220
  0.0 9.4 %copy-start.4 = (bf16[256,256]{1,0:T(8,128)(2,1)S(1)}, bf16[256,256]{1,0:T(8,128)(2,1)}, u32[]{:S(2)}) copy-start(bf16[256,256]{1,0:T(8,128)(2,1)} %down_ref.1) | copy-start | bytes 393220
  1.8 9.1 %collective-permute-start.1 = (bf16[128,1024]{1,0:T(8,128)(2,1)}, bf16[128,1024]{1,0:T(8,128)(2,1)S(1)}, u32[]{:S(2)}, u32[]{:S(2)}) collective-permute-start(bf16[128,1024]{1,0:T(8,128)(2,1)} %gather_features.1.refs_0_), channel_id=1, source_target_pairs={{0,2},{1,3},{2,0},{3,1},{4,6},{5,7},{6,4},{7,5},{8,10},{9,11},{10,... | collective-permute-start | bytes 786440 | tf_op jit(solution)/shard_map/gather_features/ppermute | solution.py:337
  5.3 11.8 %collective-permute-start = (bf16[128,1024]{1,0:T(8,128)(2,1)}, bf16[128,1024]{1,0:T(8,128)(2,1)S(1)}, u32[]{:S(2)}, u32[]{:S(2)}) collective-permute-start(bf16[128,1024]{1,0:T(8,128)(2,1)} %gather_features.1.refs_0_), channel_id=1, source_target_pairs={{0,1},{1,2},{2,3},{3,0},{4,5},{5,6},{6,7},{7,4},{8,9},{9,10},{10,1... | collective-permute-start | bytes 786440 | tf_op jit(solution)/shard_map/gather_features/ppermute | solution.py:337
  5.6 12.2 %collective-permute-start.2 = (bf16[128,1024]{1,0:T(8,128)(2,1)}, bf16[128,1024]{1,0:T(8,128)(2,1)}, u32[]{:S(2)}, u32[]{:S(2)}) collective-permute-start(bf16[128,1024]{1,0:T(8,128)(2,1)} %gather_features.1.refs_0_), channel_id=1, source_target_pairs={{0,3},{1,0},{2,1},{3,2},{4,7},{5,4},{6,5},{7,6},{8,11},{9,8},{10,9... | collective-permute-start | bytes 786440 | tf_op jit(solution)/shard_map/gather_features/ppermute | solution.py:337
  8.0 0.7 copy-start.5
  9.5 1.2 %copy-start.1 = (bf16[27,64,256]{2,1,0:T(8,128)(2,1)S(1)}, bf16[27,64,256]{2,1,0:T(8,128)(2,1)}, u32[]{:S(2)}) copy-start(bf16[27,64,256]{2,1,0:T(8,128)(2,1)} %param.13) | copy-start | bytes 2654212
  10.6 7.2 %copy-start.2 = (bf16[128,1024]{1,0:T(8,128)(2,1)S(1)}, bf16[128,1024]{1,0:T(8,128)(2,1)}, u32[]{:S(2)}) copy-start(bf16[128,1024]{1,0:T(8,128)(2,1)} %gather_features.1.refs_0_) | copy-start | bytes 786436
  10.9 28.8 %collective-permute-start.3 = (bf16[2240,128]{1,0:T(8,128)(2,1)S(1)}, bf16[2240,128]{1,0:T(8,128)(2,1)S(1)}, u32[]{:S(2)}, u32[]{:S(2)}) collective-permute-start(bf16[2240,128]{1,0:T(8,128)(2,1)S(1)} %get-tuple-element.36.refs_0_), channel_id=1, source_target_pairs={{0,1},{1,2},{2,3},{3,0},{4,5},{5,6},{6,7},{7,4},{8,9},{9,10},{10,1... | collective-permute-start | bytes 1720328 | tf_op jit(solution)/shard_map/gather_weights/ppermute | solution.py:337
  12.7 28.2 %collective-permute-start.5 = (bf16[2240,128]{1,0:T(8,128)(2,1)S(1)}, bf16[2240,128]{1,0:T(8,128)(2,1)S(1)}, u32[]{:S(2)}, u32[]{:S(2)}) collective-permute-start(bf16[2240,128]{1,0:T(8,128)(2,1)S(1)} %get-tuple-element.36.refs_0_), channel_id=1, source_target_pairs={{0,2},{1,3},{2,0},{3,1},{4,6},{5,7},{6,4},{7,5},{8,10},{9,11},{10,... | collective-permute-start | bytes 1720328 | tf_op jit(solution)/shard_map/gather_weights/ppermute | solution.py:337
  15.2 27.8 %collective-permute-start.7 = (bf16[2240,128]{1,0:T(8,128)(2,1)S(1)}, bf16[2240,128]{1,0:T(8,128)(2,1)}, u32[]{:S(2)}, u32[]{:S(2)}) collective-permute-start(bf16[2240,128]{1,0:T(8,128)(2,1)S(1)} %get-tuple-element.36.refs_0_), channel_id=1, source_target_pairs={{0,3},{1,0},{2,1},{3,2},{4,7},{5,4},{6,5},{7,6},{8,11},{9,8},{10,9... | collective-permute-start | bytes 1720328 | tf_op jit(solution)/shard_map/gather_weights/ppermute | solution.py:337
  25.8 28.4 %all-to-all-start = ((bf16[64,24,128]{2,1,0:T(8,128)(2,1)}), bf16[64,24,128]{2,1,0:T(8,128)(2,1)S(1)}, u32[]{:S(2)}, u32[]{:S(2)}) async-start(bf16[64,24,128]{2,1,0:T(8,128)(2,1)} %attention.1), calls=%async_computation | async-start | bytes 786432 | tf_op jit(solution)/shard_map/exchange/all_to_all | solution.py:341
  39.7 14.6 %collective-permute-start.4 = (bf16[2240,128]{1,0:T(8,128)(2,1)S(1)}, bf16[2240,128]{1,0:T(8,128)(2,1)}, u32[]{:S(2)}, u32[]{:S(2)}) collective-permute-start(bf16[2240,128]{1,0:T(8,128)(2,1)S(1)} %collective-permute-done.3.refs_1_), channel_id=1, source_target_pairs={{0,4},{4,0},{8,12},{12,8},{16,20},{20,16},{24,28},{28,24},{32,36},... | collective-permute-start | bytes 1720328 | tf_op jit(solution)/shard_map/gather_weights/ppermute | solution.py:386
  41.0 13.3 %collective-permute-start.6 = (bf16[2240,128]{1,0:T(8,128)(2,1)S(1)}, bf16[2240,128]{1,0:T(8,128)(2,1)}, u32[]{:S(2)}, u32[]{:S(2)}) collective-permute-start(bf16[2240,128]{1,0:T(8,128)(2,1)S(1)} %collective-permute-done.5.refs_2_), channel_id=1, source_target_pairs={{0,4},{4,0},{8,12},{12,8},{16,20},{20,16},{24,28},{28,24},{32,36},... | collective-permute-start | bytes 1720328 | tf_op jit(solution)/shard_map/gather_weights/ppermute | solution.py:386
  43.0 11.3 %collective-permute-start.8 = (bf16[2240,128]{1,0:T(8,128)(2,1)}, bf16[2240,128]{1,0:T(8,128)(2,1)}, u32[]{:S(2)}, u32[]{:S(2)}) collective-permute-start(bf16[2240,128]{1,0:T(8,128)(2,1)} %collective-permute-done.7.refs_3_), channel_id=1, source_target_pairs={{0,4},{4,0},{8,12},{12,8},{16,20},{20,16},{24,28},{28,24},{32,36},... | collective-permute-start | bytes 1720328 | tf_op jit(solution)/shard_map/gather_weights/ppermute | solution.py:386
  54.8 6.9 %collective-permute-start.10 = (bf16[320,256]{1,0:T(8,128)(2,1)S(1)}, bf16[320,256]{1,0:T(8,128)(2,1)S(1)}, u32[]{:S(2)}, u32[]{:S(2)}) collective-permute-start(bf16[320,256]{1,0:T(8,128)(2,1)S(1)} %compact.1.c0), channel_id=1, source_target_pairs={{0,2},{1,3},{2,0},{3,1},{4,6},{5,7},{6,4},{7,5},{8,10},{9,11},{10,... | collective-permute-start | bytes 491528 | tf_op jit(solution)/shard_map/compact/ppermute | solution.py:337
  56.6 8.8 %collective-permute-start.11 = (bf16[320,256]{1,0:T(8,128)(2,1)S(1)}, bf16[320,256]{1,0:T(8,128)(2,1)S(1)}, u32[]{:S(2)}, u32[]{:S(2)}) collective-permute-start(bf16[320,256]{1,0:T(8,128)(2,1)S(1)} %compact.1.c0), channel_id=1, source_target_pairs={{0,3},{1,0},{2,1},{3,2},{4,7},{5,4},{6,5},{7,6},{8,11},{9,8},{10,9... | collective-permute-start | bytes 491528 | tf_op jit(solution)/shard_map/compact/ppermute | solution.py:337
  58.4 7.0 %collective-permute-start.9 = (bf16[320,256]{1,0:T(8,128)(2,1)S(1)}, bf16[320,256]{1,0:T(8,128)(2,1)S(1)}, u32[]{:S(2)}, u32[]{:S(2)}) collective-permute-start(bf16[320,256]{1,0:T(8,128)(2,1)S(1)} %compact.1.c0), channel_id=1, source_target_pairs={{0,1},{1,2},{2,3},{3,0},{4,5},{5,6},{6,7},{7,4},{8,9},{9,10},{10,1... | collective-permute-start | bytes 491528 | tf_op jit(solution)/shard_map/compact/ppermute | solution.py:337
  66.5 9.1 %collective-permute-start.12 = (bf16[256,256]{1,0:T(8,128)(2,1)S(1)}, bf16[256,256]{1,0:T(8,128)(2,1)S(1)}, u32[]{:S(2)}, u32[]{:S(2)}) collective-permute-start(bf16[256,256]{1,0:T(8,128)(2,1)S(1)} %get-tuple-element.51.third_ref), channel_id=1, source_target_pairs={{0,4},{4,8},{8,12},{12,16},{16,20},{20,24},{24,28},{28,32},{32,36}... | collective-permute-start | bytes 393224 | tf_op jit(solution)/shard_map/window/ppermute | solution.py:418
  80.2 4.5 %collective-permute-start.13 = (bf16[64,256]{1,0:T(8,128)(2,1)S(1)}, bf16[64,256]{1,0:T(8,128)(2,1)S(1)}, u32[]{:S(2)}, u32[]{:S(2)}) collective-permute-start(bf16[64,256]{1,0:T(8,128)(2,1)S(1)} %get-tuple-element.53), channel_id=1, source_target_pairs={{0,1},{1,2},{2,3},{3,0},{4,5},{5,6},{6,7},{7,4},{8,9},{9,10},{10,1... | collective-permute-start | bytes 98312 | tf_op jit(solution)/shard_map/turn_back/ppermute | solution.py:437
  80.3 4.7 %collective-permute-start.14 = (bf16[64,256]{1,0:T(8,128)(2,1)S(1)}, bf16[64,256]{1,0:T(8,128)(2,1)S(1)}, u32[]{:S(2)}, u32[]{:S(2)}) collective-permute-start(bf16[64,256]{1,0:T(8,128)(2,1)S(1)} %get-tuple-element.54), channel_id=1, source_target_pairs={{0,2},{1,3},{2,0},{3,1},{4,6},{5,7},{6,4},{7,5},{8,10},{9,11},{10,... | collective-permute-start | bytes 98312 | tf_op jit(solution)/shard_map/turn_back/ppermute | solution.py:437
  82.7 2.8 %collective-permute-start.15 = (bf16[64,256]{1,0:T(8,128)(2,1)S(1)}, bf16[64,256]{1,0:T(8,128)(2,1)S(1)}, u32[]{:S(2)}, u32[]{:S(2)}) collective-permute-start(bf16[64,256]{1,0:T(8,128)(2,1)S(1)} %get-tuple-element.55), channel_id=1, source_target_pairs={{0,3},{1,0},{2,1},{3,2},{4,7},{5,4},{6,5},{7,6},{8,11},{9,8},{10,9... | collective-permute-start | bytes 98312 | tf_op jit(solution)/shard_map/turn_back/ppermute | solution.py:437
